TPU v7x, 32 devices: a whole 2x2x4 slice. The times are simulated.
32 devices in a mesh: segment: 4 (over z), row: 4 (over y, x), col: 2 (over core).
Axes of the slice: x: 2, y: 2, z: 4, core: 2. Of those that a mesh axis runs over, the one named last changes fastest.
Arguments:
- weights: bfloat16 [4, 4096, 4096], P('segment', 'row', 'col'), may hold values from -0.09375 to 0.09375
- layer_gains: float32 [4, 4096], P('segment', 'col'), may hold values from -0.5 to 0.5
- incoming: bfloat16 [4, 256, 4096], P('segment', 'row', 'col'), may hold values from -6 to 6
- fresh_batch: bfloat16 [256, 4096], P('row', 'col'), may hold values from -6 to 6
- returning: bfloat16 [4, 256, 4096], P('segment', 'row', 'col'), may hold values from -6 to 6
- fresh_cotangent: bfloat16 [256, 4096], P('row', 'col'), may hold values from -6 to 6
- stashed_inputs: bfloat16 [4, 2, 256, 4096], P('segment', None, 'row', 'col'), may hold values from -6 to 6
Outputs:
- layer_outputs: bfloat16 [4, 2, 256, 4096], P('segment', None, 'row', 'col')
- input_grads: bfloat16 [4, 2, 256, 4096], P('segment', None, 'row', 'col')
All inputs are finite; a program needn't handle non-finite values.
Results may differ from a plain program's by a relative error of at most 0.0055.
Values may be sent and summed in bfloat16 or wider, within the bound.
No kernel may reach another device: no remote copies, remote signals or barrier semaphores. Data moves between devices by JAX's collectives and lax.ppermute only.
A program may use at most 64 MiB of HBM per device.

v0:
```python
import jax
import jax.numpy as jnp
from jax import lax
from jax.sharding import PartitionSpec as P


def passed_along(value, axis, steps):
    count = lax.axis_size(axis)
    first, last = (max(0, -steps), min(count, count - steps))
    return lax.ppermute(value, axis, [(source, source + steps) for source in range(first, last)])


def silu_slope(values):
    sigma = jax.nn.sigmoid(values)
    return sigma * (1.0 + values * (1.0 - sigma))


def pass_on(message, direction):
    return passed_along(message, "segment", direction)


def widen(pair):
    return (
        lax.all_gather(pair[0], "col", axis=1, tiled=True),
        lax.all_gather(pair[1], "col", axis=1, tiled=True),
    )


def shards(weights, layer_gains, incoming, fresh_batch, returning, fresh_cotangent, stashed_inputs):
    segment_index = lax.axis_index("segment")
    segment_count = lax.axis_size("segment")
    weight_block = weights[0]
    weight_panel = lax.all_gather(weight_block, "row", axis=0, tiled=True)
    layer_gain = layer_gains[0][None, :]

    def advance(own_block, full_input):
        pre_act = jnp.dot(full_input, weight_panel, preferred_element_type=jnp.float32)
        return (own_block.astype(jnp.float32) + layer_gain * jax.nn.silu(pre_act)).astype(
            jnp.bfloat16
        )

    def retreat(upstream, full_stored):
        pre_act = jnp.dot(full_stored, weight_panel, preferred_element_type=jnp.float32)
        scaled = (upstream.astype(jnp.float32) * layer_gain * silu_slope(pre_act)).astype(
            jnp.bfloat16
        )
        partial_terms = lax.dot_general(
            scaled, weight_panel, (((1,), (1,)), ((), ())), preferred_element_type=jnp.float32
        )
        back_term = lax.psum_scatter(
            partial_terms.astype(jnp.bfloat16), "col", scatter_dimension=1, tiled=True
        ).astype(jnp.float32)
        return (upstream.astype(jnp.float32) + back_term).astype(jnp.bfloat16)

    full_input, full_stored = widen((incoming[0], stashed_inputs[0, 0]))
    first_out = advance(incoming[0], full_input)
    grad_first = retreat(returning[0], full_stored)
    arrived = pass_on(first_out, 1)
    feed_block = jnp.where(segment_index == 0, fresh_batch, arrived)
    full_feed, full_second = widen((feed_block, stashed_inputs[0, 1]))
    second_out = advance(feed_block, full_feed)
    arrived_grad = pass_on(grad_first, -1)
    upstream = jnp.where(segment_index == segment_count - 1, fresh_cotangent, arrived_grad)
    grad_second = retreat(upstream, full_second)
    layer_outputs = jnp.stack([first_out, second_out], axis=0)[None]
    input_grads = jnp.stack([grad_first, grad_second], axis=0)[None]
    return (layer_outputs, input_grads)


def solution(mesh):
    in_specs = (
        P("segment", "row", "col"),
        P("segment", "col"),
        P("segment", "row", "col"),
        P("row", "col"),
        P("segment", "row", "col"),
        P("row", "col"),
        P("segment", None, "row", "col"),
    )
    out_specs = (P("segment", None, "row", "col"), P("segment", None, "row", "col"))
    return jax.shard_map(shards, mesh=mesh, in_specs=in_specs, out_specs=out_specs, check_vma=False)
```

profile of v0, /device:TPU:1, one launch (start us, length us, event | category | flops | bytes accessed | tf_op | source)
XLA Modules:
  0.0 243.9 jit_solution(10237569319368178293)
XLA Ops:
  7.2 0.0 all-gather.6.cloned.1.call-start
  7.2 0.7 all-gather.6.cloned.1.call-update
  7.9 0.0 reduce-scatter.3.cloned.1.call-start
  8.0 1.1 fusion.57
  9.0 2.2 all-gather.2
  11.2 2.2 all-gather.3
  13.4 156.0 %all-gather.6.cloned.1.call-done = bf16[1,4096,2048]{2,1,0:T(8,128)(2,1)} async-done(((bf16[1,1024,2048]{2,1,0:T(8,128)(2,1)}), bf16[1,4096,2048]{2,1,0:T(8,128)(2,1)}) %all-gather.6.cloned.1.call-update) | async-done | bytes 16777232 | tf_op jit(solution)/shard_map/all_gather | solution.py:33
  169.4 0.0 copy-start.2
  169.4 0.0 copy-start.3
  169.4 15.7 %fusion.12 = bf16[64,4096]{1,0:T(8,128)(2,1)} fusion(bf16[1,4096,2048]{2,1,0:T(8,128)(2,1)} %all-gather.6.cloned.1.call-done, bf16[1,1,64,4096]{3,2,1,0:T(8,128)(2,1)S(1)} %all-gather.2, bf16[1,64,2048]{2,1,0:T(8,128)(2,1)} %param.11, f32[2048]{0:T(1024)} %bitcast.72), kind=kOutput, calls=%fused_computation.12 | convolution fusion | flops 2149187584 | bytes 18096128 | tf_op jit(solution)/shard_map/dot_general | solution.py:47
  185.1 0.0 copy-start
  185.1 0.0 copy-start.4
  185.1 0.0 copy-start.1
  185.1 0.0 reduce-scatter.3.cloned.1.call-update
  185.1 0.0 reduce-scatter.5.cloned.1.call-start
  185.2 0.0 copy-done.2
  185.2 2.6 %all-gather = bf16[1,64,4096]{2,1,0:T(8,128)(2,1)S(1)} all-gather(bf16[1,64,2048]{2,1,0:T(8,128)(2,1)S(1)} %copy-done.2), channel_id=2, replica_groups=mesh['segment'=4,'row'=4,'col'=2] {'col'}, dimensions={2}, use_global_device_ids=true | all-gather | bytes 786432 | tf_op jit(solution)/shard_map/all_gather | solution.py:24
  187.8 0.0 copy-done.3
  187.8 9.1 %fusion.24 = bf16[64,2048]{1,0:T(8,128)(2,1)S(1)} fusion(bf16[1,4096,2048]{2,1,0:T(8,128)(2,1)} %all-gather.6.cloned.1.call-done, bf16[1,64,4096]{2,1,0:T(8,128)(2,1)S(1)} %all-gather, bf16[1,64,2048]{2,1,0:T(8,128)(2,1)S(1)} %copy-done.2, f32[2048]{0:T(1024)S(1)} %bitcast.73), kind=kOutput, calls=%fused_computation.27 | convolution fusion | flops 1074790400 | bytes 17833984 | tf_op jit(solution)/shard_map/dot_general | solution.py:37
  196.9 3.1 %collective-permute-start = (bf16[64,2048]{1,0:T(8,128)(2,1)S(1)}, bf16[64,2048]{1,0:T(8,128)(2,1)S(1)}, u32[]{:S(2)}, u32[]{:S(2)}) collective-permute-start(bf16[64,2048]{1,0:T(8,128)(2,1)S(1)} %fusion.24), channel_id=1, source_target_pairs={{0,8},{8,16},{16,24},{1,9},{9,17},{17,25},{2,10},{10,18},{18,26},{... | collective-permute-start | bytes 786440 | tf_op jit(solution)/shard_map/ppermute | solution.py:10
  200.0 0.0 reduce-scatter.3.cloned.1.call-done
  200.1 0.0 copy-done
  200.1 1.0 fusion.23
  201.1 1.3 collective-permute-start.1
  202.4 2.9 %collective-permute-done = bf16[64,2048]{1,0:T(8,128)(2,1)S(1)} collective-permute-done((bf16[64,2048]{1,0:T(8,128)(2,1)S(1)}, bf16[64,2048]{1,0:T(8,128)(2,1)S(1)}, u32[]{:S(2)}, u32[]{:S(2)}) %collective-permute-start) | collective-permute-done | bytes 262176 | tf_op jit(solution)/shard_map/ppermute | solution.py:10
  205.3 0.0 copy-done.4
  205.3 3.2 %all_gather.17 = bf16[64,4096]{1,0:T(8,128)(2,1)S(1)} all-gather(bf16[64,2048]{1,0:T(8,128)(2,1)S(1)} %broadcast_select_fusion.1), channel_id=1, replica_groups=mesh['segment'=4,'row'=4,'col'=2] {'col'}, dimensions={1}, use_global_device_ids=true | all-gather | bytes 786432 | tf_op jit(solution)/shard_map/all_gather | solution.py:24
  208.6 1.6 collective-permute-done.1
  210.2 0.0 copy-done.1
  210.2 15.6 %fusion.15 = bf16[64,4096]{1,0:T(8,128)(2,1)} fusion(bf16[1,4096,2048]{2,1,0:T(8,128)(2,1)} %all-gather.6.cloned.1.call-done, bf16[1,1,64,4096]{3,2,1,0:T(8,128)(2,1)S(1)} %all-gather.3, f32[2048]{0:T(1024)S(1)} %bitcast.74, bf16[64,2048]{1,0:T(8,128)(2,1)S(1)} %copy-done.1, bf16[64,2048]{1,0:T(8,128)(2,1)S(1)} %collective-permute-done.1, pred[]{:T(512)S(6)} %eq.7), kind=kOutput, calls=%fused_computation.13 | convolution fusion | flops 2149318656 | bytes 18358272 | tf_op jit(solution)/shard_map/dot_general | solution.py:47
  225.7 0.0 reduce-scatter.5.cloned.1.call-update
  225.8 8.9 %fusion.54 = bf16[1,64,2048]{2,1,0:T(8,128)(2,1)S(1)} fusion(f32[2048]{0:T(1024)S(1)} %bitcast.75, bf16[64,2048]{1,0:T(8,128)(2,1)S(1)} %broadcast_select_fusion.1, bf16[64,4096]{1,0:T(8,128)(2,1)S(1)} %all_gather.17, bf16[1,4096,2048]{2,1,0:T(8,128)(2,1)} %all-gather.6.cloned.1.call-done), kind=kOutput, calls=%fused_computation.40 | convolution fusion | flops 1074790400 | bytes 17833984 | tf_op jit(solution)/shard_map/dot_general | solution.py:37
  234.7 0.8 maximum_bitcast_fusion
  235.5 0.0 reduce-scatter.5.cloned.1.call-done
  235.5 1.0 fusion.48
  236.5 0.8 maximum_bitcast_fusion.1
  (1 shorter events, 0.0 us)
Async XLA Ops:
  7.2 162.2 %all-gather.6.cloned.1.call-start = ((), (), s32[]{:S(2)}) async-start(), calls=%async_computation.4 | async-start | bytes 20971520 | tf_op jit(solution)/shard_map/all_gather | solution.py:33
  7.9 192.2 %reduce-scatter.3.cloned.1.call-start = ((), (), s32[]{:S(2)}) async-start(), calls=%async_computation.2 | async-start | bytes 786432 | tf_op jit(solution)/shard_map/reduce_scatter | solution.py:50
  169.4 15.8 %copy-start.2 = (bf16[1,64,2048]{2,1,0:T(8,128)(2,1)S(1)}, bf16[1,64,2048]{2,1,0:T(8,128)(2,1)}, u32[]{:S(2)}) copy-start(bf16[1,64,2048]{2,1,0:T(8,128)(2,1)} %param.9) | copy-start | bytes 786436
  169.4 18.4 %copy-start.3 = (f32[1,2048]{1,0:T(1,128)S(1)}, f32[1,2048]{1,0:T(1,128)}, u32[]{:S(2)}) copy-start(f32[1,2048]{1,0:T(1,128)} %param.8) | copy-start | bytes 24580
  185.1 15.0 %copy-start = (bf16[1,64,2048]{2,1,0:T(8,128)(2,1)S(1)}, bf16[1,64,2048]{2,1,0:T(8,128)(2,1)}, u32[]{:S(2)}) copy-start(bf16[1,64,2048]{2,1,0:T(8,128)(2,1)} %param.11) | copy-start | bytes 786436
  185.1 20.2 %copy-start.4 = (bf16[64,2048]{1,0:T(8,128)(2,1)S(1)}, bf16[64,2048]{1,0:T(8,128)(2,1)}, u32[]{:S(2)}) copy-start(bf16[64,2048]{1,0:T(8,128)(2,1)} %param.10) | copy-start | bytes 786436
  185.1 25.1 %copy-start.1 = (bf16[64,2048]{1,0:T(8,128)(2,1)S(1)}, bf16[64,2048]{1,0:T(8,128)(2,1)}, u32[]{:S(2)}) copy-start(bf16[64,2048]{1,0:T(8,128)(2,1)} %param.12) | copy-start | bytes 786436
  185.1 50.4 %reduce-scatter.5.cloned.1.call-start = ((), (), s32[]{:S(2)}) async-start(), calls=%async_computation.3 | async-start | bytes 786432 | tf_op jit(solution)/shard_map/reduce_scatter | solution.py:50
  196.9 8.4 %collective-permute-start = (bf16[64,2048]{1,0:T(8,128)(2,1)S(1)}, bf16[64,2048]{1,0:T(8,128)(2,1)S(1)}, u32[]{:S(2)}, u32[]{:S(2)}) collective-permute-start(bf16[64,2048]{1,0:T(8,128)(2,1)S(1)} %fusion.24), channel_id=1, source_target_pairs={{0,8},{8,16},{16,24},{1,9},{9,17},{17,25},{2,10},{10,18},{18,26},{... | collective-permute-start | bytes 786440 | tf_op jit(solution)/shard_map/ppermute | solution.py:10
  201.1 9.1 %collective-permute-start.1 = (bf16[64,2048]{1,0:T(8,128)(2,1)S(1)}, bf16[64,2048]{1,0:T(8,128)(2,1)S(1)}, u32[]{:S(2)}, u32[]{:S(2)}) collective-permute-start(bf16[64,2048]{1,0:T(8,128)(2,1)S(1)} %fusion.23), channel_id=1, source_target_pairs={{8,0},{16,8},{24,16},{9,1},{17,9},{25,17},{10,2},{18,10},{26,18},{... | collective-permute-start | bytes 786440 | tf_op jit(solution)/shard_map/ppermute | solution.py:10
Sparse Core Ops, SparseCore 0:
  9.8 159.4 all-gather.5
  185.3 8.3 reduce-scatter.2
  225.9 8.2 reduce-scatter.4
where the time goes:
time: 246 us; the launch traced here: 244 us
  waiting for transfers between devices  161 us (65%)
  matrix products  49.3 us (20%)
  between operations  13.8 us (6%)
  blocking collectives  10.2 us (4%)
  starting transfers between devices  4.5 us (2%)
  other arithmetic  3.77 us (2%)
    all_gather x1, waiting for transfers between devices, shards(): weight_panel = lax.all_gather(weight_block, 'row', axis=0, tiled=True)  156 us
    dot_general x2, matrix products, retreat(): lax.dot_general(scaled, weight_panel, (((1,), (1,)), ((), ())), preferred...  31.3 us
    dot_general x2, matrix products, advance(): jnp.dot(full_input, weight_panel, preferred_element_type=jnp.float32)  18 us
    all_gather x2, blocking collectives, widen(): lax.all_gather(pair[0], 'col', axis=1, tiled=True)  5.84 us
  transfers between devices with their start and end apart: 5, of which 3 were waited for; matrix products, arithmetic and copies ran while one was open for 9% of the time, Pallas kernels for 0%

commit v1 on v0

v1 whole, which is shorter than its diff:
```python
import jax
import jax.numpy as jnp
from jax import lax
from jax.sharding import PartitionSpec as P

F32 = jnp.float32
BF16 = jnp.bfloat16


def silu_slope(values):
    sigma = jax.nn.sigmoid(values)
    return sigma * (1.0 + values * (1.0 - sigma))


def passed_along(value, steps):
    count = lax.axis_size("segment")
    first, last = (max(0, -steps), min(count, count - steps))
    return lax.ppermute(value, "segment", [(source, source + steps) for source in range(first, last)])


def rows_swapped(value, flip):
    count = lax.axis_size("row")
    return lax.ppermute(value, "row", [(source, source ^ flip) for source in range(count)])


def plane_sent(value, pairs):
    cols = lax.axis_size("col")
    return lax.ppermute(
        value, ("row", "col"), [(a * cols + b, c * cols + d) for (a, b), (c, d) in pairs]
    )


def bits_of(count):
    return count.bit_length() - 1


def pick(blocks, which):
    chosen = blocks[0]
    for at in range(1, len(blocks)):
        chosen = jnp.where(which == at, blocks[at], chosen)
    return chosen


class Plane:
    def __init__(self, weight_block):
        self.rows, self.cols = lax.axis_size("row"), lax.axis_size("col")
        self.per_col = self.rows // self.cols
        self.row, self.col = lax.axis_index("row"), lax.axis_index("col")
        self.steps = bits_of(self.rows)
        self.streams = max(self.steps, 1)
        self.home = self.row // self.per_col
        self.at_home = self.col == self.home
        self.within = self.row % self.per_col
        width = weight_block.shape[1] // self.streams
        self.weight_parts = [
            weight_block[:, at * width : (at + 1) * width] for at in range(self.streams)
        ]

    def features_in(self, block):
        width = block.shape[1] // self.per_col
        pieces = [block[:, at * width : (at + 1) * width] for at in range(self.per_col)]
        relative = [
            pick([pieces[at ^ shift] for at in range(self.per_col)], self.within)
            for shift in range(self.per_col)
        ]
        gathered = [relative[0]]
        for flip in range(1, self.rows):
            pairs = [
                ((r, (r ^ flip) // self.per_col), (r ^ flip, (r ^ flip) // self.per_col))
                for r in range(self.rows)
            ]
            gathered.append(plane_sent(relative[flip % self.per_col], pairs))
        whole = jnp.concatenate(gathered, axis=0)
        shared = whole
        for shift in range(1, self.cols):
            pairs = [
                ((r, r // self.per_col), (r, (r // self.per_col) ^ shift)) for r in range(self.rows)
            ]
            shared = jnp.where(
                (self.col ^ self.home) == shift, plane_sent(whole, pairs), shared
            )
        return shared

    def features_out(self, partial):
        total = partial.astype(F32)
        sent = partial.astype(BF16)
        for shift in range(1, self.cols):
            pairs = [
                ((r, (r // self.per_col) ^ shift), (r, r // self.per_col)) for r in range(self.rows)
            ]
            total = total + plane_sent(sent, pairs).astype(F32)
        total = total.astype(BF16)
        tokens = total.shape[0] // self.rows
        arrived = [total[:tokens]]
        for flip in range(1, self.rows):
            pairs = [((r, r // self.per_col), (r ^ flip, r // self.per_col)) for r in range(self.rows)]
            arrived.append(plane_sent(total[flip * tokens : (flip + 1) * tokens], pairs))
        relative = []
        for shift in range(self.per_col):
            found = arrived[shift]
            for group in range(1, self.cols):
                found = jnp.where(
                    (self.col ^ self.home) == group, arrived[group * self.per_col + shift], found
                )
            relative.append(found)
        return jnp.concatenate(
            [
                pick([relative[at ^ within] for within in range(self.per_col)], self.within)
                for at in range(self.per_col)
            ],
            axis=1,
        )

    def forward(self, full):
        tokens = full.shape[0] // self.rows
        summed = []
        for stream, weight in enumerate(self.weight_parts):
            product = jnp.dot(full, weight, preferred_element_type=F32).astype(BF16)
            held = {k: product[k * tokens : (k + 1) * tokens] for k in range(self.rows)}
            summed.append(held)
        for step in range(self.steps):
            for stream in range(self.streams):
                held = summed[stream]
                flip = 1 << ((stream + step) % self.steps)
                away = [k for k in sorted(held) if k & flip]
                arrived = rows_swapped(
                    jnp.concatenate([held[k].astype(BF16) for k in away], axis=0), flip
                )
                summed[stream] = {
                    k ^ flip: held[k ^ flip].astype(F32)
                    + arrived[at * tokens : (at + 1) * tokens].astype(F32)
                    for at, k in enumerate(away)
                }
        return jnp.concatenate([held[0].astype(F32) for held in summed], axis=1)

    def backward(self, scaled):
        width = scaled.shape[1] // self.streams
        pieces = [
            {0: scaled[:, at * width : (at + 1) * width]} for at in range(self.streams)
        ]
        for step in range(self.steps):
            for stream in range(self.streams):
                held = pieces[stream]
                tokens = scaled.shape[0]
                flip = 1 << ((stream + step) % self.steps)
                ours = sorted(held)
                arrived = rows_swapped(jnp.concatenate([held[k] for k in ours], axis=0), flip)
                for at, k in enumerate(ours):
                    held[k ^ flip] = arrived[at * tokens : (at + 1) * tokens]
        partial = 0.0
        for held, weight in zip(pieces, self.weight_parts):
            whole = jnp.concatenate([held[k] for k in range(self.rows)], axis=0)
            partial = partial + lax.dot_general(
                whole, weight, (((1,), (1,)), ((), ())), preferred_element_type=F32
            )
        return partial


def shards(weights, layer_gains, incoming, fresh_batch, returning, fresh_cotangent, stashed_inputs):
    segment_index = lax.axis_index("segment")
    segment_count = lax.axis_size("segment")
    plane = Plane(weights[0])
    layer_gain = layer_gains[0][None, :]

    def advance(own_block, full_input):
        pre_act = plane.forward(full_input)
        return (own_block.astype(F32) + layer_gain * jax.nn.silu(pre_act)).astype(BF16)

    def retreat(upstream, pre_act):
        scaled = (upstream.astype(F32) * layer_gain * silu_slope(pre_act)).astype(BF16)
        back_term = plane.features_out(plane.backward(scaled)).astype(F32)
        return (upstream.astype(F32) + back_term).astype(BF16)

    first_stored = plane.features_in(stashed_inputs[0, 0])
    full_input = plane.features_in(incoming[0])
    second_stored = plane.features_in(stashed_inputs[0, 1])

    first_back_pre = plane.forward(first_stored)
    grad_first = retreat(returning[0], first_back_pre)
    first_out = advance(incoming[0], full_input)
    second_back_pre = plane.forward(second_stored)

    arrived = passed_along(first_out, 1)
    feed_block = jnp.where(segment_index == 0, fresh_batch, arrived)
    arrived_grad = passed_along(grad_first, -1)
    upstream = jnp.where(segment_index == segment_count - 1, fresh_cotangent, arrived_grad)
    second_out = advance(feed_block, plane.features_in(feed_block))
    grad_second = retreat(upstream, second_back_pre)
    layer_outputs = jnp.stack([first_out, second_out], axis=0)[None]
    input_grads = jnp.stack([grad_first, grad_second], axis=0)[None]
    return (layer_outputs, input_grads)


def solution(mesh):
    in_specs = (
        P("segment", "row", "col"),
        P("segment", "col"),
        P("segment", "row", "col"),
        P("row", "col"),
        P("segment", "row", "col"),
        P("row", "col"),
        P("segment", None, "row", "col"),
    )
    out_specs = (P("segment", None, "row", "col"), P("segment", None, "row", "col"))
    return jax.shard_map(shards, mesh=mesh, in_specs=in_specs, out_specs=out_specs, check_vma=False)
```

time: 246 us -> 156 us (0.63)
  waiting for transfers between devices: 161 us -> 39.3 us
  starting transfers between devices: 4.5 us -> 97.1 us
  matrix products: 49.3 us -> 10.3 us
  between operations: 13.8 us -> 1.57 us
  blocking collectives: 10.2 us -> 0 us
    all_gather x1 -> x0, waiting for transfers between devices: 156 us -> none  [shards(): weight_panel = lax.all_gather(weight_block, 'row', axis=0, tiled=True)]
    ppermute x2 -> x50, starting transfers between devices: 4.38 us -> 97.1 us  [the longest x24 60.5 us: plane_sent(): lax.ppermute(value, ('row', 'col'), [(a * cols + b, c * cols + d) for (a,...]
    dot_general x4 -> x12, matrix products: 49.3 us -> 10.3 us  [the longest x8 7.31 us: forward(): product = jnp.dot(full, weight, preferred_element_type=F32).astype(BF16)]
    ppermute x2 -> x50, waiting for transfers between devices: 4.52 us -> 39.3 us  [the longest x24 25.8 us: rows_swapped(): lax.ppermute(value, 'row', [(source, source ^ flip) for source in range(c...]
    all_gather x4 -> x0, blocking collectives: 10.2 us -> none  [the longest x2 5.84 us: widen(): lax.all_gather(pair[0], 'col', axis=1, tiled=True)]
  transfers between devices with their start and end apart: 5 -> 50, of which waited for: 3 -> 20; matrix products, arithmetic and copies ran while one was open for 9% -> 9% of each run, Pallas kernels for 0% -> 0%
where the time goes in v1:
time: 156 us; the launch traced here: 155 us
  starting transfers between devices  97.1 us (62%)
  waiting for transfers between devices  39.3 us (25%)
  matrix products  10.3 us (7%)
  other arithmetic  5.33 us (3%)
  between operations  1.57 us (1%)
    ppermute x24, starting transfers between devices, plane_sent(): lax.ppermute(value, ('row', 'col'), [(a * cols + b, c * cols + d) for (a,...  60.5 us
    ppermute x24, starting transfers between devices, rows_swapped(): lax.ppermute(value, 'row', [(source, source ^ flip) for source in range(c...  32 us
    ppermute x24, waiting for transfers between devices, rows_swapped(): lax.ppermute(value, 'row', [(source, source ^ flip) for source in range(c...  25.8 us
    ppermute x24, waiting for transfers between devices, plane_sent(): lax.ppermute(value, ('row', 'col'), [(a * cols + b, c * cols + d) for (a,...  12.1 us
    dot_general x8, matrix products, forward(): product = jnp.dot(full, weight, preferred_element_type=F32).astype(BF16)  7.31 us
    ppermute x2, starting transfers between devices, passed_along(): lax.ppermute(value, 'segment', [(source, source + steps) for source in ra...  4.6 us
  transfers between devices with their start and end apart: 50, of which 20 were waited for; matrix products, arithmetic and copies ran while one was open for 9% of the time, Pallas kernels for 0%

profile of v1, /device:TPU:1, one launch (start us, length us, event | category | flops | bytes accessed | tf_op | source)
XLA Modules:
  0.0 155.0 jit_solution(15005726595614058994)
XLA Ops:
  2.3 6.4 %collective-permute-start.2 = (bf16[64,1024]{1,0:T(8,128)(2,1)S(1)}, bf16[64,1024]{1,0:T(8,128)(2,1)S(1)}, u32[]{:S(2)}, u32[]{:S(2)}) collective-permute-start(bf16[64,1024]{1,0:T(8,128)(2,1)S(1)} %get-tuple-element.37), channel_id=1, source_target_pairs={{1,7},{3,5},{4,2},{6,0},{9,15},{11,13},{12,10},{14,8},{17,23},{19,... | collective-permute-start | bytes 393224 | tf_op jit(solution)/shard_map/ppermute | solution.py:28
  8.7 1.3 collective-permute-start.1
  11.1 1.8 %collective-permute-done.1 = bf16[64,1024]{1,0:T(8,128)(2,1)S(1)} collective-permute-done((bf16[64,1024]{1,0:T(8,128)(2,1)S(1)}, bf16[64,1024]{1,0:T(8,128)(2,1)S(1)}, u32[]{:S(2)}, u32[]{:S(2)}) %collective-permute-start.1) | collective-permute-done | bytes 131104 | tf_op jit(solution)/shard_map/ppermute | solution.py:28
  13.0 1.3 collective-permute-start.3
  15.0 7.0 %collective-permute-start.19 = (bf16[64,1024]{1,0:T(8,128)(2,1)S(1)}, bf16[64,1024]{1,0:T(8,128)(2,1)S(1)}, u32[]{:S(2)}, u32[]{:S(2)}) collective-permute-start(bf16[64,1024]{1,0:T(8,128)(2,1)S(1)} %get-tuple-element.31), channel_id=1, source_target_pairs={{1,7},{3,5},{4,2},{6,0},{9,15},{11,13},{12,10},{14,8},{17,23},{19,... | collective-permute-start | bytes 393224 | tf_op jit(solution)/shard_map/ppermute | solution.py:28
  22.0 1.3 collective-permute-start.18
  23.4 1.3 collective-permute-start.35
  26.1 6.2 %collective-permute-start.36 = (bf16[64,1024]{1,0:T(8,128)(2,1)S(1)}, bf16[64,1024]{1,0:T(8,128)(2,1)S(1)}, u32[]{:S(2)}, u32[]{:S(2)}) collective-permute-start(bf16[64,1024]{1,0:T(8,128)(2,1)S(1)} %get-tuple-element.33), channel_id=1, source_target_pairs={{1,7},{3,5},{4,2},{6,0},{9,15},{11,13},{12,10},{14,8},{17,23},{19,... | collective-permute-start | bytes 393224 | tf_op jit(solution)/shard_map/ppermute | solution.py:28
  32.4 1.6 %collective-permute-start.20 = (bf16[256,1024]{1,0:T(8,128)(2,1)S(1)}, bf16[256,1024]{1,0:T(8,128)(2,1)S(1)}, u32[]{:S(2)}, u32[]{:S(2)}) collective-permute-start(bf16[256,1024]{1,0:T(8,128)(2,1)S(1)} %pad_maximum_fusion.5), channel_id=1, source_target_pairs={{0,1},{2,3},{5,4},{7,6},{8,9},{10,11},{13,12},{15,14},{16,17},{18,... | collective-permute-start | bytes 1572872 | tf_op jit(solution)/shard_map/ppermute | solution.py:28
  34.0 1.6 %collective-permute-done.36 = bf16[64,1024]{1,0:T(8,128)(2,1)S(1)} collective-permute-done((bf16[64,1024]{1,0:T(8,128)(2,1)S(1)}, bf16[64,1024]{1,0:T(8,128)(2,1)S(1)}, u32[]{:S(2)}, u32[]{:S(2)}) %collective-permute-start.36) | collective-permute-done | bytes 131104 | tf_op jit(solution)/shard_map/ppermute | solution.py:28
  35.6 1.3 collective-permute-start.37
  36.9 2.3 %convolution_convert_fusion.7 = bf16[256,1024]{1,0:T(8,128)(2,1)S(1)} fusion(bf16[1024,2048]{1,0:T(8,128)(2,1)} %bitcast.40, bf16[256,1024]{1,0:T(8,128)(2,1)S(1)} %collective-permute-done.3, pred[]{:T(512)S(6)} %eq.10, bf16[64,1024]{1,0:T(8,128)(2,1)S(1)} %collective-permute-done.2, bf16[64,1024]{1,0:T(8,128)(2,1)S(1)} %collective-permute-done.1, ...), kind=kOutput, calls=%fused_computation.9 | convolution fusion | flops 539492352 | bytes 3670017 | tf_op jit(solution)/shard_map/dot_general | solution.py:118
  40.4 4.4 %collective-permute-start.6 = (bf16[128,1024]{1,0:T(8,128)(2,1)S(1)}, bf16[128,1024]{1,0:T(8,128)(2,1)S(1)}, u32[]{:S(2)}, u32[]{:S(2)}) collective-permute-start(bf16[128,1024]{1,0:T(8,128)(2,1)S(1)} %concatenate.144), channel_id=1, source_target_pairs={{0,4},{2,6},{4,0},{6,2},{1,5},{3,7},{5,1},{7,3},{8,12},{10,14},{12... | collective-permute-start | bytes 786440 | tf_op jit(solution)/shard_map/ppermute | solution.py:23
  47.4 1.3 collective-permute-start.38
  49.5 1.5 collective-permute-start.40
  51.1 1.6 %collective-permute-start.5 = (bf16[64,1024]{1,0:T(8,128)(2,1)S(1)}, bf16[64,1024]{1,0:T(8,128)(2,1)S(1)}, u32[]{:S(2)}, u32[]{:S(2)}) collective-permute-start(bf16[64,1024]{1,0:T(8,128)(2,1)S(1)} %add_convert_fusion.12), channel_id=1, source_target_pairs={{0,4},{2,6},{4,0},{6,2},{1,5},{3,7},{5,1},{7,3},{8,12},{10,14},{12... | collective-permute-start | bytes 393224 | tf_op jit(solution)/shard_map/ppermute | solution.py:23
  52.7 1.2 collective-permute-done.21
  54.2 1.9 %collective-permute-done.23 = bf16[128,1024]{1,0:T(8,128)(2,1)S(1)} collective-permute-done((bf16[128,1024]{1,0:T(8,128)(2,1)S(1)}, bf16[128,1024]{1,0:T(8,128)(2,1)S(1)}, u32[]{:S(2)}, u32[]{:S(2)}) %collective-permute-start.23) | collective-permute-done | bytes 262176 | tf_op jit(solution)/shard_map/ppermute | solution.py:23
  56.1 2.2 %collective-permute-start.22 = (bf16[64,1024]{1,0:T(8,128)(2,1)S(1)}, bf16[64,1024]{1,0:T(8,128)(2,1)S(1)}, u32[]{:S(2)}, u32[]{:S(2)}) collective-permute-start(bf16[64,1024]{1,0:T(8,128)(2,1)S(1)} %add_convert_fusion.8), channel_id=1, source_target_pairs={{0,4},{2,6},{4,0},{6,2},{1,5},{3,7},{5,1},{7,3},{8,12},{10,14},{12... | collective-permute-start | bytes 393224 | tf_op jit(solution)/shard_map/ppermute | solution.py:23
  58.4 1.2 collective-permute-done.38
  59.8 4.7 %collective-permute-done.5 = bf16[64,1024]{1,0:T(8,128)(2,1)S(1)} collective-permute-done((bf16[64,1024]{1,0:T(8,128)(2,1)S(1)}, bf16[64,1024]{1,0:T(8,128)(2,1)S(1)}, u32[]{:S(2)}, u32[]{:S(2)}) %collective-permute-start.5) | collective-permute-done | bytes 131104 | tf_op jit(solution)/shard_map/ppermute | solution.py:23
  64.5 2.2 %collective-permute-start.39 = (bf16[64,1024]{1,0:T(8,128)(2,1)S(1)}, bf16[64,1024]{1,0:T(8,128)(2,1)S(1)}, u32[]{:S(2)}, u32[]{:S(2)}) collective-permute-start(bf16[64,1024]{1,0:T(8,128)(2,1)S(1)} %add_convert_fusion.6), channel_id=1, source_target_pairs={{0,4},{2,6},{4,0},{6,2},{1,5},{3,7},{5,1},{7,3},{8,12},{10,14},{12... | collective-permute-start | bytes 393224 | tf_op jit(solution)/shard_map/ppermute | solution.py:23
  68.1 2.2 %collective-permute-start.27 = (bf16[64,1024]{1,0:T(8,128)(2,1)S(1)}, bf16[64,1024]{1,0:T(8,128)(2,1)S(1)}, u32[]{:S(2)}, u32[]{:S(2)}) collective-permute-start(bf16[64,1024]{1,0:T(8,128)(2,1)S(1)} %get-tuple-element.27), channel_id=1, source_target_pairs={{0,4},{2,6},{4,0},{6,2},{1,5},{3,7},{5,1},{7,3},{8,12},{10,14},{12... | collective-permute-start | bytes 393224 | tf_op jit(solution)/shard_map/ppermute | solution.py:23
  70.3 3.1 %collective-permute-start.8 = (bf16[64,2048]{1,0:T(8,128)(2,1)S(1)}, bf16[64,2048]{1,0:T(8,128)(2,1)S(1)}, u32[]{:S(2)}, u32[]{:S(2)}) collective-permute-start(bf16[64,2048]{1,0:T(8,128)(2,1)S(1)} %get-tuple-element.41), channel_id=1, source_target_pairs={{0,8},{8,16},{16,24},{1,9},{9,17},{17,25},{2,10},{10,18},{18,26},{... | collective-permute-start | bytes 786440 | tf_op jit(solution)/shard_map/ppermute | solution.py:18
  73.5 1.5 collective-permute-start.41
  75.2 1.5 collective-permute-done.8
  76.7 3.4 %collective-permute-start.11 = (bf16[64,1024]{1,0:T(8,128)(2,1)S(1)}, bf16[64,1024]{1,0:T(8,128)(2,1)S(1)}, u32[]{:S(2)}, u32[]{:S(2)}) collective-permute-start(bf16[64,1024]{1,0:T(8,128)(2,1)S(1)} %get-tuple-element.35), channel_id=1, source_target_pairs={{1,7},{3,5},{4,2},{6,0},{9,15},{11,13},{12,10},{14,8},{17,23},{19,... | collective-permute-start | bytes 393224 | tf_op jit(solution)/shard_map/ppermute | solution.py:28
  82.7 5.7 %collective-permute-start.10 = (bf16[64,1024]{1,0:T(8,128)(2,1)S(1)}, bf16[64,1024]{1,0:T(8,128)(2,1)S(1)}, u32[]{:S(2)}, u32[]{:S(2)}) collective-permute-start(bf16[64,1024]{1,0:T(8,128)(2,1)S(1)} %get-tuple-element.34), channel_id=1, source_target_pairs={{1,5},{3,7},{4,0},{6,2},{9,13},{11,15},{12,8},{14,10},{17,21},{19,... | collective-permute-start | bytes 393224 | tf_op jit(solution)/shard_map/ppermute | solution.py:28
  89.2 5.7 %collective-permute-start.29 = (bf16[256,1024]{1,0:T(8,128)(2,1)S(1)}, bf16[256,1024]{1,0:T(8,128)(2,1)S(1)}, u32[]{:S(2)}, u32[]{:S(2)}) collective-permute-start(bf16[256,1024]{1,0:T(8,128)(2,1)S(1)} %get-tuple-element.42), channel_id=1, source_target_pairs={{1,0},{3,2},{4,5},{6,7},{9,8},{11,10},{12,13},{14,15},{17,16},{19,... | collective-permute-start | bytes 1572872 | tf_op jit(solution)/shard_map/ppermute | solution.py:28
  95.0 1.3 collective-permute-start.12
  96.6 1.3 collective-permute-start.30
  98.6 1.3 collective-permute-start.32
  102.3 4.7 %collective-permute-start.15 = (bf16[128,1024]{1,0:T(8,128)(2,1)S(1)}, bf16[128,1024]{1,0:T(8,128)(2,1)S(1)}, u32[]{:S(2)}, u32[]{:S(2)}) collective-permute-start(bf16[128,1024]{1,0:T(8,128)(2,1)S(1)} %concatenate.145), channel_id=1, source_target_pairs={{0,4},{2,6},{4,0},{6,2},{1,5},{3,7},{5,1},{7,3},{8,12},{10,14},{12... | collective-permute-start | bytes 786440 | tf_op jit(solution)/shard_map/ppermute | solution.py:23
  107.1 1.5 collective-permute-start.33
  108.8 3.5 %collective-permute-start.14 = (bf16[64,1024]{1,0:T(8,128)(2,1)S(1)}, bf16[64,1024]{1,0:T(8,128)(2,1)S(1)}, u32[]{:S(2)}, u32[]{:S(2)}) collective-permute-start(bf16[64,1024]{1,0:T(8,128)(2,1)S(1)} %add_convert_fusion.10), channel_id=1, source_target_pairs={{0,4},{2,6},{4,0},{6,2},{1,5},{3,7},{5,1},{7,3},{8,12},{10,14},{12... | collective-permute-start | bytes 393224 | tf_op jit(solution)/shard_map/ppermute | solution.py:23
  113.0 2.7 %collective-permute-done.14 = bf16[64,1024]{1,0:T(8,128)(2,1)S(1)} collective-permute-done((bf16[64,1024]{1,0:T(8,128)(2,1)S(1)}, bf16[64,1024]{1,0:T(8,128)(2,1)S(1)}, u32[]{:S(2)}, u32[]{:S(2)}) %collective-permute-start.14) | collective-permute-done | bytes 131104 | tf_op jit(solution)/shard_map/ppermute | solution.py:23
  117.1 2.0 %collective-permute-start.44 = (bf16[64,1024]{1,0:T(8,128)(2,1)S(1)}, bf16[64,1024]{1,0:T(8,128)(2,1)S(1)}, u32[]{:S(2)}, u32[]{:S(2)}) collective-permute-start(bf16[64,1024]{1,0:T(8,128)(2,1)S(1)} %get-tuple-element.23), channel_id=1, source_target_pairs={{0,4},{2,6},{4,0},{6,2},{1,5},{3,7},{5,1},{7,3},{8,12},{10,14},{12... | collective-permute-start | bytes 393224 | tf_op jit(solution)/shard_map/ppermute | solution.py:23
  119.1 2.4 %collective-permute-done.44 = bf16[64,1024]{1,0:T(8,128)(2,1)S(1)} collective-permute-done((bf16[64,1024]{1,0:T(8,128)(2,1)S(1)}, bf16[64,1024]{1,0:T(8,128)(2,1)S(1)}, u32[]{:S(2)}, u32[]{:S(2)}) %collective-permute-start.44) | collective-permute-done | bytes 131104 | tf_op jit(solution)/shard_map/ppermute | solution.py:23
  121.7 1.3 collective-permute-start.42
  123.0 5.6 %collective-permute-done.42 = bf16[64,1024]{1,0:T(8,128)(2,1)S(1)} collective-permute-done((bf16[64,1024]{1,0:T(8,128)(2,1)S(1)}, bf16[64,1024]{1,0:T(8,128)(2,1)S(1)}, u32[]{:S(2)}, u32[]{:S(2)}) %collective-permute-start.42) | collective-permute-done | bytes 131104 | tf_op jit(solution)/shard_map/ppermute | solution.py:23
  128.6 1.1 collective-permute-start.43
  130.5 3.4 %collective-permute-done.43 = bf16[128,1024]{1,0:T(8,128)(2,1)S(1)} collective-permute-done((bf16[128,1024]{1,0:T(8,128)(2,1)S(1)}, bf16[128,1024]{1,0:T(8,128)(2,1)S(1)}, u32[]{:S(2)}, u32[]{:S(2)}) %collective-permute-start.43) | collective-permute-done | bytes 262176 | tf_op jit(solution)/shard_map/ppermute | solution.py:23
  134.6 7.6 %collective-permute-start.46 = (bf16[256,1024]{1,0:T(8,128)(2,1)S(1)}, bf16[256,1024]{1,0:T(8,128)(2,1)S(1)}, u32[]{:S(2)}, u32[]{:S(2)}) collective-permute-start(bf16[256,1024]{1,0:T(8,128)(2,1)S(1)} %get-tuple-element.44), channel_id=1, source_target_pairs={{1,0},{3,2},{4,5},{6,7},{9,8},{11,10},{12,13},{14,15},{17,16},{19,... | collective-permute-start | bytes 1572872 | tf_op jit(solution)/shard_map/ppermute | solution.py:28
  142.4 1.2 collective-permute-done.46
  143.9 1.3 collective-permute-start.47
  145.9 1.3 collective-permute-start.49
  148.0 2.5 %collective-permute-done.47 = bf16[64,1024]{1,0:T(8,128)(2,1)S(1)} collective-permute-done((bf16[64,1024]{1,0:T(8,128)(2,1)S(1)}, bf16[64,1024]{1,0:T(8,128)(2,1)S(1)}, u32[]{:S(2)}, u32[]{:S(2)}) %collective-permute-start.47) | collective-permute-done | bytes 131104 | tf_op jit(solution)/shard_map/ppermute | solution.py:28
  150.5 3.5 %collective-permute-done.49 = bf16[64,1024]{1,0:T(8,128)(2,1)S(1)} collective-permute-done((bf16[64,1024]{1,0:T(8,128)(2,1)S(1)}, bf16[64,1024]{1,0:T(8,128)(2,1)S(1)}, u32[]{:S(2)}, u32[]{:S(2)}) %collective-permute-start.49) | collective-permute-done | bytes 131104 | tf_op jit(solution)/shard_map/ppermute | solution.py:28
  (136 shorter events, 25.3 us)
Async XLA Ops:
  1.6 11.3 %collective-permute-start = (bf16[64,1024]{1,0:T(8,128)(2,1)S(1)}, bf16[64,1024]{1,0:T(8,128)(2,1)S(1)}, u32[]{:S(2)}, u32[]{:S(2)}) collective-permute-start(bf16[64,1024]{1,0:T(8,128)(2,1)S(1)} %get-tuple-element.37), channel_id=1, source_target_pairs={{0,2},{2,0},{5,7},{7,5},{8,10},{10,8},{13,15},{15,13},{16,18},{18,... | collective-permute-start | bytes 393224 | tf_op jit(solution)/shard_map/ppermute | solution.py:28
  2.3 10.6 %collective-permute-start.2 = (bf16[64,1024]{1,0:T(8,128)(2,1)S(1)}, bf16[64,1024]{1,0:T(8,128)(2,1)S(1)}, u32[]{:S(2)}, u32[]{:S(2)}) collective-permute-start(bf16[64,1024]{1,0:T(8,128)(2,1)S(1)} %get-tuple-element.37), channel_id=1, source_target_pairs={{1,7},{3,5},{4,2},{6,0},{9,15},{11,13},{12,10},{14,8},{17,23},{19,... | collective-permute-start | bytes 393224 | tf_op jit(solution)/shard_map/ppermute | solution.py:28
  8.7 4.2 %collective-permute-start.1 = (bf16[64,1024]{1,0:T(8,128)(2,1)S(1)}, bf16[64,1024]{1,0:T(8,128)(2,1)S(1)}, u32[]{:S(2)}, u32[]{:S(2)}) collective-permute-start(bf16[64,1024]{1,0:T(8,128)(2,1)S(1)} %get-tuple-element.36), channel_id=1, source_target_pairs={{1,5},{3,7},{4,0},{6,2},{9,13},{11,15},{12,8},{14,10},{17,21},{19,... | collective-permute-start | bytes 393224 | tf_op jit(solution)/shard_map/ppermute | solution.py:28
  13.0 23.9 %collective-permute-start.3 = (bf16[256,1024]{1,0:T(8,128)(2,1)S(1)}, bf16[256,1024]{1,0:T(8,128)(2,1)S(1)}, u32[]{:S(2)}, u32[]{:S(2)}) collective-permute-start(bf16[256,1024]{1,0:T(8,128)(2,1)S(1)} %pad_maximum_fusion), channel_id=1, source_target_pairs={{0,1},{2,3},{5,4},{7,6},{8,9},{10,11},{13,12},{15,14},{16,17},{18,... | collective-permute-start | bytes 1572872 | tf_op jit(solution)/shard_map/ppermute | solution.py:28
  14.3 11.7 %collective-permute-start.17 = (bf16[64,1024]{1,0:T(8,128)(2,1)S(1)}, bf16[64,1024]{1,0:T(8,128)(2,1)S(1)}, u32[]{:S(2)}, u32[]{:S(2)}) collective-permute-start(bf16[64,1024]{1,0:T(8,128)(2,1)S(1)} %get-tuple-element.31), channel_id=1, source_target_pairs={{0,2},{2,0},{5,7},{7,5},{8,10},{10,8},{13,15},{15,13},{16,18},{18,... | collective-permute-start | bytes 393224 | tf_op jit(solution)/shard_map/ppermute | solution.py:28
  15.0 17.3 %collective-permute-start.19 = (bf16[64,1024]{1,0:T(8,128)(2,1)S(1)}, bf16[64,1024]{1,0:T(8,128)(2,1)S(1)}, u32[]{:S(2)}, u32[]{:S(2)}) collective-permute-start(bf16[64,1024]{1,0:T(8,128)(2,1)S(1)} %get-tuple-element.31), channel_id=1, source_target_pairs={{1,7},{3,5},{4,2},{6,0},{9,15},{11,13},{12,10},{14,8},{17,23},{19,... | collective-permute-start | bytes 393224 | tf_op jit(solution)/shard_map/ppermute | solution.py:28
  23.4 10.6 %collective-permute-start.35 = (bf16[64,1024]{1,0:T(8,128)(2,1)S(1)}, bf16[64,1024]{1,0:T(8,128)(2,1)S(1)}, u32[]{:S(2)}, u32[]{:S(2)}) collective-permute-start(bf16[64,1024]{1,0:T(8,128)(2,1)S(1)} %get-tuple-element.32), channel_id=1, source_target_pairs={{1,5},{3,7},{4,0},{6,2},{9,13},{11,15},{12,8},{14,10},{17,21},{19,... | collective-permute-start | bytes 393224 | tf_op jit(solution)/shard_map/ppermute | solution.py:28
  25.4 8.6 %collective-permute-start.34 = (bf16[64,1024]{1,0:T(8,128)(2,1)S(1)}, bf16[64,1024]{1,0:T(8,128)(2,1)S(1)}, u32[]{:S(2)}, u32[]{:S(2)}) collective-permute-start(bf16[64,1024]{1,0:T(8,128)(2,1)S(1)} %get-tuple-element.33), channel_id=1, source_target_pairs={{0,2},{2,0},{5,7},{7,5},{8,10},{10,8},{13,15},{15,13},{16,18},{18,... | collective-permute-start | bytes 393224 | tf_op jit(solution)/shard_map/ppermute | solution.py:28
  26.1 9.5 %collective-permute-start.36 = (bf16[64,1024]{1,0:T(8,128)(2,1)S(1)}, bf16[64,1024]{1,0:T(8,128)(2,1)S(1)}, u32[]{:S(2)}, u32[]{:S(2)}) collective-permute-start(bf16[64,1024]{1,0:T(8,128)(2,1)S(1)} %get-tuple-element.33), channel_id=1, source_target_pairs={{1,7},{3,5},{4,2},{6,0},{9,15},{11,13},{12,10},{14,8},{17,23},{19,... | collective-permute-start | bytes 393224 | tf_op jit(solution)/shard_map/ppermute | solution.py:28
  32.4 12.4 %collective-permute-start.20 = (bf16[256,1024]{1,0:T(8,128)(2,1)S(1)}, bf16[256,1024]{1,0:T(8,128)(2,1)S(1)}, u32[]{:S(2)}, u32[]{:S(2)}) collective-permute-start(bf16[256,1024]{1,0:T(8,128)(2,1)S(1)} %pad_maximum_fusion.5), channel_id=1, source_target_pairs={{0,1},{2,3},{5,4},{7,6},{8,9},{10,11},{13,12},{15,14},{16,17},{18,... | collective-permute-start | bytes 1572872 | tf_op jit(solution)/shard_map/ppermute | solution.py:28
  35.6 11.0 %collective-permute-start.37 = (bf16[256,1024]{1,0:T(8,128)(2,1)S(1)}, bf16[256,1024]{1,0:T(8,128)(2,1)S(1)}, u32[]{:S(2)}, u32[]{:S(2)}) collective-permute-start(bf16[256,1024]{1,0:T(8,128)(2,1)S(1)} %pad_maximum_fusion.7), channel_id=1, source_target_pairs={{0,1},{2,3},{5,4},{7,6},{8,9},{10,11},{13,12},{15,14},{16,17},{18,... | collective-permute-start | bytes 1572872 | tf_op jit(solution)/shard_map/ppermute | solution.py:28
  39.3 10.2 %collective-permute-start.4 = (bf16[128,1024]{1,0:T(8,128)(2,1)S(1)}, bf16[128,1024]{1,0:T(8,128)(2,1)S(1)}, u32[]{:S(2)}, u32[]{:S(2)}) collective-permute-start(bf16[128,1024]{1,0:T(8,128)(2,1)S(1)} %pad_maximum_fusion.9), channel_id=1, source_target_pairs={{0,2},{2,0},{4,6},{6,4},{1,3},{3,1},{5,7},{7,5},{8,10},{10,8},{12,... | collective-permute-start | bytes 786440 | tf_op jit(solution)/shard_map/ppermute | solution.py:23
  40.4 10.8 %collective-permute-start.6 = (bf16[128,1024]{1,0:T(8,128)(2,1)S(1)}, bf16[128,1024]{1,0:T(8,128)(2,1)S(1)}, u32[]{:S(2)}, u32[]{:S(2)}) collective-permute-start(bf16[128,1024]{1,0:T(8,128)(2,1)S(1)} %concatenate.144), channel_id=1, source_target_pairs={{0,4},{2,6},{4,0},{6,2},{1,5},{3,7},{5,1},{7,3},{8,12},{10,14},{12... | collective-permute-start | bytes 786440 | tf_op jit(solution)/shard_map/ppermute | solution.py:23
  45.5 8.4 %collective-permute-start.21 = (bf16[128,1024]{1,0:T(8,128)(2,1)S(1)}, bf16[128,1024]{1,0:T(8,128)(2,1)S(1)}, u32[]{:S(2)}, u32[]{:S(2)}) collective-permute-start(bf16[128,1024]{1,0:T(8,128)(2,1)S(1)} %pad_maximum_fusion.11), channel_id=1, source_target_pairs={{0,2},{2,0},{4,6},{6,4},{1,3},{3,1},{5,7},{7,5},{8,10},{10,8},{12,... | collective-permute-start | bytes 786440 | tf_op jit(solution)/shard_map/ppermute | solution.py:23
  46.5 9.6 %collective-permute-start.23 = (bf16[128,1024]{1,0:T(8,128)(2,1)S(1)}, bf16[128,1024]{1,0:T(8,128)(2,1)S(1)}, u32[]{:S(2)}, u32[]{:S(2)}) collective-permute-start(bf16[128,1024]{1,0:T(8,128)(2,1)S(1)} %concatenate.146), channel_id=1, source_target_pairs={{0,4},{2,6},{4,0},{6,2},{1,5},{3,7},{5,1},{7,3},{8,12},{10,14},{12... | collective-permute-start | bytes 786440 | tf_op jit(solution)/shard_map/ppermute | solution.py:23
  47.4 12.2 %collective-permute-start.38 = (bf16[128,1024]{1,0:T(8,128)(2,1)S(1)}, bf16[128,1024]{1,0:T(8,128)(2,1)S(1)}, u32[]{:S(2)}, u32[]{:S(2)}) collective-permute-start(bf16[128,1024]{1,0:T(8,128)(2,1)S(1)} %pad_maximum_fusion.14), channel_id=1, source_target_pairs={{0,2},{2,0},{4,6},{6,4},{1,3},{3,1},{5,7},{7,5},{8,10},{10,8},{12,... | collective-permute-start | bytes 786440 | tf_op jit(solution)/shard_map/ppermute | solution.py:23
  49.5 23.9 %collective-permute-start.40 = (bf16[128,1024]{1,0:T(8,128)(2,1)S(1)}, bf16[128,1024]{1,0:T(8,128)(2,1)S(1)}, u32[]{:S(2)}, u32[]{:S(2)}) collective-permute-start(bf16[128,1024]{1,0:T(8,128)(2,1)S(1)} %concatenate.147), channel_id=1, source_target_pairs={{0,4},{2,6},{4,0},{6,2},{1,5},{3,7},{5,1},{7,3},{8,12},{10,14},{12... | collective-permute-start | bytes 786440 | tf_op jit(solution)/shard_map/ppermute | solution.py:23
  51.1 13.4 %collective-permute-start.5 = (bf16[64,1024]{1,0:T(8,128)(2,1)S(1)}, bf16[64,1024]{1,0:T(8,128)(2,1)S(1)}, u32[]{:S(2)}, u32[]{:S(2)}) collective-permute-start(bf16[64,1024]{1,0:T(8,128)(2,1)S(1)} %add_convert_fusion.12), channel_id=1, source_target_pairs={{0,4},{2,6},{4,0},{6,2},{1,5},{3,7},{5,1},{7,3},{8,12},{10,14},{12... | collective-permute-start | bytes 393224 | tf_op jit(solution)/shard_map/ppermute | solution.py:23
  54.0 12.8 %collective-permute-start.7 = (bf16[64,1024]{1,0:T(8,128)(2,1)S(1)}, bf16[64,1024]{1,0:T(8,128)(2,1)S(1)}, u32[]{:S(2)}, u32[]{:S(2)}) collective-permute-start(bf16[64,1024]{1,0:T(8,128)(2,1)S(1)} %add_convert_fusion.11), channel_id=1, source_target_pairs={{0,2},{2,0},{4,6},{6,4},{1,3},{3,1},{5,7},{7,5},{8,10},{10,8},{12,... | collective-permute-start | bytes 393224 | tf_op jit(solution)/shard_map/ppermute | solution.py:23
  56.1 11.2 %collective-permute-start.22 = (bf16[64,1024]{1,0:T(8,128)(2,1)S(1)}, bf16[64,1024]{1,0:T(8,128)(2,1)S(1)}, u32[]{:S(2)}, u32[]{:S(2)}) collective-permute-start(bf16[64,1024]{1,0:T(8,128)(2,1)S(1)} %add_convert_fusion.8), channel_id=1, source_target_pairs={{0,4},{2,6},{4,0},{6,2},{1,5},{3,7},{5,1},{7,3},{8,12},{10,14},{12... | collective-permute-start | bytes 393224 | tf_op jit(solution)/shard_map/ppermute | solution.py:23
  59.6 7.8 %collective-permute-start.24 = (bf16[64,1024]{1,0:T(8,128)(2,1)S(1)}, bf16[64,1024]{1,0:T(8,128)(2,1)S(1)}, u32[]{:S(2)}, u32[]{:S(2)}) collective-permute-start(bf16[64,1024]{1,0:T(8,128)(2,1)S(1)} %add_convert_fusion.7), channel_id=1, source_target_pairs={{0,2},{2,0},{4,6},{6,4},{1,3},{3,1},{5,7},{7,5},{8,10},{10,8},{12,... | collective-permute-start | bytes 393224 | tf_op jit(solution)/shard_map/ppermute | solution.py:23
  64.5 24.6 %collective-permute-start.39 = (bf16[64,1024]{1,0:T(8,128)(2,1)S(1)}, bf16[64,1024]{1,0:T(8,128)(2,1)S(1)}, u32[]{:S(2)}, u32[]{:S(2)}) collective-permute-start(bf16[64,1024]{1,0:T(8,128)(2,1)S(1)} %add_convert_fusion.6), channel_id=1, source_target_pairs={{0,4},{2,6},{4,0},{6,2},{1,5},{3,7},{5,1},{7,3},{8,12},{10,14},{12... | collective-permute-start | bytes 393224 | tf_op jit(solution)/shard_map/ppermute | solution.py:23
  67.9 7.0 %collective-permute-start.25 = (bf16[64,1024]{1,0:T(8,128)(2,1)S(1)}, bf16[64,1024]{1,0:T(8,128)(2,1)S(1)}, u32[]{:S(2)}, u32[]{:S(2)}) collective-permute-start(bf16[64,1024]{1,0:T(8,128)(2,1)S(1)} %get-tuple-element.26), channel_id=1, source_target_pairs={{0,2},{2,0},{4,6},{6,4},{1,3},{3,1},{5,7},{7,5},{8,10},{10,8},{12,... | collective-permute-start | bytes 393224 | tf_op jit(solution)/shard_map/ppermute | solution.py:23
  68.1 6.9 %collective-permute-start.27 = (bf16[64,1024]{1,0:T(8,128)(2,1)S(1)}, bf16[64,1024]{1,0:T(8,128)(2,1)S(1)}, u32[]{:S(2)}, u32[]{:S(2)}) collective-permute-start(bf16[64,1024]{1,0:T(8,128)(2,1)S(1)} %get-tuple-element.27), channel_id=1, source_target_pairs={{0,4},{2,6},{4,0},{6,2},{1,5},{3,7},{5,1},{7,3},{8,12},{10,14},{12... | collective-permute-start | bytes 393224 | tf_op jit(solution)/shard_map/ppermute | solution.py:23
  70.3 6.4 %collective-permute-start.8 = (bf16[64,2048]{1,0:T(8,128)(2,1)S(1)}, bf16[64,2048]{1,0:T(8,128)(2,1)S(1)}, u32[]{:S(2)}, u32[]{:S(2)}) collective-permute-start(bf16[64,2048]{1,0:T(8,128)(2,1)S(1)} %get-tuple-element.41), channel_id=1, source_target_pairs={{0,8},{8,16},{16,24},{1,9},{9,17},{17,25},{2,10},{10,18},{18,26},{... | collective-permute-start | bytes 786440 | tf_op jit(solution)/shard_map/ppermute | solution.py:18
  73.5 22.8 %collective-permute-start.41 = (bf16[64,1024]{1,0:T(8,128)(2,1)S(1)}, bf16[64,1024]{1,0:T(8,128)(2,1)S(1)}, u32[]{:S(2)}, u32[]{:S(2)}) collective-permute-start(bf16[64,1024]{1,0:T(8,128)(2,1)S(1)} %add_convert_fusion.5), channel_id=1, source_target_pairs={{0,2},{2,0},{4,6},{6,4},{1,3},{3,1},{5,7},{7,5},{8,10},{10,8},{12,... | collective-permute-start | bytes 393224 | tf_op jit(solution)/shard_map/ppermute | solution.py:23
  74.9 7.8 %collective-permute-start.26 = (bf16[128,1024]{1,0:T(8,128)(2,1)S(1)}, bf16[128,1024]{1,0:T(8,128)(2,1)S(1)}, u32[]{:S(2)}, u32[]{:S(2)}) collective-permute-start(bf16[128,1024]{1,0:T(8,128)(2,1)S(1)} %pad_maximum_fusion.12), channel_id=1, source_target_pairs={{0,4},{2,6},{4,0},{6,2},{1,5},{3,7},{5,1},{7,3},{8,12},{10,14},{12... | collective-permute-start | bytes 786440 | tf_op jit(solution)/shard_map/ppermute | solution.py:23
  75.0 6.2 %collective-permute-start.28 = (bf16[128,1024]{1,0:T(8,128)(2,1)S(1)}, bf16[128,1024]{1,0:T(8,128)(2,1)S(1)}, u32[]{:S(2)}, u32[]{:S(2)}) collective-permute-start(bf16[128,1024]{1,0:T(8,128)(2,1)S(1)} %pad_maximum_fusion.13), channel_id=1, source_target_pairs={{0,2},{2,0},{4,6},{6,4},{1,3},{3,1},{5,7},{7,5},{8,10},{10,8},{12,... | collective-permute-start | bytes 786440 | tf_op jit(solution)/shard_map/ppermute | solution.py:23
  76.7 18.2 %collective-permute-start.11 = (bf16[64,1024]{1,0:T(8,128)(2,1)S(1)}, bf16[64,1024]{1,0:T(8,128)(2,1)S(1)}, u32[]{:S(2)}, u32[]{:S(2)}) collective-permute-start(bf16[64,1024]{1,0:T(8,128)(2,1)S(1)} %get-tuple-element.35), channel_id=1, source_target_pairs={{1,7},{3,5},{4,2},{6,0},{9,15},{11,13},{12,10},{14,8},{17,23},{19,... | collective-permute-start | bytes 393224 | tf_op jit(solution)/shard_map/ppermute | solution.py:28
  81.2 13.7 %collective-permute-start.9 = (bf16[64,1024]{1,0:T(8,128)(2,1)S(1)}, bf16[64,1024]{1,0:T(8,128)(2,1)S(1)}, u32[]{:S(2)}, u32[]{:S(2)}) collective-permute-start(bf16[64,1024]{1,0:T(8,128)(2,1)S(1)} %get-tuple-element.35), channel_id=1, source_target_pairs={{0,2},{2,0},{5,7},{7,5},{8,10},{10,8},{13,15},{15,13},{16,18},{18,... | collective-permute-start | bytes 393224 | tf_op jit(solution)/shard_map/ppermute | solution.py:28
  82.7 12.2 %collective-permute-start.10 = (bf16[64,1024]{1,0:T(8,128)(2,1)S(1)}, bf16[64,1024]{1,0:T(8,128)(2,1)S(1)}, u32[]{:S(2)}, u32[]{:S(2)}) collective-permute-start(bf16[64,1024]{1,0:T(8,128)(2,1)S(1)} %get-tuple-element.34), channel_id=1, source_target_pairs={{1,5},{3,7},{4,0},{6,2},{9,13},{11,15},{12,8},{14,10},{17,21},{19,... | collective-permute-start | bytes 393224 | tf_op jit(solution)/shard_map/ppermute | solution.py:28
  89.2 7.2 %collective-permute-start.29 = (bf16[256,1024]{1,0:T(8,128)(2,1)S(1)}, bf16[256,1024]{1,0:T(8,128)(2,1)S(1)}, u32[]{:S(2)}, u32[]{:S(2)}) collective-permute-start(bf16[256,1024]{1,0:T(8,128)(2,1)S(1)} %get-tuple-element.42), channel_id=1, source_target_pairs={{1,0},{3,2},{4,5},{6,7},{9,8},{11,10},{12,13},{14,15},{17,16},{19,... | collective-permute-start | bytes 1572872 | tf_op jit(solution)/shard_map/ppermute | solution.py:28
  95.0 5.4 %collective-permute-start.12 = (bf16[256,1024]{1,0:T(8,128)(2,1)S(1)}, bf16[256,1024]{1,0:T(8,128)(2,1)S(1)}, u32[]{:S(2)}, u32[]{:S(2)}) collective-permute-start(bf16[256,1024]{1,0:T(8,128)(2,1)S(1)} %pad_maximum_fusion.3), channel_id=1, source_target_pairs={{0,1},{2,3},{5,4},{7,6},{8,9},{10,11},{13,12},{15,14},{16,17},{18,... | collective-permute-start | bytes 1572872 | tf_op jit(solution)/shard_map/ppermute | solution.py:28
  96.6 10.4 %collective-permute-start.30 = (bf16[64,1024]{1,0:T(8,128)(2,1)S(1)}, bf16[64,1024]{1,0:T(8,128)(2,1)S(1)}, u32[]{:S(2)}, u32[]{:S(2)}) collective-permute-start(bf16[64,1024]{1,0:T(8,128)(2,1)S(1)} %get-tuple-element.11), channel_id=1, source_target_pairs={{0,6},{2,4},{5,3},{7,1},{8,14},{10,12},{13,11},{15,9},{16,22},{18,... | collective-permute-start | bytes 393224 | tf_op jit(solution)/shard_map/ppermute | solution.py:28
  97.9 9.1 %collective-permute-start.31 = (bf16[64,1024]{1,0:T(8,128)(2,1)S(1)}, bf16[64,1024]{1,0:T(8,128)(2,1)S(1)}, u32[]{:S(2)}, u32[]{:S(2)}) collective-permute-start(bf16[64,1024]{1,0:T(8,128)(2,1)S(1)} %get-tuple-element.10), channel_id=1, source_target_pairs={{0,2},{2,0},{5,7},{7,5},{8,10},{10,8},{13,15},{15,13},{16,18},{18,... | collective-permute-start | bytes 393224 | tf_op jit(solution)/shard_map/ppermute | solution.py:28
  98.6 8.4 %collective-permute-start.32 = (bf16[64,1024]{1,0:T(8,128)(2,1)S(1)}, bf16[64,1024]{1,0:T(8,128)(2,1)S(1)}, u32[]{:S(2)}, u32[]{:S(2)}) collective-permute-start(bf16[64,1024]{1,0:T(8,128)(2,1)S(1)} %get-tuple-element.9), channel_id=1, source_target_pairs={{0,4},{2,6},{5,1},{7,3},{8,12},{10,14},{13,9},{15,11},{16,20},{18,... | collective-permute-start | bytes 393224 | tf_op jit(solution)/shard_map/ppermute | solution.py:28
  101.2 7.5 %collective-permute-start.13 = (bf16[128,1024]{1,0:T(8,128)(2,1)S(1)}, bf16[128,1024]{1,0:T(8,128)(2,1)S(1)}, u32[]{:S(2)}, u32[]{:S(2)}) collective-permute-start(bf16[128,1024]{1,0:T(8,128)(2,1)S(1)} %pad_maximum_fusion.10), channel_id=1, source_target_pairs={{0,2},{2,0},{4,6},{6,4},{1,3},{3,1},{5,7},{7,5},{8,10},{10,8},{12,... | collective-permute-start | bytes 786440 | tf_op jit(solution)/shard_map/ppermute | solution.py:23
  102.3 10.1 %collective-permute-start.15 = (bf16[128,1024]{1,0:T(8,128)(2,1)S(1)}, bf16[128,1024]{1,0:T(8,128)(2,1)S(1)}, u32[]{:S(2)}, u32[]{:S(2)}) collective-permute-start(bf16[128,1024]{1,0:T(8,128)(2,1)S(1)} %concatenate.145), channel_id=1, source_target_pairs={{0,4},{2,6},{4,0},{6,2},{1,5},{3,7},{5,1},{7,3},{8,12},{10,14},{12... | collective-permute-start | bytes 786440 | tf_op jit(solution)/shard_map/ppermute | solution.py:23
  107.1 9.5 %collective-permute-start.33 = (bf16[64,2048]{1,0:T(8,128)(2,1)S(1)}, bf16[64,2048]{1,0:T(8,128)(2,1)S(1)}, u32[]{:S(2)}, u32[]{:S(2)}) collective-permute-start(bf16[64,2048]{1,0:T(8,128)(2,1)S(1)} %fusion.18), channel_id=1, source_target_pairs={{8,0},{16,8},{24,16},{9,1},{17,9},{25,17},{10,2},{18,10},{26,18},{... | collective-permute-start | bytes 786440 | tf_op jit(solution)/shard_map/ppermute | solution.py:18
  108.8 6.9 %collective-permute-start.14 = (bf16[64,1024]{1,0:T(8,128)(2,1)S(1)}, bf16[64,1024]{1,0:T(8,128)(2,1)S(1)}, u32[]{:S(2)}, u32[]{:S(2)}) collective-permute-start(bf16[64,1024]{1,0:T(8,128)(2,1)S(1)} %add_convert_fusion.10), channel_id=1, source_target_pairs={{0,4},{2,6},{4,0},{6,2},{1,5},{3,7},{5,1},{7,3},{8,12},{10,14},{12... | collective-permute-start | bytes 393224 | tf_op jit(solution)/shard_map/ppermute | solution.py:23
  117.1 4.3 %collective-permute-start.44 = (bf16[64,1024]{1,0:T(8,128)(2,1)S(1)}, bf16[64,1024]{1,0:T(8,128)(2,1)S(1)}, u32[]{:S(2)}, u32[]{:S(2)}) collective-permute-start(bf16[64,1024]{1,0:T(8,128)(2,1)S(1)} %get-tuple-element.23), channel_id=1, source_target_pairs={{0,4},{2,6},{4,0},{6,2},{1,5},{3,7},{5,1},{7,3},{8,12},{10,14},{12... | collective-permute-start | bytes 393224 | tf_op jit(solution)/shard_map/ppermute | solution.py:23
  121.4 8.2 %collective-permute-start.45 = (bf16[128,1024]{1,0:T(8,128)(2,1)S(1)}, bf16[128,1024]{1,0:T(8,128)(2,1)S(1)}, u32[]{:S(2)}, u32[]{:S(2)}) collective-permute-start(bf16[128,1024]{1,0:T(8,128)(2,1)S(1)} %pad_maximum_fusion.16), channel_id=1, source_target_pairs={{0,2},{2,0},{4,6},{6,4},{1,3},{3,1},{5,7},{7,5},{8,10},{10,8},{12,... | collective-permute-start | bytes 786440 | tf_op jit(solution)/shard_map/ppermute | solution.py:23
  121.7 6.8 %collective-permute-start.42 = (bf16[64,1024]{1,0:T(8,128)(2,1)S(1)}, bf16[64,1024]{1,0:T(8,128)(2,1)S(1)}, u32[]{:S(2)}, u32[]{:S(2)}) collective-permute-start(bf16[64,1024]{1,0:T(8,128)(2,1)S(1)} %get-tuple-element.22), channel_id=1, source_target_pairs={{0,2},{2,0},{4,6},{6,4},{1,3},{3,1},{5,7},{7,5},{8,10},{10,8},{12,... | collective-permute-start | bytes 393224 | tf_op jit(solution)/shard_map/ppermute | solution.py:23
  128.6 5.3 %collective-permute-start.43 = (bf16[128,1024]{1,0:T(8,128)(2,1)S(1)}, bf16[128,1024]{1,0:T(8,128)(2,1)S(1)}, u32[]{:S(2)}, u32[]{:S(2)}) collective-permute-start(bf16[128,1024]{1,0:T(8,128)(2,1)S(1)} %pad_maximum_fusion.15), channel_id=1, source_target_pairs={{0,4},{2,6},{4,0},{6,2},{1,5},{3,7},{5,1},{7,3},{8,12},{10,14},{12... | collective-permute-start | bytes 786440 | tf_op jit(solution)/shard_map/ppermute | solution.py:23
  134.6 9.1 %collective-permute-start.46 = (bf16[256,1024]{1,0:T(8,128)(2,1)S(1)}, bf16[256,1024]{1,0:T(8,128)(2,1)S(1)}, u32[]{:S(2)}, u32[]{:S(2)}) collective-permute-start(bf16[256,1024]{1,0:T(8,128)(2,1)S(1)} %get-tuple-element.44), channel_id=1, source_target_pairs={{1,0},{3,2},{4,5},{6,7},{9,8},{11,10},{12,13},{14,15},{17,16},{19,... | collective-permute-start | bytes 1572872 | tf_op jit(solution)/shard_map/ppermute | solution.py:28
  143.9 6.6 %collective-permute-start.47 = (bf16[64,1024]{1,0:T(8,128)(2,1)S(1)}, bf16[64,1024]{1,0:T(8,128)(2,1)S(1)}, u32[]{:S(2)}, u32[]{:S(2)}) collective-permute-start(bf16[64,1024]{1,0:T(8,128)(2,1)S(1)} %get-tuple-element.8), channel_id=1, source_target_pairs={{0,6},{2,4},{5,3},{7,1},{8,14},{10,12},{13,11},{15,9},{16,22},{18,... | collective-permute-start | bytes 393224 | tf_op jit(solution)/shard_map/ppermute | solution.py:28
  145.2 5.3 %collective-permute-start.48 = (bf16[64,1024]{1,0:T(8,128)(2,1)S(1)}, bf16[64,1024]{1,0:T(8,128)(2,1)S(1)}, u32[]{:S(2)}, u32[]{:S(2)}) collective-permute-start(bf16[64,1024]{1,0:T(8,128)(2,1)S(1)} %get-tuple-element.7), channel_id=1, source_target_pairs={{0,2},{2,0},{5,7},{7,5},{8,10},{10,8},{13,15},{15,13},{16,18},{18,... | collective-permute-start | bytes 393224 | tf_op jit(solution)/shard_map/ppermute | solution.py:28
  145.9 8.2 %collective-permute-start.49 = (bf16[64,1024]{1,0:T(8,128)(2,1)S(1)}, bf16[64,1024]{1,0:T(8,128)(2,1)S(1)}, u32[]{:S(2)}, u32[]{:S(2)}) collective-permute-start(bf16[64,1024]{1,0:T(8,128)(2,1)S(1)} %get-tuple-element.6), channel_id=1, source_target_pairs={{0,4},{2,6},{5,1},{7,3},{8,12},{10,14},{13,9},{15,11},{16,20},{18,... | collective-permute-start | bytes 393224 | tf_op jit(solution)/shard_map/ppermute | solution.py:28
  (8 other events, 116.0 us)

commit v2 on v0

v2 whole, which is shorter than its diff:
```python
import jax
import jax.numpy as jnp
from jax import lax
from jax.sharding import PartitionSpec as P

F32 = jnp.float32
BF16 = jnp.bfloat16


def silu_slope(values):
    sigma = jax.nn.sigmoid(values)
    return sigma * (1.0 + values * (1.0 - sigma))


def passed_along(value, steps):
    count = lax.axis_size("segment")
    first, last = (max(0, -steps), min(count, count - steps))
    return lax.ppermute(value, "segment", [(source, source + steps) for source in range(first, last)])


def after(value, other):
    return lax.optimization_barrier((value, other))[0]


def bits_of(count):
    return count.bit_length() - 1


def xor_order(blocks, index):
    for bit in range(bits_of(len(blocks))):
        flip = 1 << bit
        is_set = (index & flip) != 0
        blocks = [
            jnp.where(is_set, blocks[k ^ flip], blocks[k]) for k in range(len(blocks))
        ]
    return blocks


def cut(value, count, axis=0):
    return jnp.split(value, count, axis=axis)


def row_swap(value, flip):
    count = lax.axis_size("row")
    return lax.ppermute(value, "row", [(source, source ^ flip) for source in range(count)])


def col_swap(value, flip):
    count = lax.axis_size("col")
    return lax.ppermute(value, "col", [(source, source ^ flip) for source in range(count)])


class Plane:
    def __init__(self, weight):
        self.weight = weight
        self.rows, self.cols = lax.axis_size("row"), lax.axis_size("col")
        self.row, self.col = lax.axis_index("row"), lax.axis_index("col")
        self.steps = bits_of(self.rows)

    def flips(self, col):
        return [1 << ((col + step) % self.steps) for step in range(self.steps)]

    def places(self, col):
        flips = self.flips(col)
        return [
            sum(flip for at, flip in enumerate(flips) if place >> (self.steps - 1 - at) & 1)
            for place in range(self.rows)
        ]

    def by_place(self, blocks):
        orders = [[blocks[k] for k in self.places(col)] for col in range(max(self.steps, 1))]
        return self.choose(orders)

    def by_k(self, blocks):
        orders = []
        for col in range(max(self.steps, 1)):
            places = self.places(col)
            orders.append([blocks[places.index(k)] for k in range(self.rows)])
        return self.choose(orders)

    def choose(self, orders):
        chosen = orders[0]
        for at in range(1, len(orders)):
            picked = self.col % len(orders) == at
            chosen = [
                old if old is new else jnp.where(picked, new, old)
                for old, new in zip(chosen, orders[at])
            ]
        return chosen

    def step_swap(self, value, step):
        pairs = []
        for row in range(self.rows):
            for col in range(self.cols):
                other = row ^ self.flips(col)[step]
                pairs.append((row * self.cols + col, other * self.cols + col))
        return lax.ppermute(value, ("row", "col"), pairs)

    def exchanged(self, value):
        return [value] + [col_swap(value, flip) for flip in range(1, self.cols)]

    def wanted(self, columns):
        mine = xor_order(cut(columns, self.cols), self.col)[0]
        return xor_order(cut(mine, self.rows, axis=1), self.row)

    def sent(self, blocks):
        return blocks[:1] + [row_swap(blocks[k], k) for k in range(1, self.rows)]

    def spread(self, block):
        parts = xor_order(cut(block, self.cols), self.col)
        pieces = [parts[0]] + [col_swap(parts[flip], flip) for flip in range(1, self.cols)]
        columns = jnp.concatenate(xor_order(pieces, self.col), axis=1)
        return self.sent(xor_order(cut(columns, self.rows, axis=1), self.row))

    def joined(self, arrived):
        half = jnp.concatenate(arrived, axis=0)
        halves = [half] + [col_swap(half, flip) for flip in range(1, self.cols)]
        ordered = [cut(h, self.rows) for h in xor_order(halves, self.col)]
        return [jnp.concatenate([h[k] for h in ordered], axis=0) for k in range(self.rows)]

    def product(self, blocks):
        full = jnp.concatenate(self.by_place(blocks), axis=0)
        return jnp.dot(full, self.weight, preferred_element_type=F32).astype(BF16)

    def summed(self, partial, waits=()):
        total, messages = partial, []
        for step in range(self.steps):
            ours, away = cut(total, 2)
            messages.append(away.astype(BF16))
            arrived = self.step_swap(messages[-1], step)
            if step < len(waits):
                arrived = after(arrived, waits[step])
            total = ours.astype(F32) + arrived.astype(F32)
        return total.astype(F32), messages

    def gathered(self, block):
        messages = []
        for step in reversed(range(self.steps)):
            messages.append(block)
            block = jnp.concatenate([block, self.step_swap(block, step)], axis=0)
        return block, messages

    def returned(self, scaled):
        partial = lax.dot_general(
            scaled, self.weight, (((1,), (1,)), ((), ())), preferred_element_type=F32
        ).astype(BF16)
        blocks = [cut(block, self.cols) for block in self.by_k(cut(partial, self.rows))]
        shares = xor_order(
            [jnp.concatenate([b[at] for b in blocks], axis=0) for at in range(self.cols)], self.col
        )
        total = shares[0].astype(F32)
        for flip in range(1, self.cols):
            total = total + col_swap(shares[flip], flip).astype(F32)
        total = total.astype(BF16)
        arrived = self.sent(cut(total, self.rows))
        columns = jnp.concatenate(xor_order(arrived, self.row), axis=1)
        pieces = xor_order(cut(columns, self.cols, axis=1), self.col)
        last = pieces[0]
        pieces = pieces[:1] + [col_swap(pieces[flip], flip) for flip in range(1, self.cols)]
        return jnp.concatenate(xor_order(pieces, self.col), axis=0), [shares[0], total, last]


def shards(weights, layer_gains, incoming, fresh_batch, returning, fresh_cotangent, stashed_inputs):
    segment_index = lax.axis_index("segment")
    segment_count = lax.axis_size("segment")
    plane = Plane(weights[0])
    layer_gain = layer_gains[0][None, :]

    def advance(own_block, pre_act):
        return (own_block.astype(F32) + layer_gain * jax.nn.silu(pre_act)).astype(BF16)

    def scale(upstream, pre_act):
        return (upstream.astype(F32) * layer_gain * silu_slope(pre_act)).astype(BF16)

    def retreat(upstream, back_term):
        return (upstream.astype(F32) + back_term.astype(F32)).astype(BF16)

    def side_by_side(pieces):
        return jnp.concatenate(xor_order(pieces, plane.col), axis=-1)

    stored = side_by_side(plane.exchanged(stashed_inputs[0]))
    entering = side_by_side(plane.exchanged(incoming[0]))
    batches = [stored[0], entering, stored[1]]
    spread = plane.sent(
        [jnp.concatenate(blocks, axis=0) for blocks in zip(*map(plane.wanted, batches))]
    )
    spread = [cut(block, len(batches)) for block in spread]
    first_spread = [block[0] for block in spread]
    rest_spread = [jnp.concatenate(block[1:], axis=0) for block in spread]

    first_back = plane.product(plane.joined(first_spread))
    back_pre, back_sent = plane.summed(first_back)
    scaled_first = scale(returning[0], back_pre)
    gathered_first, gather_sent = plane.gathered(scaled_first)
    back_first, return_sent = plane.returned(gathered_first)
    grad_first = retreat(returning[0], back_first)

    rest = plane.joined([after(block, back_sent[0]) for block in rest_spread])
    rest = [cut(block, 2 * plane.cols) for block in rest]
    entered = [jnp.concatenate(block[0::2], axis=0) for block in rest]
    second_stored = [jnp.concatenate(block[1::2], axis=0) for block in rest]
    first_pre, _ = plane.summed(plane.product(entered), [gather_sent[0], gather_sent[1]])
    first_out = advance(incoming[0], first_pre)
    arrived = passed_along(first_out, 1)
    second_back_pre, _ = plane.summed(
        plane.product([after(block, first_out) for block in second_stored]),
        [return_sent[1], grad_first],
    )
    feed_block = jnp.where(segment_index == 0, fresh_batch, after(arrived, return_sent[0]))
    feed_spread = [after(block, grad_first) for block in plane.spread(feed_block)]
    second_partial = plane.product(plane.joined(feed_spread))

    arrived_grad = after(passed_along(grad_first, -1), first_out)
    upstream = jnp.where(segment_index == segment_count - 1, fresh_cotangent, arrived_grad)
    scaled_second = scale(upstream, second_back_pre)
    gathered_second, gather_sent = plane.gathered(scaled_second)
    back_second, return_sent = plane.returned(gathered_second)
    grad_second = retreat(upstream, back_second)
    second_pre, _ = plane.summed(second_partial, [gather_sent[0], return_sent[0]])
    second_out = advance(feed_block, second_pre)
    layer_outputs = jnp.stack([first_out, second_out], axis=0)[None]
    input_grads = jnp.stack([grad_first, grad_second], axis=0)[None]
    return (layer_outputs, input_grads)


def solution(mesh):
    in_specs = (
        P("segment", "row", "col"),
        P("segment", "col"),
        P("segment", "row", "col"),
        P("row", "col"),
        P("segment", "row", "col"),
        P("row", "col"),
        P("segment", None, "row", "col"),
    )
    out_specs = (P("segment", None, "row", "col"), P("segment", None, "row", "col"))
    return jax.shard_map(shards, mesh=mesh, in_specs=in_specs, out_specs=out_specs, check_vma=False)
```

time: 246 us -> 123 us (0.50)
  waiting for transfers between devices: 161 us -> 64.7 us
  matrix products: 49.3 us -> 9.88 us
  starting transfers between devices: 4.5 us -> 38.9 us
  between operations: 13.8 us -> 1.37 us
  blocking collectives: 10.2 us -> 0 us
  other arithmetic: 3.77 us -> 7.18 us
    all_gather x1 -> x0, waiting for transfers between devices: 156 us -> none  [shards(): weight_panel = lax.all_gather(weight_block, 'row', axis=0, tiled=True)]
    ppermute x2 -> x36, waiting for transfers between devices: 4.52 us -> 64.7 us  [the longest x12 43.7 us: step_swap(): return lax.ppermute(value, ('row', 'col'), pairs)]
    dot_general x4 -> x6, matrix products: 49.3 us -> 9.88 us  [the longest x4 7.32 us: product(): return jnp.dot(full, self.weight, preferred_element_type=F32).astype(BF16)]
    ppermute x2 -> x36, starting transfers between devices: 4.38 us -> 38.9 us  [the longest x10 13 us: col_swap(): lax.ppermute(value, 'col', [(source, source ^ flip) for source in range(c...]
    all_gather x4 -> x0, blocking collectives: 10.2 us -> none  [the longest x2 5.84 us: widen(): lax.all_gather(pair[0], 'col', axis=1, tiled=True)]
    select_n x1 -> x25, other arithmetic: 0.03 us -> 3.17 us  [the longest x21 3.07 us: xor_order(): jnp.where(is_set, blocks[k ^ flip], blocks[k])]
  transfers between devices with their start and end apart: 5 -> 36, of which waited for: 3 -> 25; matrix products, arithmetic and copies ran while one was open for 9% -> 8% of each run, Pallas kernels for 0% -> 0%
where the time goes in v2:
time: 123 us
  waiting for transfers between devices  64.7 us (53%)
  starting transfers between devices  38.9 us (32%)
  matrix products  9.88 us (8%)
  other arithmetic  7.18 us (6%)
  between operations  1.37 us (1%)
    ppermute x12, waiting for transfers between devices, step_swap(): return lax.ppermute(value, ('row', 'col'), pairs)  43.7 us
    ppermute x12, waiting for transfers between devices, row_swap(): lax.ppermute(value, 'row', [(source, source ^ flip) for source in range(c...  13.8 us
    ppermute x10, starting transfers between devices, col_swap(): lax.ppermute(value, 'col', [(source, source ^ flip) for source in range(c...  13 us
    ppermute x12, starting transfers between devices, row_swap(): lax.ppermute(value, 'row', [(source, source ^ flip) for source in range(c...  11.9 us
    ppermute x12, starting transfers between devices, step_swap(): return lax.ppermute(value, ('row', 'col'), pairs)  9.25 us
    dot_general x4, matrix products, product(): return jnp.dot(full, self.weight, preferred_element_type=F32).astype(BF16)  7.32 us
    ppermute x2, starting transfers between devices, passed_along(): lax.ppermute(value, 'segment', [(source, source + steps) for source in ra...  4.69 us
    ppermute x2, waiting for transfers between devices, passed_along(): lax.ppermute(value, 'segment', [(source, source + steps) for source in ra...  3.82 us
  transfers between devices with their start and end apart: 36, of which 25 were waited for; matrix products, arithmetic and copies ran while one was open for 8% of the time, Pallas kernels for 0%

profile of v2, /device:TPU:1, one launch (start us, length us, event | category | flops | bytes accessed | tf_op | source)
XLA Modules:
  0.0 122.7 jit_solution(18212556038699855943)
XLA Ops:
  1.2 1.2 %collective-permute-done = bf16[64,2048]{1,0:T(8,128)(2,1)S(1)} collective-permute-done((bf16[64,2048]{1,0:T(8,128)(2,1)}, bf16[64,2048]{1,0:T(8,128)(2,1)S(1)}, u32[]{:S(2)}, u32[]{:S(2)}) %collective-permute-start) | collective-permute-done | bytes 262176 | tf_op jit(solution)/shard_map/ppermute | solution.py:50
  2.4 1.0 broadcast_select_fusion.14
  3.6 1.1 broadcast_select_fusion
  4.9 2.4 %collective-permute-start.2 = (bf16[96,1024]{1,0:T(8,128)(2,1)S(1)}, bf16[96,1024]{1,0:T(8,128)(2,1)S(1)}, u32[]{:S(2)}, u32[]{:S(2)}) collective-permute-start(bf16[96,1024]{1,0:T(8,128)(2,1)S(1)} %pad_maximum_fusion.9), channel_id=1, source_target_pairs={{0,2},{2,0},{4,6},{6,4},{1,3},{3,1},{5,7},{7,5},{8,10},{10,8},{12,... | collective-permute-start | bytes 589832 | tf_op jit(solution)/shard_map/ppermute | solution.py:45
  7.3 1.3 %collective-permute-start.3 = (bf16[96,1024]{1,0:T(8,128)(2,1)S(1)}, bf16[96,1024]{1,0:T(8,128)(2,1)S(1)}, u32[]{:S(2)}, u32[]{:S(2)}) collective-permute-start(bf16[96,1024]{1,0:T(8,128)(2,1)S(1)} %pad_maximum_fusion.10), channel_id=1, source_target_pairs={{0,4},{2,6},{4,0},{6,2},{1,5},{3,7},{5,1},{7,3},{8,12},{10,14},{12... | collective-permute-start | bytes 589832 | tf_op jit(solution)/shard_map/ppermute | solution.py:45
  8.7 3.6 %collective-permute-done.2 = bf16[96,1024]{1,0:T(8,128)(2,1)S(1)} collective-permute-done((bf16[96,1024]{1,0:T(8,128)(2,1)S(1)}, bf16[96,1024]{1,0:T(8,128)(2,1)S(1)}, u32[]{:S(2)}, u32[]{:S(2)}) %collective-permute-start.2) | collective-permute-done | bytes 196640 | tf_op jit(solution)/shard_map/ppermute | solution.py:45
  12.3 4.0 %collective-permute-done.3 = bf16[96,1024]{1,0:T(8,128)(2,1)S(1)} collective-permute-done((bf16[96,1024]{1,0:T(8,128)(2,1)S(1)}, bf16[96,1024]{1,0:T(8,128)(2,1)S(1)}, u32[]{:S(2)}, u32[]{:S(2)}) %collective-permute-start.3) | collective-permute-done | bytes 196640 | tf_op jit(solution)/shard_map/ppermute | solution.py:45
  16.3 1.1 collective-permute-done.4
  17.5 1.6 %collective-permute-start.5 = (bf16[128,1024]{1,0:T(8,128)(2,1)S(1)}, bf16[128,1024]{1,0:T(8,128)(2,1)S(1)}, u32[]{:S(2)}, u32[]{:S(2)}) collective-permute-start(bf16[128,1024]{1,0:T(8,128)(2,1)S(1)} %pad_maximum_fusion.4), channel_id=1, source_target_pairs={{0,1},{1,0},{2,3},{3,2},{4,5},{5,4},{6,7},{7,6},{8,9},{9,8},{10,11... | collective-permute-start | bytes 786440 | tf_op jit(solution)/shard_map/ppermute | solution.py:50
  19.0 1.2 collective-permute-done.5
  20.5 3.5 %fusion.12 = bf16[256,2048]{1,0:T(8,128)(2,1)S(1)} fusion(bf16[256,1024]{1,0:T(8,128)(2,1)S(1)} %slice_dynamic-update-slice_fusion.8, bf16[1,1024,2048]{2,1,0:T(8,128)(2,1)} %param.7), kind=kOutput, calls=%fused_computation.12 | convolution fusion | flops 1074266112 | bytes 5767168 | tf_op jit(solution)/shard_map/dot_general | solution.py:123
  24.0 1.3 %collective-permute-start.8 = (bf16[128,2048]{1,0:T(8,128)(2,1)S(1)}, bf16[128,2048]{1,0:T(8,128)(2,1)S(1)}, u32[]{:S(2)}, u32[]{:S(2)}) collective-permute-start(bf16[128,2048]{1,0:T(8,128)(2,1)S(1)} %split.469), channel_id=1, source_target_pairs={{0,2},{1,5},{2,0},{3,7},{4,6},{5,1},{6,4},{7,3},{8,10},{9,13},{10,... | collective-permute-start | bytes 1572872 | tf_op jit(solution)/shard_map/ppermute | solution.py:97
  25.8 6.6 %collective-permute-done.8 = bf16[128,2048]{1,0:T(8,128)(2,1)S(1)} collective-permute-done((bf16[128,2048]{1,0:T(8,128)(2,1)S(1)}, bf16[128,2048]{1,0:T(8,128)(2,1)S(1)}, u32[]{:S(2)}, u32[]{:S(2)}) %collective-permute-start.8) | collective-permute-done | bytes 524320 | tf_op jit(solution)/shard_map/ppermute | solution.py:97
  32.6 0.9 collective-permute-start.9
  33.8 1.3 %fusion.15 = bf16[256,2048]{1,0:T(8,128)(2,1)S(1)} fusion(bf16[256,1024]{1,0:T(8,128)(2,1)S(1)} %get-tuple-element.67, bf16[1,1024,2048]{2,1,0:T(8,128)(2,1)S(1)} %copy-done.5), kind=kOutput, calls=%fused_computation.13 | convolution fusion | flops 1074266112 | bytes 5767168 | tf_op jit(solution)/shard_map/dot_general | solution.py:123
  35.9 2.3 %collective-permute-done.9 = bf16[64,2048]{1,0:T(8,128)(2,1)S(1)} collective-permute-done((bf16[64,2048]{1,0:T(8,128)(2,1)S(1)}, bf16[64,2048]{1,0:T(8,128)(2,1)S(1)}, u32[]{:S(2)}, u32[]{:S(2)}) %collective-permute-start.9) | collective-permute-done | bytes 262176 | tf_op jit(solution)/shard_map/ppermute | solution.py:97
  38.4 0.9 collective-permute-start.11
  39.3 6.1 %collective-permute-done.7 = bf16[128,2048]{1,0:T(8,128)(2,1)S(1)} collective-permute-done((bf16[128,2048]{1,0:T(8,128)(2,1)S(1)}, bf16[128,2048]{1,0:T(8,128)(2,1)S(1)}, u32[]{:S(2)}, u32[]{:S(2)}) %collective-permute-start.7) | collective-permute-done | bytes 524320 | tf_op jit(solution)/shard_map/ppermute | solution.py:97
  45.6 0.9 collective-permute-start.10
  46.8 1.4 %collective-permute-start.13 = (bf16[128,2048]{1,0:T(8,128)(2,1)S(1)}, bf16[128,2048]{1,0:T(8,128)(2,1)S(1)}, u32[]{:S(2)}, u32[]{:S(2)}) collective-permute-start(bf16[128,2048]{1,0:T(8,128)(2,1)S(1)} %pad_maximum_fusion), channel_id=1, source_target_pairs={{0,2},{1,5},{2,0},{3,7},{4,6},{5,1},{6,4},{7,3},{8,10},{9,13},{10,... | collective-permute-start | bytes 1572872 | tf_op jit(solution)/shard_map/ppermute | solution.py:97
  48.2 3.0 %collective-permute-done.10 = bf16[64,2048]{1,0:T(8,128)(2,1)S(1)} collective-permute-done((bf16[64,2048]{1,0:T(8,128)(2,1)S(1)}, bf16[64,2048]{1,0:T(8,128)(2,1)S(1)}, u32[]{:S(2)}, u32[]{:S(2)}) %collective-permute-start.10) | collective-permute-done | bytes 262176 | tf_op jit(solution)/shard_map/ppermute | solution.py:97
  51.5 3.2 %collective-permute-start.12 = (bf16[64,2048]{1,0:T(8,128)(2,1)S(1)}, bf16[64,2048]{1,0:T(8,128)(2,1)S(1)}, u32[]{:S(2)}, u32[]{:S(2)}) collective-permute-start(bf16[64,2048]{1,0:T(8,128)(2,1)S(1)} %add_convert_fusion.3), channel_id=1, source_target_pairs={{0,8},{8,16},{16,24},{1,9},{9,17},{17,25},{2,10},{10,18},{18,26},{... | collective-permute-start | bytes 786440 | tf_op jit(solution)/shard_map/ppermute | solution.py:18
  54.7 2.9 %collective-permute-done.13 = bf16[128,2048]{1,0:T(8,128)(2,1)S(1)} collective-permute-done((bf16[128,2048]{1,0:T(8,128)(2,1)S(1)}, bf16[128,2048]{1,0:T(8,128)(2,1)S(1)}, u32[]{:S(2)}, u32[]{:S(2)}) %collective-permute-start.13) | collective-permute-done | bytes 524320 | tf_op jit(solution)/shard_map/ppermute | solution.py:97
  57.6 1.3 %fusion.24 = bf16[256,1024]{1,0:T(8,128)(2,1)S(1)} fusion(bf16[1,1024,2048]{2,1,0:T(8,128)(2,1)S(1)} %copy-done.5, bf16[128,2048]{1,0:T(8,128)(2,1)S(1)} %collective-permute-done.13, bf16[64,2048]{1,0:T(8,128)(2,1)S(1)} %collective-permute-done.11, bf16[64,2048]{1,0:T(8,128)(2,1)S(1)} %fusion.46), kind=kOutput, calls=%fused_computation.22 | convolution fusion | flops 1077149696 | bytes 5767168 | tf_op jit(solution)/shard_map/dot_general | solution.py:144
  59.1 4.6 %collective-permute-start.15 = (bf16[128,1024]{1,0:T(8,128)(2,1)S(1)}, bf16[128,1024]{1,0:T(8,128)(2,1)S(1)}, u32[]{:S(2)}, u32[]{:S(2)}) collective-permute-start(bf16[128,1024]{1,0:T(8,128)(2,1)S(1)} %broadcast_select_fusion.10), channel_id=1, source_target_pairs={{0,1},{1,0},{2,3},{3,2},{4,5},{5,4},{6,7},{7,6},{8,9},{9,8},{10,11... | collective-permute-start | bytes 786440 | tf_op jit(solution)/shard_map/ppermute | solution.py:50
  63.7 1.3 %fusion.21 = bf16[256,2048]{1,0:T(8,128)(2,1)S(1)} fusion(bf16[1,1024,2048]{2,1,0:T(8,128)(2,1)S(1)} %copy-done.5, bf16[64,1024]{1,0:T(8,128)(2,1)S(1)} %get-tuple-element.37, bf16[64,1024]{1,0:T(8,128)(2,1)S(1)} %get-tuple-element.104, bf16[64,1024]{1,0:T(8,128)(2,1)S(1)} %get-tuple-element.103, bf16[64,1024]{1,0:T(8,128)(2,1)S(1)} %get-tuple-element.34), kind=kOutput, calls=%fused_computation.15 | convolution fusion | flops 1076363264 | bytes 5767168 | tf_op jit(solution)/shard_map/dot_general | solution.py:123
  65.7 1.3 %collective-permute-start.16 = (bf16[32,1024]{1,0:T(8,128)(2,1)S(1)}, bf16[32,1024]{1,0:T(8,128)(2,1)S(1)}, u32[]{:S(2)}, u32[]{:S(2)}) collective-permute-start(bf16[32,1024]{1,0:T(8,128)(2,1)S(1)} %get-tuple-element.117), channel_id=1, source_target_pairs={{0,6},{2,4},{4,2},{6,0},{1,7},{3,5},{5,3},{7,1},{8,14},{10,12},{12... | collective-permute-start | bytes 196616 | tf_op jit(solution)/shard_map/ppermute | solution.py:45
  68.5 1.2 %collective-permute-start.14 = (bf16[32,2048]{1,0:T(8,128)(2,1)S(1)}, bf16[32,2048]{1,0:T(8,128)(2,1)S(1)}, u32[]{:S(2)}, u32[]{:S(2)}) collective-permute-start(bf16[32,2048]{1,0:T(8,128)(2,1)S(1)} %broadcast_select_fusion.26), channel_id=1, source_target_pairs={{0,1},{1,0},{2,3},{3,2},{4,5},{5,4},{6,7},{7,6},{8,9},{9,8},{10,11... | collective-permute-start | bytes 393224 | tf_op jit(solution)/shard_map/ppermute | solution.py:50
  69.7 5.1 %collective-permute-done.26 = bf16[128,2048]{1,0:T(8,128)(2,1)S(1)} collective-permute-done((bf16[128,2048]{1,0:T(8,128)(2,1)S(1)}, bf16[128,2048]{1,0:T(8,128)(2,1)S(1)}, u32[]{:S(2)}, u32[]{:S(2)}) %collective-permute-start.26) | collective-permute-done | bytes 524320 | tf_op jit(solution)/shard_map/ppermute | solution.py:97
  76.3 0.9 collective-permute-start.19
  77.3 1.0 collective-permute-start.22
  79.0 1.0 collective-permute-start.20
  80.2 1.5 %collective-permute-start.25 = (bf16[64,2048]{1,0:T(8,128)(2,1)S(1)}, bf16[64,2048]{1,0:T(8,128)(2,1)S(1)}, u32[]{:S(2)}, u32[]{:S(2)}) collective-permute-start(bf16[64,2048]{1,0:T(8,128)(2,1)S(1)} %fusion.47), channel_id=1, source_target_pairs={{8,0},{16,8},{24,16},{9,1},{17,9},{25,17},{10,2},{18,10},{26,18},{... | collective-permute-start | bytes 786440 | tf_op jit(solution)/shard_map/ppermute | solution.py:18
  81.7 1.1 collective-permute-done.20
  82.8 1.2 collective-permute-done.21
  83.9 1.3 %collective-permute-start.23 = (bf16[128,1024]{1,0:T(8,128)(2,1)S(1)}, bf16[128,1024]{1,0:T(8,128)(2,1)S(1)}, u32[]{:S(2)}, u32[]{:S(2)}) collective-permute-start(bf16[128,1024]{1,0:T(8,128)(2,1)S(1)} %constant_dynamic-update-slice_fusion.4), channel_id=1, source_target_pairs={{0,1},{1,0},{2,3},{3,2},{4,5},{5,4},{6,7},{7,6},{8,9},{9,8},{10,11... | collective-permute-start | bytes 786440 | tf_op jit(solution)/shard_map/ppermute | solution.py:50
  85.2 3.8 %collective-permute-done.25 = bf16[64,2048]{1,0:T(8,128)(2,1)S(1)} collective-permute-done((bf16[64,2048]{1,0:T(8,128)(2,1)S(1)}, bf16[64,2048]{1,0:T(8,128)(2,1)S(1)}, u32[]{:S(2)}, u32[]{:S(2)}) %collective-permute-start.25) | collective-permute-done | bytes 262176 | tf_op jit(solution)/shard_map/ppermute | solution.py:18
  90.0 1.3 %fusion.18 = bf16[256,2048]{1,0:T(8,128)(2,1)S(1)} fusion(bf16[256,1024]{1,0:T(8,128)(2,1)S(1)} %slice_dynamic-update-slice_fusion, bf16[1,1024,2048]{2,1,0:T(8,128)(2,1)S(1)} %copy-done.5), kind=kOutput, calls=%fused_computation.14 | convolution fusion | flops 1074266112 | bytes 5767168 | tf_op jit(solution)/shard_map/dot_general | solution.py:123
  92.3 2.7 %collective-permute-done.29 = bf16[64,2048]{1,0:T(8,128)(2,1)S(1)} collective-permute-done((bf16[64,2048]{1,0:T(8,128)(2,1)S(1)}, bf16[64,2048]{1,0:T(8,128)(2,1)S(1)}, u32[]{:S(2)}, u32[]{:S(2)}) %collective-permute-start.29) | collective-permute-done | bytes 262176 | tf_op jit(solution)/shard_map/ppermute | solution.py:97
  95.7 6.8 %collective-permute-done.24 = bf16[128,2048]{1,0:T(8,128)(2,1)S(1)} collective-permute-done((bf16[128,2048]{1,0:T(8,128)(2,1)S(1)}, bf16[128,2048]{1,0:T(8,128)(2,1)S(1)}, u32[]{:S(2)}, u32[]{:S(2)}) %collective-permute-start.24) | collective-permute-done | bytes 524320 | tf_op jit(solution)/shard_map/ppermute | solution.py:97
  102.4 5.8 %collective-permute-done.30 = bf16[128,2048]{1,0:T(8,128)(2,1)S(1)} collective-permute-done((bf16[128,2048]{1,0:T(8,128)(2,1)S(1)}, bf16[128,2048]{1,0:T(8,128)(2,1)S(1)}, u32[]{:S(2)}, u32[]{:S(2)}) %collective-permute-start.30) | collective-permute-done | bytes 524320 | tf_op jit(solution)/shard_map/ppermute | solution.py:97
  108.2 1.3 %fusion.27 = bf16[256,1024]{1,0:T(8,128)(2,1)S(1)} fusion(bf16[1,1024,2048]{2,1,0:T(8,128)(2,1)S(1)} %copy-done.5, bf16[128,2048]{1,0:T(8,128)(2,1)S(1)} %collective-permute-done.30, bf16[64,2048]{1,0:T(8,128)(2,1)S(1)} %collective-permute-done.29, bf16[64,2048]{1,0:T(8,128)(2,1)S(1)} %fusion.43), kind=kOutput, calls=%fused_computation.23 | convolution fusion | flops 1077149696 | bytes 5767168 | tf_op jit(solution)/shard_map/dot_general | solution.py:144
  109.7 1.5 %collective-permute-start.31 = (bf16[128,1024]{1,0:T(8,128)(2,1)S(1)}, bf16[128,1024]{1,0:T(8,128)(2,1)S(1)}, u32[]{:S(2)}, u32[]{:S(2)}) collective-permute-start(bf16[128,1024]{1,0:T(8,128)(2,1)S(1)} %broadcast_select_fusion.6), channel_id=1, source_target_pairs={{0,1},{1,0},{2,3},{3,2},{4,5},{5,4},{6,7},{7,6},{8,9},{9,8},{10,11... | collective-permute-start | bytes 786440 | tf_op jit(solution)/shard_map/ppermute | solution.py:50
  113.4 0.9 collective-permute-start.33
  114.3 0.9 collective-permute-start.34
  115.2 2.2 %collective-permute-done.28 = bf16[64,2048]{1,0:T(8,128)(2,1)S(1)} collective-permute-done((bf16[64,2048]{1,0:T(8,128)(2,1)S(1)}, bf16[64,2048]{1,0:T(8,128)(2,1)S(1)}, u32[]{:S(2)}, u32[]{:S(2)}) %collective-permute-start.28) | collective-permute-done | bytes 262176 | tf_op jit(solution)/shard_map/ppermute | solution.py:97
  117.6 0.9 collective-permute-done.32
  119.8 0.9 collective-permute-start.35
  (138 shorter events, 16.7 us)
Async XLA Ops:
  0.6 1.8 %collective-permute-start = (bf16[64,2048]{1,0:T(8,128)(2,1)}, bf16[64,2048]{1,0:T(8,128)(2,1)S(1)}, u32[]{:S(2)}, u32[]{:S(2)}) collective-permute-start(bf16[64,2048]{1,0:T(8,128)(2,1)} %bitcast.65), channel_id=1, source_target_pairs={{0,1},{1,0},{2,3},{3,2},{4,5},{5,4},{6,7},{7,6},{8,9},{9,8},{10,11... | collective-permute-start | bytes 786440 | tf_op jit(solution)/shard_map/ppermute | solution.py:50
  0.8 2.8 %collective-permute-start.1 = (bf16[2,64,2048]{2,1,0:T(8,128)(2,1)}, bf16[2,64,2048]{2,1,0:T(8,128)(2,1)S(1)}, u32[]{:S(2)}, u32[]{:S(2)}) collective-permute-start(bf16[2,64,2048]{2,1,0:T(8,128)(2,1)} %bitcast.67), channel_id=1, source_target_pairs={{0,1},{1,0},{2,3},{3,2},{4,5},{5,4},{6,7},{7,6},{8,9},{9,8},{10,11... | collective-permute-start | bytes 1572872 | tf_op jit(solution)/shard_map/ppermute | solution.py:50
  4.9 7.4 %collective-permute-start.2 = (bf16[96,1024]{1,0:T(8,128)(2,1)S(1)}, bf16[96,1024]{1,0:T(8,128)(2,1)S(1)}, u32[]{:S(2)}, u32[]{:S(2)}) collective-permute-start(bf16[96,1024]{1,0:T(8,128)(2,1)S(1)} %pad_maximum_fusion.9), channel_id=1, source_target_pairs={{0,2},{2,0},{4,6},{6,4},{1,3},{3,1},{5,7},{7,5},{8,10},{10,8},{12,... | collective-permute-start | bytes 589832 | tf_op jit(solution)/shard_map/ppermute | solution.py:45
  7.3 9.0 %collective-permute-start.3 = (bf16[96,1024]{1,0:T(8,128)(2,1)S(1)}, bf16[96,1024]{1,0:T(8,128)(2,1)S(1)}, u32[]{:S(2)}, u32[]{:S(2)}) collective-permute-start(bf16[96,1024]{1,0:T(8,128)(2,1)S(1)} %pad_maximum_fusion.10), channel_id=1, source_target_pairs={{0,4},{2,6},{4,0},{6,2},{1,5},{3,7},{5,1},{7,3},{8,12},{10,14},{12... | collective-permute-start | bytes 589832 | tf_op jit(solution)/shard_map/ppermute | solution.py:45
  8.7 8.8 %collective-permute-start.4 = (bf16[96,1024]{1,0:T(8,128)(2,1)S(1)}, bf16[96,1024]{1,0:T(8,128)(2,1)S(1)}, u32[]{:S(2)}, u32[]{:S(2)}) collective-permute-start(bf16[96,1024]{1,0:T(8,128)(2,1)S(1)} %pad_maximum_fusion.11), channel_id=1, source_target_pairs={{0,6},{2,4},{4,2},{6,0},{1,7},{3,5},{5,3},{7,1},{8,14},{10,12},{12... | collective-permute-start | bytes 589832 | tf_op jit(solution)/shard_map/ppermute | solution.py:45
  17.5 2.7 %collective-permute-start.5 = (bf16[128,1024]{1,0:T(8,128)(2,1)S(1)}, bf16[128,1024]{1,0:T(8,128)(2,1)S(1)}, u32[]{:S(2)}, u32[]{:S(2)}) collective-permute-start(bf16[128,1024]{1,0:T(8,128)(2,1)S(1)} %pad_maximum_fusion.4), channel_id=1, source_target_pairs={{0,1},{1,0},{2,3},{3,2},{4,5},{5,4},{6,7},{7,6},{8,9},{9,8},{10,11... | collective-permute-start | bytes 786440 | tf_op jit(solution)/shard_map/ppermute | solution.py:50
  24.0 8.4 %collective-permute-start.8 = (bf16[128,2048]{1,0:T(8,128)(2,1)S(1)}, bf16[128,2048]{1,0:T(8,128)(2,1)S(1)}, u32[]{:S(2)}, u32[]{:S(2)}) collective-permute-start(bf16[128,2048]{1,0:T(8,128)(2,1)S(1)} %split.469), channel_id=1, source_target_pairs={{0,2},{1,5},{2,0},{3,7},{4,6},{5,1},{6,4},{7,3},{8,10},{9,13},{10,... | collective-permute-start | bytes 1572872 | tf_op jit(solution)/shard_map/ppermute | solution.py:97
  25.5 8.0 %collective-permute-start.6 = (bf16[256,1024]{1,0:T(8,128)(2,1)S(1)}, bf16[256,1024]{1,0:T(8,128)(2,1)S(1)}, u32[]{:S(2)}, u32[]{:S(2)}) collective-permute-start(bf16[256,1024]{1,0:T(8,128)(2,1)S(1)} %constant_dynamic-update-slice_fusion), channel_id=1, source_target_pairs={{0,1},{1,0},{2,3},{3,2},{4,5},{5,4},{6,7},{7,6},{8,9},{9,8},{10,11... | collective-permute-start | bytes 1572872 | tf_op jit(solution)/shard_map/ppermute | solution.py:50
  25.8 8.0 %copy-start.5 = (bf16[1,1024,2048]{2,1,0:T(8,128)(2,1)S(1)}, bf16[1,1024,2048]{2,1,0:T(8,128)(2,1)}, u32[]{:S(2)}) copy-start(bf16[1,1024,2048]{2,1,0:T(8,128)(2,1)} %param.7) | copy-start | bytes 12582916
  32.6 5.6 %collective-permute-start.9 = (bf16[64,2048]{1,0:T(8,128)(2,1)S(1)}, bf16[64,2048]{1,0:T(8,128)(2,1)S(1)}, u32[]{:S(2)}, u32[]{:S(2)}) collective-permute-start(bf16[64,2048]{1,0:T(8,128)(2,1)S(1)} %split.816), channel_id=1, source_target_pairs={{0,4},{1,3},{2,6},{3,1},{4,0},{5,7},{6,2},{7,5},{8,12},{9,11},{10,... | collective-permute-start | bytes 786440 | tf_op jit(solution)/shard_map/ppermute | solution.py:97
  33.8 4.4 %copy-start = (bf16[1,64,2048]{2,1,0:T(8,128)(2,1)S(1)}, bf16[1,64,2048]{2,1,0:T(8,128)(2,1)}, u32[]{:S(2)}) copy-start(bf16[1,64,2048]{2,1,0:T(8,128)(2,1)} %param.11) | copy-start | bytes 786436
  33.8 4.4 %copy-start.4 = (f32[1,2048]{1,0:T(1,128)S(1)}, f32[1,2048]{1,0:T(1,128)}, u32[]{:S(2)}) copy-start(f32[1,2048]{1,0:T(1,128)} %param.8) | copy-start | bytes 24580
  35.1 16.1 %copy-start.1 = (bf16[1,64,2048]{2,1,0:T(8,128)(2,1)S(1)}, bf16[1,64,2048]{2,1,0:T(8,128)(2,1)}, u32[]{:S(2)}) copy-start(bf16[1,64,2048]{2,1,0:T(8,128)(2,1)} %param.9) | copy-start | bytes 786436
  35.2 10.3 %collective-permute-start.7 = (bf16[128,2048]{1,0:T(8,128)(2,1)S(1)}, bf16[128,2048]{1,0:T(8,128)(2,1)S(1)}, u32[]{:S(2)}, u32[]{:S(2)}) collective-permute-start(bf16[128,2048]{1,0:T(8,128)(2,1)S(1)} %split.479), channel_id=1, source_target_pairs={{0,2},{1,5},{2,0},{3,7},{4,6},{5,1},{6,4},{7,3},{8,10},{9,13},{10,... | collective-permute-start | bytes 1572872 | tf_op jit(solution)/shard_map/ppermute | solution.py:97
  38.4 8.4 %collective-permute-start.11 = (bf16[64,2048]{1,0:T(8,128)(2,1)S(1)}, bf16[64,2048]{1,0:T(8,128)(2,1)S(1)}, u32[]{:S(2)}, u32[]{:S(2)}) collective-permute-start(bf16[64,2048]{1,0:T(8,128)(2,1)S(1)} %fusion.46), channel_id=1, source_target_pairs={{0,4},{1,3},{2,6},{3,1},{4,0},{5,7},{6,2},{7,5},{8,12},{9,11},{10,... | collective-permute-start | bytes 786440 | tf_op jit(solution)/shard_map/ppermute | solution.py:97
  45.6 5.6 %collective-permute-start.10 = (bf16[64,2048]{1,0:T(8,128)(2,1)S(1)}, bf16[64,2048]{1,0:T(8,128)(2,1)S(1)}, u32[]{:S(2)}, u32[]{:S(2)}) collective-permute-start(bf16[64,2048]{1,0:T(8,128)(2,1)S(1)} %split.815), channel_id=1, source_target_pairs={{0,4},{1,3},{2,6},{3,1},{4,0},{5,7},{6,2},{7,5},{8,12},{9,11},{10,... | collective-permute-start | bytes 786440 | tf_op jit(solution)/shard_map/ppermute | solution.py:97
  46.8 10.8 %collective-permute-start.13 = (bf16[128,2048]{1,0:T(8,128)(2,1)S(1)}, bf16[128,2048]{1,0:T(8,128)(2,1)S(1)}, u32[]{:S(2)}, u32[]{:S(2)}) collective-permute-start(bf16[128,2048]{1,0:T(8,128)(2,1)S(1)} %pad_maximum_fusion), channel_id=1, source_target_pairs={{0,2},{1,5},{2,0},{3,7},{4,6},{5,1},{6,4},{7,3},{8,10},{9,13},{10,... | collective-permute-start | bytes 1572872 | tf_op jit(solution)/shard_map/ppermute | solution.py:97
  51.5 16.9 %collective-permute-start.12 = (bf16[64,2048]{1,0:T(8,128)(2,1)S(1)}, bf16[64,2048]{1,0:T(8,128)(2,1)S(1)}, u32[]{:S(2)}, u32[]{:S(2)}) collective-permute-start(bf16[64,2048]{1,0:T(8,128)(2,1)S(1)} %add_convert_fusion.3), channel_id=1, source_target_pairs={{0,8},{8,16},{16,24},{1,9},{9,17},{17,25},{2,10},{10,18},{18,26},{... | collective-permute-start | bytes 786440 | tf_op jit(solution)/shard_map/ppermute | solution.py:18
  59.1 6.4 %collective-permute-start.15 = (bf16[128,1024]{1,0:T(8,128)(2,1)S(1)}, bf16[128,1024]{1,0:T(8,128)(2,1)S(1)}, u32[]{:S(2)}, u32[]{:S(2)}) collective-permute-start(bf16[128,1024]{1,0:T(8,128)(2,1)S(1)} %broadcast_select_fusion.10), channel_id=1, source_target_pairs={{0,1},{1,0},{2,3},{3,2},{4,5},{5,4},{6,7},{7,6},{8,9},{9,8},{10,11... | collective-permute-start | bytes 786440 | tf_op jit(solution)/shard_map/ppermute | solution.py:50
  63.7 4.7 %copy-start.3 = (bf16[64,2048]{1,0:T(8,128)(2,1)S(1)}, bf16[64,2048]{1,0:T(8,128)(2,1)}, u32[]{:S(2)}) copy-start(bf16[64,2048]{1,0:T(8,128)(2,1)} %param.10) | copy-start | bytes 786436
  65.0 9.8 %collective-permute-start.26 = (bf16[128,2048]{1,0:T(8,128)(2,1)S(1)}, bf16[128,2048]{1,0:T(8,128)(2,1)S(1)}, u32[]{:S(2)}, u32[]{:S(2)}) collective-permute-start(bf16[128,2048]{1,0:T(8,128)(2,1)S(1)} %split.524), channel_id=1, source_target_pairs={{0,2},{1,5},{2,0},{3,7},{4,6},{5,1},{6,4},{7,3},{8,10},{9,13},{10,... | collective-permute-start | bytes 1572872 | tf_op jit(solution)/shard_map/ppermute | solution.py:97
  65.6 23.4 %copy-start.2 = (bf16[64,2048]{1,0:T(8,128)(2,1)S(1)}, bf16[64,2048]{1,0:T(8,128)(2,1)}, u32[]{:S(2)}) copy-start(bf16[64,2048]{1,0:T(8,128)(2,1)} %param.12) | copy-start | bytes 786436
  65.7 9.8 %collective-permute-start.16 = (bf16[32,1024]{1,0:T(8,128)(2,1)S(1)}, bf16[32,1024]{1,0:T(8,128)(2,1)S(1)}, u32[]{:S(2)}, u32[]{:S(2)}) collective-permute-start(bf16[32,1024]{1,0:T(8,128)(2,1)S(1)} %get-tuple-element.117), channel_id=1, source_target_pairs={{0,6},{2,4},{4,2},{6,0},{1,7},{3,5},{5,3},{7,1},{8,14},{10,12},{12... | collective-permute-start | bytes 196616 | tf_op jit(solution)/shard_map/ppermute | solution.py:45
  67.0 9.3 %collective-permute-start.17 = (bf16[32,1024]{1,0:T(8,128)(2,1)S(1)}, bf16[32,1024]{1,0:T(8,128)(2,1)S(1)}, u32[]{:S(2)}, u32[]{:S(2)}) collective-permute-start(bf16[32,1024]{1,0:T(8,128)(2,1)S(1)} %get-tuple-element.116), channel_id=1, source_target_pairs={{0,4},{2,6},{4,0},{6,2},{1,5},{3,7},{5,1},{7,3},{8,12},{10,14},{12... | collective-permute-start | bytes 196616 | tf_op jit(solution)/shard_map/ppermute | solution.py:45
  67.8 8.5 %collective-permute-start.18 = (bf16[32,1024]{1,0:T(8,128)(2,1)S(1)}, bf16[32,1024]{1,0:T(8,128)(2,1)S(1)}, u32[]{:S(2)}, u32[]{:S(2)}) collective-permute-start(bf16[32,1024]{1,0:T(8,128)(2,1)S(1)} %get-tuple-element.115), channel_id=1, source_target_pairs={{0,2},{2,0},{4,6},{6,4},{1,3},{3,1},{5,7},{7,5},{8,10},{10,8},{12,... | collective-permute-start | bytes 196616 | tf_op jit(solution)/shard_map/ppermute | solution.py:45
  68.5 8.8 %collective-permute-start.14 = (bf16[32,2048]{1,0:T(8,128)(2,1)S(1)}, bf16[32,2048]{1,0:T(8,128)(2,1)S(1)}, u32[]{:S(2)}, u32[]{:S(2)}) collective-permute-start(bf16[32,2048]{1,0:T(8,128)(2,1)S(1)} %broadcast_select_fusion.26), channel_id=1, source_target_pairs={{0,1},{1,0},{2,3},{3,2},{4,5},{5,4},{6,7},{7,6},{8,9},{9,8},{10,11... | collective-permute-start | bytes 393224 | tf_op jit(solution)/shard_map/ppermute | solution.py:50
  75.0 10.2 %collective-permute-start.27 = (bf16[64,2048]{1,0:T(8,128)(2,1)S(1)}, bf16[64,2048]{1,0:T(8,128)(2,1)S(1)}, u32[]{:S(2)}, u32[]{:S(2)}) collective-permute-start(bf16[64,2048]{1,0:T(8,128)(2,1)S(1)} %split.814), channel_id=1, source_target_pairs={{0,4},{1,3},{2,6},{3,1},{4,0},{5,7},{6,2},{7,5},{8,12},{9,11},{10,... | collective-permute-start | bytes 786440 | tf_op jit(solution)/shard_map/ppermute | solution.py:97
  76.3 3.7 %collective-permute-start.19 = (bf16[32,2048]{1,0:T(8,128)(2,1)S(1)}, bf16[32,2048]{1,0:T(8,128)(2,1)S(1)}, u32[]{:S(2)}, u32[]{:S(2)}) collective-permute-start(bf16[32,2048]{1,0:T(8,128)(2,1)S(1)} %broadcast_select_fusion.23), channel_id=1, source_target_pairs={{0,1},{1,0},{2,3},{3,2},{4,5},{5,4},{6,7},{7,6},{8,9},{9,8},{10,11... | collective-permute-start | bytes 393224 | tf_op jit(solution)/shard_map/ppermute | solution.py:50
  77.3 5.4 %collective-permute-start.22 = (bf16[32,1024]{1,0:T(8,128)(2,1)S(1)}, bf16[32,1024]{1,0:T(8,128)(2,1)S(1)}, u32[]{:S(2)}, u32[]{:S(2)}) collective-permute-start(bf16[32,1024]{1,0:T(8,128)(2,1)S(1)} %get-tuple-element.111), channel_id=1, source_target_pairs={{0,6},{2,4},{4,2},{6,0},{1,7},{3,5},{5,3},{7,1},{8,14},{10,12},{12... | collective-permute-start | bytes 196616 | tf_op jit(solution)/shard_map/ppermute | solution.py:45
  78.4 5.6 %collective-permute-start.21 = (bf16[32,1024]{1,0:T(8,128)(2,1)S(1)}, bf16[32,1024]{1,0:T(8,128)(2,1)S(1)}, u32[]{:S(2)}, u32[]{:S(2)}) collective-permute-start(bf16[32,1024]{1,0:T(8,128)(2,1)S(1)} %get-tuple-element.114), channel_id=1, source_target_pairs={{0,4},{2,6},{4,0},{6,2},{1,5},{3,7},{5,1},{7,3},{8,12},{10,14},{12... | collective-permute-start | bytes 196616 | tf_op jit(solution)/shard_map/ppermute | solution.py:45
  79.0 3.7 %collective-permute-start.20 = (bf16[32,1024]{1,0:T(8,128)(2,1)S(1)}, bf16[32,1024]{1,0:T(8,128)(2,1)S(1)}, u32[]{:S(2)}, u32[]{:S(2)}) collective-permute-start(bf16[32,1024]{1,0:T(8,128)(2,1)S(1)} %get-tuple-element.113), channel_id=1, source_target_pairs={{0,2},{2,0},{4,6},{6,4},{1,3},{3,1},{5,7},{7,5},{8,10},{10,8},{12,... | collective-permute-start | bytes 196616 | tf_op jit(solution)/shard_map/ppermute | solution.py:45
  80.2 8.8 %collective-permute-start.25 = (bf16[64,2048]{1,0:T(8,128)(2,1)S(1)}, bf16[64,2048]{1,0:T(8,128)(2,1)S(1)}, u32[]{:S(2)}, u32[]{:S(2)}) collective-permute-start(bf16[64,2048]{1,0:T(8,128)(2,1)S(1)} %fusion.47), channel_id=1, source_target_pairs={{8,0},{16,8},{24,16},{9,1},{17,9},{25,17},{10,2},{18,10},{26,18},{... | collective-permute-start | bytes 786440 | tf_op jit(solution)/shard_map/ppermute | solution.py:18
  83.9 5.9 %collective-permute-start.23 = (bf16[128,1024]{1,0:T(8,128)(2,1)S(1)}, bf16[128,1024]{1,0:T(8,128)(2,1)S(1)}, u32[]{:S(2)}, u32[]{:S(2)}) collective-permute-start(bf16[128,1024]{1,0:T(8,128)(2,1)S(1)} %constant_dynamic-update-slice_fusion.4), channel_id=1, source_target_pairs={{0,1},{1,0},{2,3},{3,2},{4,5},{5,4},{6,7},{7,6},{8,9},{9,8},{10,11... | collective-permute-start | bytes 786440 | tf_op jit(solution)/shard_map/ppermute | solution.py:50
  89.3 5.6 %collective-permute-start.29 = (bf16[64,2048]{1,0:T(8,128)(2,1)S(1)}, bf16[64,2048]{1,0:T(8,128)(2,1)S(1)}, u32[]{:S(2)}, u32[]{:S(2)}) collective-permute-start(bf16[64,2048]{1,0:T(8,128)(2,1)S(1)} %fusion.43), channel_id=1, source_target_pairs={{0,4},{1,3},{2,6},{3,1},{4,0},{5,7},{6,2},{7,5},{8,12},{9,11},{10,... | collective-permute-start | bytes 786440 | tf_op jit(solution)/shard_map/ppermute | solution.py:97
  91.4 11.1 %collective-permute-start.24 = (bf16[128,2048]{1,0:T(8,128)(2,1)S(1)}, bf16[128,2048]{1,0:T(8,128)(2,1)S(1)}, u32[]{:S(2)}, u32[]{:S(2)}) collective-permute-start(bf16[128,2048]{1,0:T(8,128)(2,1)S(1)} %split.514), channel_id=1, source_target_pairs={{0,2},{1,5},{2,0},{3,7},{4,6},{5,1},{6,4},{7,3},{8,10},{9,13},{10,... | collective-permute-start | bytes 1572872 | tf_op jit(solution)/shard_map/ppermute | solution.py:97
  95.0 13.2 %collective-permute-start.30 = (bf16[128,2048]{1,0:T(8,128)(2,1)S(1)}, bf16[128,2048]{1,0:T(8,128)(2,1)S(1)}, u32[]{:S(2)}, u32[]{:S(2)}) collective-permute-start(bf16[128,2048]{1,0:T(8,128)(2,1)S(1)} %pad_maximum_fusion.1), channel_id=1, source_target_pairs={{0,2},{1,5},{2,0},{3,7},{4,6},{5,1},{6,4},{7,3},{8,10},{9,13},{10,... | collective-permute-start | bytes 1572872 | tf_op jit(solution)/shard_map/ppermute | solution.py:97
  109.7 2.7 %collective-permute-start.31 = (bf16[128,1024]{1,0:T(8,128)(2,1)S(1)}, bf16[128,1024]{1,0:T(8,128)(2,1)S(1)}, u32[]{:S(2)}, u32[]{:S(2)}) collective-permute-start(bf16[128,1024]{1,0:T(8,128)(2,1)S(1)} %broadcast_select_fusion.6), channel_id=1, source_target_pairs={{0,1},{1,0},{2,3},{3,2},{4,5},{5,4},{6,7},{7,6},{8,9},{9,8},{10,11... | collective-permute-start | bytes 786440 | tf_op jit(solution)/shard_map/ppermute | solution.py:50
  111.3 6.1 %collective-permute-start.28 = (bf16[64,2048]{1,0:T(8,128)(2,1)S(1)}, bf16[64,2048]{1,0:T(8,128)(2,1)S(1)}, u32[]{:S(2)}, u32[]{:S(2)}) collective-permute-start(bf16[64,2048]{1,0:T(8,128)(2,1)S(1)} %split.813), channel_id=1, source_target_pairs={{0,4},{1,3},{2,6},{3,1},{4,0},{5,7},{6,2},{7,5},{8,12},{9,11},{10,... | collective-permute-start | bytes 786440 | tf_op jit(solution)/shard_map/ppermute | solution.py:97
  112.5 6.0 %collective-permute-start.32 = (bf16[32,1024]{1,0:T(8,128)(2,1)S(1)}, bf16[32,1024]{1,0:T(8,128)(2,1)S(1)}, u32[]{:S(2)}, u32[]{:S(2)}) collective-permute-start(bf16[32,1024]{1,0:T(8,128)(2,1)S(1)} %get-tuple-element.102), channel_id=1, source_target_pairs={{0,6},{2,4},{4,2},{6,0},{1,7},{3,5},{5,3},{7,1},{8,14},{10,12},{12... | collective-permute-start | bytes 196616 | tf_op jit(solution)/shard_map/ppermute | solution.py:45
  113.4 5.6 %collective-permute-start.33 = (bf16[32,1024]{1,0:T(8,128)(2,1)S(1)}, bf16[32,1024]{1,0:T(8,128)(2,1)S(1)}, u32[]{:S(2)}, u32[]{:S(2)}) collective-permute-start(bf16[32,1024]{1,0:T(8,128)(2,1)S(1)} %get-tuple-element.101), channel_id=1, source_target_pairs={{0,4},{2,6},{4,0},{6,2},{1,5},{3,7},{5,1},{7,3},{8,12},{10,14},{12... | collective-permute-start | bytes 196616 | tf_op jit(solution)/shard_map/ppermute | solution.py:45
  114.3 5.5 %collective-permute-start.34 = (bf16[32,1024]{1,0:T(8,128)(2,1)S(1)}, bf16[32,1024]{1,0:T(8,128)(2,1)S(1)}, u32[]{:S(2)}, u32[]{:S(2)}) collective-permute-start(bf16[32,1024]{1,0:T(8,128)(2,1)S(1)} %get-tuple-element.100), channel_id=1, source_target_pairs={{0,2},{2,0},{4,6},{6,4},{1,3},{3,1},{5,7},{7,5},{8,10},{10,8},{12,... | collective-permute-start | bytes 196616 | tf_op jit(solution)/shard_map/ppermute | solution.py:45
  119.8 1.9 %collective-permute-start.35 = (bf16[32,2048]{1,0:T(8,128)(2,1)S(1)}, bf16[32,2048]{1,0:T(8,128)(2,1)S(1)}, u32[]{:S(2)}, u32[]{:S(2)}) collective-permute-start(bf16[32,2048]{1,0:T(8,128)(2,1)S(1)} %broadcast_select_fusion.19), channel_id=1, source_target_pairs={{0,1},{1,0},{2,3},{3,2},{4,5},{5,4},{6,7},{7,6},{8,9},{9,8},{10,11... | collective-permute-start | bytes 393224 | tf_op jit(solution)/shard_map/ppermute | solution.py:50

commit v3 on v2

v3 whole, which is shorter than its diff:
```python
import jax
import jax.numpy as jnp
from jax import lax
from jax.sharding import PartitionSpec as P

F32 = jnp.float32
BF16 = jnp.bfloat16


def silu_slope(values):
    sigma = jax.nn.sigmoid(values)
    return sigma * (1.0 + values * (1.0 - sigma))


def passed_along(value, steps):
    count = lax.axis_size("segment")
    first, last = (max(0, -steps), min(count, count - steps))
    return lax.ppermute(value, "segment", [(source, source + steps) for source in range(first, last)])


def after(value, other):
    return value if other is None else lax.optimization_barrier((value, other))[0]


def bits_of(count):
    return count.bit_length() - 1


def xor_order(blocks, index):
    for bit in range(bits_of(len(blocks))):
        flip = 1 << bit
        is_set = (index & flip) != 0
        blocks = [
            jnp.where(is_set, blocks[k ^ flip], blocks[k]) for k in range(len(blocks))
        ]
    return blocks


def cut(value, count, axis=0):
    return jnp.split(value, count, axis=axis)


def row_swap(value, flip):
    count = lax.axis_size("row")
    return lax.ppermute(value, "row", [(source, source ^ flip) for source in range(count)])


def col_swap(value, flip):
    count = lax.axis_size("col")
    return lax.ppermute(value, "col", [(source, source ^ flip) for source in range(count)])


class Plane:
    def __init__(self, weight):
        self.weight = weight
        self.rows, self.cols = lax.axis_size("row"), lax.axis_size("col")
        self.row, self.col = lax.axis_index("row"), lax.axis_index("col")
        self.steps = bits_of(self.rows)
        self.per_col = self.rows // self.cols

    def flips(self, col):
        return [1 << ((col + step) % self.steps) for step in range(self.steps)]

    def places(self, col):
        flips = self.flips(col)
        return [
            sum(flip for at, flip in enumerate(flips) if place >> (self.steps - 1 - at) & 1)
            for place in range(self.rows)
        ]

    def by_place(self, blocks):
        orders = [[blocks[k] for k in self.places(col)] for col in range(max(self.steps, 1))]
        return self.choose(orders)

    def by_k(self, blocks):
        orders = []
        for col in range(max(self.steps, 1)):
            places = self.places(col)
            orders.append([blocks[places.index(k)] for k in range(self.rows)])
        return self.choose(orders)

    def choose(self, orders):
        chosen = orders[0]
        for at in range(1, len(orders)):
            picked = self.col % len(orders) == at
            chosen = [
                old if old is new else jnp.where(picked, new, old)
                for old, new in zip(chosen, orders[at])
            ]
        return chosen

    def step_swap(self, value, step):
        pairs = []
        for row in range(self.rows):
            for col in range(self.cols):
                other = row ^ self.flips(col)[step]
                pairs.append((row * self.cols + col, other * self.cols + col))
        return lax.ppermute(value, ("row", "col"), pairs)

    def home_of(self, row):
        return row // self.per_col

    def across(self, value, shift, onward=0):
        pairs = []
        for row in range(self.rows):
            home = self.home_of(row)
            for j in range(self.cols):
                other = row ^ (j * self.per_col + shift)
                pairs.append((row * self.cols + (home ^ j), other * self.cols + home))
        if not onward:
            return lax.ppermute(value, ("row", "col"), pairs)
        sections, size = lax.axis_size("segment"), self.rows * self.cols
        pairs = [
            (at * size + source, (at + onward) * size + target)
            for at in range(sections)
            if 0 <= at + onward < sections
            for source, target in pairs
        ]
        return lax.ppermute(value, ("segment", "row", "col"), pairs)

    def spread(self, block):
        pieces = xor_order(cut(block, self.per_col, axis=1), self.row % self.per_col)
        return [self.across(piece, shift) for shift, piece in enumerate(pieces)]

    def joined(self, arrived):
        half = jnp.concatenate(arrived, axis=0)
        halves = [half] + [col_swap(half, flip) for flip in range(1, self.cols)]
        halves = xor_order(halves, self.col ^ self.home_of(self.row))
        return [block for half in halves for block in cut(half, self.per_col)]

    def product(self, blocks):
        full = jnp.concatenate(self.by_place(blocks), axis=0)
        return jnp.dot(full, self.weight, preferred_element_type=F32).astype(BF16)

    def halved(self, total, step, wait=None):
        if step >= self.steps:
            return total, None
        ours, away = cut(total, 2)
        message = lax.optimization_barrier(away.astype(BF16))
        arrived = after(self.step_swap(message, step), wait)
        return ours.astype(F32) + arrived.astype(F32), message

    def doubled(self, block, step, wait=None):
        if step >= self.steps:
            return block, None
        block = lax.optimization_barrier(block)
        arrived = after(self.step_swap(block, step), wait)
        return jnp.concatenate([block, arrived], axis=0), block

    def transposed(self, scaled):
        return lax.dot_general(
            scaled, self.weight, (((1,), (1,)), ((), ())), preferred_element_type=F32
        ).astype(BF16)

    def shares(self, partial):
        ordered = jnp.concatenate(self.by_k(cut(partial, self.rows)), axis=0)
        shares = xor_order(cut(ordered, self.cols), self.col ^ self.home_of(self.row))
        return lax.optimization_barrier(shares)

    def shared(self, shares, wait=None):
        total = shares[0].astype(F32)
        for flip in range(1, self.cols):
            total = total + after(col_swap(shares[flip], flip), wait).astype(F32)
        return lax.optimization_barrier(total.astype(BF16))

    def delivered(self, total, onward=0):
        pieces = cut(total, self.per_col)
        arrived = [self.across(piece, at, onward) for at, piece in enumerate(pieces)]
        return jnp.concatenate(xor_order(arrived, self.row % self.per_col), axis=1)


def shards(weights, layer_gains, incoming, fresh_batch, returning, fresh_cotangent, stashed_inputs):
    segment_index = lax.axis_index("segment")
    segment_count = lax.axis_size("segment")
    plane = Plane(weights[0])
    layer_gain = layer_gains[0][None, :]

    def advance(own_block, pre_act):
        return (own_block.astype(F32) + layer_gain * jax.nn.silu(pre_act)).astype(BF16)

    def scale(upstream, pre_act):
        return (upstream.astype(F32) * layer_gain * silu_slope(pre_act)).astype(BF16)

    def retreat(upstream, back_term):
        return (upstream.astype(F32) + back_term.astype(F32)).astype(BF16)

    tokens, steps = incoming.shape[1], plane.steps
    spread = plane.spread(jnp.concatenate([stashed_inputs[0, 0], incoming[0], stashed_inputs[0, 1]]))
    first_stored = plane.joined([block[:tokens] for block in spread])
    rest = plane.joined([block[tokens:] for block in spread])
    entered = [block[:tokens] for block in rest]
    second_stored = [block[tokens:] for block in rest]
    returning_ahead = passed_along(returning[0], -1)

    first_back = after(plane.product(first_stored), rest[0])
    first_pre = plane.product([after(block, first_back) for block in entered])
    first_back, _ = plane.halved(first_back, 0, first_pre)
    first_back = lax.optimization_barrier(first_back)
    first_pre, _ = plane.halved(first_pre, 0, first_back)
    for step in range(1, steps):
        first_back, _ = plane.halved(first_back, step, first_pre)
    scaled_first = lax.optimization_barrier(scale(returning[0], first_back))
    for step in range(1, steps):
        first_pre, _ = plane.halved(first_pre, step, scaled_first)
    first_out = lax.optimization_barrier(advance(incoming[0], first_pre))
    arrived = passed_along(first_out, 1)

    second_back = plane.product([after(block, first_out) for block in second_stored])
    gathered = scaled_first
    for step in reversed(range(1, steps)):
        gathered, _ = plane.doubled(gathered, step, first_out)
    gathered, _ = plane.doubled(gathered, 0, second_back)
    partial = plane.transposed(gathered)
    feed_block = jnp.where(segment_index == 0, fresh_batch, after(arrived, partial))
    shares = plane.shares(after(partial, feed_block))
    second_back, _ = plane.halved(second_back, 0, shares[-1])
    total = plane.shared(shares)
    feed_spread = plane.spread(after(feed_block, total))
    for step in range(1, steps):
        second_back, _ = plane.halved(second_back, step, total)
    arrived_grad = retreat(after(returning_ahead, total), plane.delivered(total, -1))
    grad_first = retreat(returning[0], plane.delivered(total))

    upstream = jnp.where(segment_index == segment_count - 1, fresh_cotangent, arrived_grad)
    scaled_second = lax.optimization_barrier(scale(upstream, second_back))
    second_pre = plane.product(plane.joined([after(block, scaled_second) for block in feed_spread]))
    gathered = scaled_second
    for step in reversed(range(1, steps)):
        gathered, _ = plane.doubled(gathered, step, second_pre)
    gathered = lax.optimization_barrier(gathered)
    second_pre, _ = plane.halved(second_pre, 0, gathered)
    gathered, _ = plane.doubled(gathered, 0, second_pre)
    shares = plane.shares(plane.transposed(gathered))
    grad_first = after(grad_first, shares[-1])
    total = plane.shared(shares)
    for step in range(1, steps):
        second_pre, _ = plane.halved(second_pre, step, total)
    second_out = advance(feed_block, second_pre)
    grad_second = retreat(upstream, plane.delivered(total))
    layer_outputs = jnp.stack([first_out, second_out], axis=0)[None]
    input_grads = jnp.stack([grad_first, grad_second], axis=0)[None]
    return (layer_outputs, input_grads)


def solution(mesh):
    in_specs = (
        P("segment", "row", "col"),
        P("segment", "col"),
        P("segment", "row", "col"),
        P("row", "col"),
        P("segment", "row", "col"),
        P("row", "col"),
        P("segment", None, "row", "col"),
    )
    out_specs = (P("segment", None, "row", "col"), P("segment", None, "row", "col"))
    return jax.shard_map(shards, mesh=mesh, in_specs=in_specs, out_specs=out_specs, check_vma=False)
```

time: 123 us -> 112 us (0.911)
  waiting for transfers between devices: 64.7 us -> 48.5 us
  starting transfers between devices: 38.9 us -> 42.4 us
  local copies, waits for them, and re-layouts: 0.7 us -> 3.57 us
  matrix products: 9.88 us -> 7.62 us
  other arithmetic: 7.18 us -> 8.57 us
    ppermute x12, waiting for transfers between devices: 43.7 us -> 25.2 us  [step_swap(): return lax.ppermute(value, ('row', 'col'), pairs)]
    ppermute x12 -> x10, starting transfers between devices: 11.9 us -> 24.8 us  [the longest x8 22.3 us: across(): return lax.ppermute(value, ('row', 'col'), pairs)]
    ppermute x10 -> x5, starting transfers between devices: 13 us -> 4.47 us  [col_swap(): lax.ppermute(value, 'col', [(source, source ^ flip) for source in range(c...]
    ppermute x12 -> x10, waiting for transfers between devices: 13.8 us -> 20.5 us  [the longest x8 20.5 us: across(): return lax.ppermute(value, ('row', 'col'), pairs)]
    ppermute x2, waiting for transfers between devices: 3.82 us -> 0.01 us  [passed_along(): lax.ppermute(value, 'segment', [(source, source + steps) for source in ra...]
    select_n x21 -> x10, other arithmetic: 3.07 us -> 0.76 us  [xor_order(): jnp.where(is_set, blocks[k ^ flip], blocks[k])]
    dot_general x4, matrix products: 7.32 us -> 5.06 us  [product(): return jnp.dot(full, self.weight, preferred_element_type=F32).astype(BF16)]
    add x4, other arithmetic: 0.5 us -> 2.58 us  [halved(): return (ours.astype(F32) + arrived.astype(F32), message)]
  transfers between devices with their start and end apart: 36 -> 29, of which waited for: 25 -> 17; matrix products, arithmetic and copies ran while one was open for 8% -> 13% of each run, Pallas kernels for 0% -> 0%
where the time goes in v3:
time: 112 us
  waiting for transfers between devices  48.5 us (43%)
  starting transfers between devices  42.4 us (38%)
  other arithmetic  8.57 us (8%)
  matrix products  7.62 us (7%)
  local copies, waits for them, and re-layouts  3.57 us (3%)
  between operations  1.31 us (1%)
    ppermute x12, waiting for transfers between devices, step_swap(): return lax.ppermute(value, ('row', 'col'), pairs)  25.2 us
    ppermute x8, starting transfers between devices, across(): return lax.ppermute(value, ('row', 'col'), pairs)  22.3 us
    ppermute x8, waiting for transfers between devices, across(): return lax.ppermute(value, ('row', 'col'), pairs)  20.5 us
    ppermute x12, starting transfers between devices, step_swap(): return lax.ppermute(value, ('row', 'col'), pairs)  8.62 us
    dot_general x4, matrix products, product(): return jnp.dot(full, self.weight, preferred_element_type=F32).astype(BF16)  5.06 us
    ppermute x2, starting transfers between devices, passed_along(): lax.ppermute(value, 'segment', [(source, source + steps) for source in ra...  4.5 us
    ppermute x5, starting transfers between devices, col_swap(): lax.ppermute(value, 'col', [(source, source ^ flip) for source in range(c...  4.47 us
    ppermute x5, waiting for transfers between devices, col_swap(): lax.ppermute(value, 'col', [(source, source ^ flip) for source in range(c...  2.81 us
  transfers between devices with their start and end apart: 29, of which 17 were waited for; matrix products, arithmetic and copies ran while one was open for 13% of the time, Pallas kernels for 0%

profile of v3, /device:TPU:1, one launch (start us, length us, event | category | flops | bytes accessed | tf_op | source)
XLA Modules:
  0.0 111.9 jit_solution(8620338639506316161)
XLA Ops:
  0.6 1.1 slice_bitcast_fusion.1
  1.7 1.0 pad_maximum_fusion
  2.8 4.5 %collective-permute-start = (bf16[192,1024]{1,0:T(8,128)(2,1)S(1)}, bf16[192,1024]{1,0:T(8,128)(2,1)S(1)}, u32[]{:S(2)}, u32[]{:S(2)}) collective-permute-start(bf16[192,1024]{1,0:T(8,128)(2,1)S(1)} %get-tuple-element.68), channel_id=1, source_target_pairs={{0,0},{1,4},{2,2},{3,6},{5,5},{4,1},{7,7},{6,3},{8,8},{9,12},{10,1... | collective-permute-start | bytes 1179656 | tf_op jit(solution)/shard_map/ppermute | solution.py:111
  7.3 1.0 collective-permute-start.1
  8.3 8.7 %collective-permute-done = bf16[192,1024]{1,0:T(8,128)(2,1)S(1)} collective-permute-done((bf16[192,1024]{1,0:T(8,128)(2,1)S(1)}, bf16[192,1024]{1,0:T(8,128)(2,1)S(1)}, u32[]{:S(2)}, u32[]{:S(2)}) %collective-permute-start) | collective-permute-done | bytes 393248 | tf_op jit(solution)/shard_map/ppermute | solution.py:111
  17.8 0.9 collective-permute-done.3
  19.4 1.3 %fusion.12 = bf16[256,2048]{1,0:T(8,128)(2,1)S(1)} fusion(bf16[1,1024,2048]{2,1,0:T(8,128)(2,1)S(1)} %copy-done.6, bf16[64,1024]{1,0:T(8,128)(2,1)S(1)} %get-tuple-element.119, bf16[64,1024]{1,0:T(8,128)(2,1)S(1)} %get-tuple-element.95, bf16[64,1024]{1,0:T(8,128)(2,1)S(1)} %get-tuple-element.94, bf16[64,1024]{1,0:T(8,128)(2,1)S(1)} %get-tuple-element.118), kind=kOutput, calls=%fused_computation.12 | convolution fusion | flops 1076363264 | bytes 5767168 | tf_op jit(solution)/shard_map/dot_general | solution.py:133
  20.7 1.9 %collective-permute-start.5 = (bf16[128,2048]{1,0:T(8,128)(2,1)S(1)}, bf16[128,2048]{1,0:T(8,128)(2,1)}, u32[]{:S(2)}, u32[]{:S(2)}) collective-permute-start(bf16[128,2048]{1,0:T(8,128)(2,1)S(1)} %split.183), channel_id=1, source_target_pairs={{0,2},{1,5},{2,0},{3,7},{4,6},{5,1},{6,4},{7,3},{8,10},{9,13},{10,... | collective-permute-start | bytes 1572872 | tf_op jit(solution)/shard_map/ppermute | solution.py:98
  22.8 0.7 fusion.80
  23.6 1.3 %fusion.15 = bf16[256,2048]{1,0:T(8,128)(2,1)S(1)} fusion(bf16[1,1024,2048]{2,1,0:T(8,128)(2,1)S(1)} %copy-done.6, bf16[64,1024]{1,0:T(8,128)(2,1)S(1)} %get-tuple-element.36, bf16[64,1024]{1,0:T(8,128)(2,1)S(1)} %get-tuple-element.117, bf16[64,1024]{1,0:T(8,128)(2,1)S(1)} %get-tuple-element.116, bf16[64,1024]{1,0:T(8,128)(2,1)S(1)} %get-tuple-element.33), kind=kOutput, calls=%fused_computation.13 | convolution fusion | flops 1076363264 | bytes 5767168 | tf_op jit(solution)/shard_map/dot_general | solution.py:133
  24.9 0.8 split.181
  25.8 1.3 %collective-permute-start.13 = (bf16[64,2048]{1,0:T(8,128)(2,1)S(1)}, bf16[64,2048]{1,0:T(8,128)(2,1)}, u32[]{:S(2)}, u32[]{:S(2)}) collective-permute-start(bf16[64,2048]{1,0:T(8,128)(2,1)S(1)} %bitcast.45), channel_id=1, source_target_pairs={{8,0},{16,8},{24,16},{9,1},{17,9},{25,17},{10,2},{18,10},{26,18},{... | collective-permute-start | bytes 786440 | tf_op jit(solution)/shard_map/ppermute | solution.py:18
  27.1 2.5 %collective-permute-done.5 = bf16[128,2048]{1,0:T(8,128)(2,1)} collective-permute-done((bf16[128,2048]{1,0:T(8,128)(2,1)S(1)}, bf16[128,2048]{1,0:T(8,128)(2,1)}, u32[]{:S(2)}, u32[]{:S(2)}) %collective-permute-start.5) | collective-permute-done | bytes 524320 | tf_op jit(solution)/shard_map/ppermute | solution.py:98
  29.5 1.2 %convert_add_fusion.3 = f32[128,2048]{1,0:T(8,128)S(1)} fusion(bf16[128,2048]{1,0:T(8,128)(2,1)} %collective-permute-done.5, bf16[256,2048]{1,0:T(8,128)(2,1)S(1)} %fusion.12), kind=kLoop, calls=%fused_computation.27 | loop fusion | flops 786432 | bytes 2097152 | tf_op jit(solution)/shard_map/add | solution.py:141
  30.8 1.3 %collective-permute-start.7 = (bf16[64,2048]{1,0:T(8,128)(2,1)S(1)}, bf16[64,2048]{1,0:T(8,128)(2,1)S(1)}, u32[]{:S(2)}, u32[]{:S(2)}) collective-permute-start(bf16[64,2048]{1,0:T(8,128)(2,1)S(1)} %split.256), channel_id=1, source_target_pairs={{0,4},{1,3},{2,6},{3,1},{4,0},{5,7},{6,2},{7,5},{8,12},{9,11},{10,... | collective-permute-start | bytes 786440 | tf_op jit(solution)/shard_map/ppermute | solution.py:98
  32.0 3.1 %collective-permute-done.4 = bf16[128,2048]{1,0:T(8,128)(2,1)} collective-permute-done((bf16[128,2048]{1,0:T(8,128)(2,1)}, bf16[128,2048]{1,0:T(8,128)(2,1)}, u32[]{:S(2)}, u32[]{:S(2)}) %collective-permute-start.4) | collective-permute-done | bytes 524320 | tf_op jit(solution)/shard_map/ppermute | solution.py:98
  35.2 1.2 %convert_add_fusion.2 = f32[128,2048]{1,0:T(8,128)S(1)} fusion(bf16[128,2048]{1,0:T(8,128)(2,1)} %collective-permute-done.4, bf16[256,2048]{1,0:T(8,128)(2,1)S(1)} %fusion.15), kind=kLoop, calls=%fused_computation.26 | loop fusion | flops 786432 | bytes 2097152 | tf_op jit(solution)/shard_map/add | solution.py:141
  36.4 1.8 %collective-permute-done.7 = bf16[64,2048]{1,0:T(8,128)(2,1)S(1)} collective-permute-done((bf16[64,2048]{1,0:T(8,128)(2,1)S(1)}, bf16[64,2048]{1,0:T(8,128)(2,1)S(1)}, u32[]{:S(2)}, u32[]{:S(2)}) %collective-permute-start.7) | collective-permute-done | bytes 262176 | tf_op jit(solution)/shard_map/ppermute | solution.py:98
  38.1 1.2 %collective-permute-start.6 = (bf16[64,2048]{1,0:T(8,128)(2,1)S(1)}, bf16[64,2048]{1,0:T(8,128)(2,1)S(1)}, u32[]{:S(2)}, u32[]{:S(2)}) collective-permute-start(bf16[64,2048]{1,0:T(8,128)(2,1)S(1)} %split.257), channel_id=1, source_target_pairs={{0,4},{1,3},{2,6},{3,1},{4,0},{5,7},{6,2},{7,5},{8,12},{9,11},{10,... | collective-permute-start | bytes 786440 | tf_op jit(solution)/shard_map/ppermute | solution.py:98
  39.9 3.7 %collective-permute-done.6 = bf16[64,2048]{1,0:T(8,128)(2,1)S(1)} collective-permute-done((bf16[64,2048]{1,0:T(8,128)(2,1)S(1)}, bf16[64,2048]{1,0:T(8,128)(2,1)S(1)}, u32[]{:S(2)}, u32[]{:S(2)}) %collective-permute-start.6) | collective-permute-done | bytes 262176 | tf_op jit(solution)/shard_map/ppermute | solution.py:98
  43.9 3.2 %collective-permute-start.8 = (bf16[64,2048]{1,0:T(8,128)(2,1)S(1)}, bf16[64,2048]{1,0:T(8,128)(2,1)S(1)}, u32[]{:S(2)}, u32[]{:S(2)}) collective-permute-start(bf16[64,2048]{1,0:T(8,128)(2,1)S(1)} %add_convert_fusion.4), channel_id=1, source_target_pairs={{0,8},{8,16},{16,24},{1,9},{9,17},{17,25},{2,10},{10,18},{18,26},{... | collective-permute-start | bytes 786440 | tf_op jit(solution)/shard_map/ppermute | solution.py:18
  47.1 1.4 %collective-permute-start.10 = (bf16[128,2048]{1,0:T(8,128)(2,1)S(1)}, bf16[128,2048]{1,0:T(8,128)(2,1)S(1)}, u32[]{:S(2)}, u32[]{:S(2)}) collective-permute-start(bf16[128,2048]{1,0:T(8,128)(2,1)S(1)} %pad_maximum_fusion.2), channel_id=1, source_target_pairs={{0,2},{1,5},{2,0},{3,7},{4,6},{5,1},{6,4},{7,3},{8,10},{9,13},{10,... | collective-permute-start | bytes 1572872 | tf_op jit(solution)/shard_map/ppermute | solution.py:98
  48.6 1.3 %fusion.18 = bf16[256,2048]{1,0:T(8,128)(2,1)S(1)} fusion(bf16[1,1024,2048]{2,1,0:T(8,128)(2,1)S(1)} %copy-done.7, bf16[64,1024]{1,0:T(8,128)(2,1)S(1)} %copy-done.5, bf16[64,1024]{1,0:T(8,128)(2,1)S(1)} %get-tuple-element.115, bf16[64,1024]{1,0:T(8,128)(2,1)S(1)} %get-tuple-element.114, bf16[64,1024]{1,0:T(8,128)(2,1)S(1)} %get-tuple-element.42), kind=kOutput, calls=%fused_computation.14 | convolution fusion | flops 1076363264 | bytes 5767168 | tf_op jit(solution)/shard_map/dot_general | solution.py:133
  50.1 5.4 %collective-permute-done.10 = bf16[128,2048]{1,0:T(8,128)(2,1)S(1)} collective-permute-done((bf16[128,2048]{1,0:T(8,128)(2,1)S(1)}, bf16[128,2048]{1,0:T(8,128)(2,1)S(1)}, u32[]{:S(2)}, u32[]{:S(2)}) %collective-permute-start.10) | collective-permute-done | bytes 524320 | tf_op jit(solution)/shard_map/ppermute | solution.py:98
  55.5 1.3 %fusion.24 = bf16[256,1024]{1,0:T(8,128)(2,1)S(1)} fusion(bf16[1,1024,2048]{2,1,0:T(8,128)(2,1)S(1)} %copy-done.7, bf16[128,2048]{1,0:T(8,128)(2,1)S(1)} %collective-permute-done.10, bf16[128,2048]{1,0:T(8,128)(2,1)S(1)} %pad_maximum_fusion.2), kind=kOutput, calls=%fused_computation.16 | convolution fusion | flops 1076101120 | bytes 5767168 | tf_op jit(solution)/shard_map/dot_general | solution.py:151
  57.1 3.3 %collective-permute-start.11 = (bf16[128,1024]{1,0:T(8,128)(2,1)S(1)}, bf16[128,1024]{1,0:T(8,128)(2,1)S(1)}, u32[]{:S(2)}, u32[]{:S(2)}) collective-permute-start(bf16[128,1024]{1,0:T(8,128)(2,1)S(1)} %get-tuple-element.50), channel_id=1, source_target_pairs={{0,1},{1,0},{2,3},{3,2},{4,5},{5,4},{6,7},{7,6},{8,9},{9,8},{10,11... | collective-permute-start | bytes 786440 | tf_op jit(solution)/shard_map/ppermute | solution.py:50
  60.4 0.7 collective-permute-done.16
  61.3 1.3 %collective-permute-start.17 = (bf16[64,2048]{1,0:T(8,128)(2,1)S(1)}, bf16[64,2048]{1,0:T(8,128)(2,1)S(1)}, u32[]{:S(2)}, u32[]{:S(2)}) collective-permute-start(bf16[64,2048]{1,0:T(8,128)(2,1)S(1)} %split.255), channel_id=1, source_target_pairs={{0,4},{1,3},{2,6},{3,1},{4,0},{5,7},{6,2},{7,5},{8,12},{9,11},{10,... | collective-permute-start | bytes 786440 | tf_op jit(solution)/shard_map/ppermute | solution.py:98
  62.7 1.3 %collective-permute-start.14 = (bf16[64,1024]{1,0:T(8,128)(2,1)S(1)}, bf16[64,1024]{1,0:T(8,128)(2,1)S(1)}, u32[]{:S(2)}, u32[]{:S(2)}) collective-permute-start(bf16[64,1024]{1,0:T(8,128)(2,1)S(1)} %get-tuple-element.112), channel_id=1, source_target_pairs={{8,2},{9,6},{10,0},{11,4},{13,7},{12,3},{15,5},{14,1},{16,10},{17,... | collective-permute-start | bytes 393224 | tf_op jit(solution)/shard_map/ppermute | solution.py:119
  64.0 1.3 %collective-permute-start.15 = (bf16[64,1024]{1,0:T(8,128)(2,1)S(1)}, bf16[64,1024]{1,0:T(8,128)(2,1)S(1)}, u32[]{:S(2)}, u32[]{:S(2)}) collective-permute-start(bf16[64,1024]{1,0:T(8,128)(2,1)S(1)} %get-tuple-element.113), channel_id=1, source_target_pairs={{8,0},{9,4},{10,2},{11,6},{13,5},{12,1},{15,7},{14,3},{16,8},{17,1... | collective-permute-start | bytes 393224 | tf_op jit(solution)/shard_map/ppermute | solution.py:119
  65.3 1.3 %collective-permute-done.17 = bf16[64,2048]{1,0:T(8,128)(2,1)S(1)} collective-permute-done((bf16[64,2048]{1,0:T(8,128)(2,1)S(1)}, bf16[64,2048]{1,0:T(8,128)(2,1)S(1)}, u32[]{:S(2)}, u32[]{:S(2)}) %collective-permute-start.17) | collective-permute-done | bytes 262176 | tf_op jit(solution)/shard_map/ppermute | solution.py:98
  66.6 6.6 %collective-permute-start.18 = (bf16[64,1024]{1,0:T(8,128)(2,1)S(1)}, bf16[64,1024]{1,0:T(8,128)(2,1)S(1)}, u32[]{:S(2)}, u32[]{:S(2)}) collective-permute-start(bf16[64,1024]{1,0:T(8,128)(2,1)S(1)} %get-tuple-element.108), channel_id=1, source_target_pairs={{0,2},{1,6},{2,0},{3,4},{5,7},{4,3},{7,5},{6,1},{8,10},{9,14},{10,... | collective-permute-start | bytes 393224 | tf_op jit(solution)/shard_map/ppermute | solution.py:111
  73.3 1.9 %collective-permute-start.12 = (bf16[64,1024]{1,0:T(8,128)(2,1)S(1)}, bf16[64,1024]{1,0:T(8,128)(2,1)S(1)}, u32[]{:S(2)}, u32[]{:S(2)}) collective-permute-start(bf16[64,1024]{1,0:T(8,128)(2,1)S(1)} %get-tuple-element.109), channel_id=1, source_target_pairs={{0,0},{1,4},{2,2},{3,6},{5,5},{4,1},{7,7},{6,3},{8,8},{9,12},{10,1... | collective-permute-start | bytes 393224 | tf_op jit(solution)/shard_map/ppermute | solution.py:111
  75.2 1.3 %fusion.40 = (bf16[64,2048]{1,0:T(8,128)(2,1)S(1)}, bf16[64,2048]{1,0:T(8,128)(2,1)S(1)}) fusion(f32[128,2048]{1,0:T(8,128)S(1)} %convert_add_fusion.1, bf16[64,2048]{1,0:T(8,128)(2,1)S(1)} %collective-permute-done.17, f32[2048]{0:T(1024)S(1)} %bitcast.51, bf16[64,2048]{1,0:T(8,128)(2,1)S(1)} %copy-done.2, bf16[64,1024]{1,0:T(8,128)(2,1)S(1)} %get-tuple-element.111, ...), kind=kLoop, calls=%fused_computation.37 | loop fusion | flops 2752512 | bytes 2105345 | tf_op jit(solution)/shard_map/convert_element_type | solution.py:182
  76.5 3.0 %collective-permute-done.12 = bf16[64,1024]{1,0:T(8,128)(2,1)S(1)} collective-permute-done((bf16[64,1024]{1,0:T(8,128)(2,1)S(1)}, bf16[64,1024]{1,0:T(8,128)(2,1)S(1)}, u32[]{:S(2)}, u32[]{:S(2)}) %collective-permute-start.12) | collective-permute-done | bytes 131104 | tf_op jit(solution)/shard_map/ppermute | solution.py:111
  80.0 1.2 %collective-permute-done.19 = bf16[128,1024]{1,0:T(8,128)(2,1)S(1)} collective-permute-done((bf16[128,1024]{1,0:T(8,128)(2,1)S(1)}, bf16[128,1024]{1,0:T(8,128)(2,1)S(1)}, u32[]{:S(2)}, u32[]{:S(2)}) %collective-permute-start.19) | collective-permute-done | bytes 262176 | tf_op jit(solution)/shard_map/ppermute | solution.py:50
  81.3 1.3 %fusion.21 = bf16[256,2048]{1,0:T(8,128)(2,1)S(1)} fusion(bf16[1,1024,2048]{2,1,0:T(8,128)(2,1)S(1)} %copy-done.7, bf16[64,1024]{1,0:T(8,128)(2,1)S(1)} %get-tuple-element.107, bf16[64,1024]{1,0:T(8,128)(2,1)S(1)} %get-tuple-element.77, bf16[64,1024]{1,0:T(8,128)(2,1)S(1)} %get-tuple-element.76, bf16[64,1024]{1,0:T(8,128)(2,1)S(1)} %get-tuple-element.106), kind=kOutput, calls=%fused_computation.15 | convolution fusion | flops 1076363264 | bytes 5767168 | tf_op jit(solution)/shard_map/dot_general | solution.py:133
  82.9 1.8 %collective-permute-start.25 = (bf16[64,1024]{1,0:T(8,128)(2,1)S(1)}, bf16[64,1024]{1,0:T(8,128)(2,1)S(1)}, u32[]{:S(2)}, u32[]{:S(2)}) collective-permute-start(bf16[64,1024]{1,0:T(8,128)(2,1)S(1)} %get-tuple-element.112), channel_id=1, source_target_pairs={{0,2},{1,6},{2,0},{3,4},{5,7},{4,3},{7,5},{6,1},{8,10},{9,14},{10,... | collective-permute-start | bytes 393224 | tf_op jit(solution)/shard_map/ppermute | solution.py:111
  84.7 2.5 %collective-permute-start.26 = (bf16[64,1024]{1,0:T(8,128)(2,1)S(1)}, bf16[64,1024]{1,0:T(8,128)(2,1)S(1)}, u32[]{:S(2)}, u32[]{:S(2)}) collective-permute-start(bf16[64,1024]{1,0:T(8,128)(2,1)S(1)} %get-tuple-element.113), channel_id=1, source_target_pairs={{0,0},{1,4},{2,2},{3,6},{5,5},{4,1},{7,7},{6,3},{8,8},{9,12},{10,1... | collective-permute-start | bytes 393224 | tf_op jit(solution)/shard_map/ppermute | solution.py:111
  87.3 7.1 %collective-permute-done.25 = bf16[64,1024]{1,0:T(8,128)(2,1)S(1)} collective-permute-done((bf16[64,1024]{1,0:T(8,128)(2,1)S(1)}, bf16[64,1024]{1,0:T(8,128)(2,1)S(1)}, u32[]{:S(2)}, u32[]{:S(2)}) %collective-permute-start.25) | collective-permute-done | bytes 131104 | tf_op jit(solution)/shard_map/ppermute | solution.py:111
  94.7 5.3 %collective-permute-done.23 = bf16[128,2048]{1,0:T(8,128)(2,1)S(1)} collective-permute-done((bf16[128,2048]{1,0:T(8,128)(2,1)S(1)}, bf16[128,2048]{1,0:T(8,128)(2,1)S(1)}, u32[]{:S(2)}, u32[]{:S(2)}) %collective-permute-start.23) | collective-permute-done | bytes 524320 | tf_op jit(solution)/shard_map/ppermute | solution.py:98
  100.0 1.3 %fusion.27 = bf16[256,1024]{1,0:T(8,128)(2,1)S(1)} fusion(bf16[1,1024,2048]{2,1,0:T(8,128)(2,1)S(1)} %copy-done.7, bf16[128,2048]{1,0:T(8,128)(2,1)S(1)} %collective-permute-done.23, bf16[128,2048]{1,0:T(8,128)(2,1)S(1)} %pad_maximum_fusion.3), kind=kOutput, calls=%fused_computation.17 | convolution fusion | flops 1076101120 | bytes 5767168 | tf_op jit(solution)/shard_map/dot_general | solution.py:151
  103.1 1.2 %collective-permute-start.27 = (bf16[64,1024]{1,0:T(8,128)(2,1)S(1)}, bf16[64,1024]{1,0:T(8,128)(2,1)S(1)}, u32[]{:S(2)}, u32[]{:S(2)}) collective-permute-start(bf16[64,1024]{1,0:T(8,128)(2,1)S(1)} %get-tuple-element.104), channel_id=1, source_target_pairs={{0,2},{1,6},{2,0},{3,4},{5,7},{4,3},{7,5},{6,1},{8,10},{9,14},{10,... | collective-permute-start | bytes 393224 | tf_op jit(solution)/shard_map/ppermute | solution.py:111
  104.4 2.7 %collective-permute-start.28 = (bf16[64,1024]{1,0:T(8,128)(2,1)S(1)}, bf16[64,1024]{1,0:T(8,128)(2,1)S(1)}, u32[]{:S(2)}, u32[]{:S(2)}) collective-permute-start(bf16[64,1024]{1,0:T(8,128)(2,1)S(1)} %get-tuple-element.105), channel_id=1, source_target_pairs={{0,0},{1,4},{2,2},{3,6},{5,5},{4,1},{7,7},{6,3},{8,8},{9,12},{10,1... | collective-permute-start | bytes 393224 | tf_op jit(solution)/shard_map/ppermute | solution.py:111
  107.1 1.3 %collective-permute-done.22 = bf16[64,2048]{1,0:T(8,128)(2,1)S(1)} collective-permute-done((bf16[64,2048]{1,0:T(8,128)(2,1)S(1)}, bf16[64,2048]{1,0:T(8,128)(2,1)S(1)}, u32[]{:S(2)}, u32[]{:S(2)}) %collective-permute-start.22) | collective-permute-done | bytes 262176 | tf_op jit(solution)/shard_map/ppermute | solution.py:98
  108.5 0.8 maximum_bitcast_fusion
  110.0 1.0 collective-permute-done.28
  111.1 0.8 maximum_bitcast_fusion.1
  (86 shorter events, 7.3 us)
Async XLA Ops:
  2.8 14.2 %collective-permute-start = (bf16[192,1024]{1,0:T(8,128)(2,1)S(1)}, bf16[192,1024]{1,0:T(8,128)(2,1)S(1)}, u32[]{:S(2)}, u32[]{:S(2)}) collective-permute-start(bf16[192,1024]{1,0:T(8,128)(2,1)S(1)} %get-tuple-element.68), channel_id=1, source_target_pairs={{0,0},{1,4},{2,2},{3,6},{5,5},{4,1},{7,7},{6,3},{8,8},{9,12},{10,1... | collective-permute-start | bytes 1179656 | tf_op jit(solution)/shard_map/ppermute | solution.py:111
  7.3 9.7 %collective-permute-start.1 = (bf16[192,1024]{1,0:T(8,128)(2,1)S(1)}, bf16[192,1024]{1,0:T(8,128)(2,1)S(1)}, u32[]{:S(2)}, u32[]{:S(2)}) collective-permute-start(bf16[192,1024]{1,0:T(8,128)(2,1)S(1)} %get-tuple-element.69), channel_id=1, source_target_pairs={{0,2},{1,6},{2,0},{3,4},{5,7},{4,3},{7,5},{6,1},{8,10},{9,14},{10,... | collective-permute-start | bytes 1179656 | tf_op jit(solution)/shard_map/ppermute | solution.py:111
  17.1 1.6 %collective-permute-start.3 = (bf16[128,1024]{1,0:T(8,128)(2,1)S(1)}, bf16[128,1024]{1,0:T(8,128)(2,1)S(1)}, u32[]{:S(2)}, u32[]{:S(2)}) collective-permute-start(bf16[128,1024]{1,0:T(8,128)(2,1)S(1)} %pad_maximum_fusion.4), channel_id=1, source_target_pairs={{0,1},{1,0},{2,3},{3,2},{4,5},{5,4},{6,7},{7,6},{8,9},{9,8},{10,11... | collective-permute-start | bytes 786440 | tf_op jit(solution)/shard_map/ppermute | solution.py:50
  17.2 2.2 %copy-start.6 = (bf16[1,1024,2048]{2,1,0:T(8,128)(2,1)S(1)}, bf16[1,1024,2048]{2,1,0:T(8,128)(2,1)}, u32[]{:S(2)}) copy-start(bf16[1,1024,2048]{2,1,0:T(8,128)(2,1)} %param.7) | copy-start | bytes 12582916
  17.3 5.3 %collective-permute-start.2 = (bf16[256,1024]{1,0:T(8,128)(2,1)S(1)}, bf16[256,1024]{1,0:T(8,128)(2,1)S(1)}, u32[]{:S(2)}, u32[]{:S(2)}) collective-permute-start(bf16[256,1024]{1,0:T(8,128)(2,1)S(1)} %pad_maximum_fusion.1), channel_id=1, source_target_pairs={{0,1},{1,0},{2,3},{3,2},{4,5},{5,4},{6,7},{7,6},{8,9},{9,8},{10,11... | collective-permute-start | bytes 1572872 | tf_op jit(solution)/shard_map/ppermute | solution.py:50
  20.7 8.8 %collective-permute-start.5 = (bf16[128,2048]{1,0:T(8,128)(2,1)S(1)}, bf16[128,2048]{1,0:T(8,128)(2,1)}, u32[]{:S(2)}, u32[]{:S(2)}) collective-permute-start(bf16[128,2048]{1,0:T(8,128)(2,1)S(1)} %split.183), channel_id=1, source_target_pairs={{0,2},{1,5},{2,0},{3,7},{4,6},{5,1},{6,4},{7,3},{8,10},{9,13},{10,... | collective-permute-start | bytes 1572872 | tf_op jit(solution)/shard_map/ppermute | solution.py:98
  23.6 2.2 %copy-start = (bf16[1,64,2048]{2,1,0:T(8,128)(2,1)S(1)}, bf16[1,64,2048]{2,1,0:T(8,128)(2,1)}, u32[]{:S(2)}) copy-start(bf16[1,64,2048]{2,1,0:T(8,128)(2,1)} %param.11) | copy-start | bytes 786436
  24.9 14.5 %copy-start.4 = (f32[1,2048]{1,0:T(1,128)S(1)}, f32[1,2048]{1,0:T(1,128)}, u32[]{:S(2)}) copy-start(f32[1,2048]{1,0:T(1,128)} %param.8) | copy-start | bytes 24580
  24.9 18.8 %copy-start.1 = (bf16[1,64,2048]{2,1,0:T(8,128)(2,1)S(1)}, bf16[1,64,2048]{2,1,0:T(8,128)(2,1)}, u32[]{:S(2)}) copy-start(bf16[1,64,2048]{2,1,0:T(8,128)(2,1)} %param.9) | copy-start | bytes 786436
  25.7 9.4 %collective-permute-start.4 = (bf16[128,2048]{1,0:T(8,128)(2,1)}, bf16[128,2048]{1,0:T(8,128)(2,1)}, u32[]{:S(2)}, u32[]{:S(2)}) collective-permute-start(bf16[128,2048]{1,0:T(8,128)(2,1)} %split.181), channel_id=1, source_target_pairs={{0,2},{1,5},{2,0},{3,7},{4,6},{5,1},{6,4},{7,3},{8,10},{9,13},{10,... | collective-permute-start | bytes 1572872 | tf_op jit(solution)/shard_map/ppermute | solution.py:98
  25.8 40.9 %collective-permute-start.13 = (bf16[64,2048]{1,0:T(8,128)(2,1)S(1)}, bf16[64,2048]{1,0:T(8,128)(2,1)}, u32[]{:S(2)}, u32[]{:S(2)}) collective-permute-start(bf16[64,2048]{1,0:T(8,128)(2,1)S(1)} %bitcast.45), channel_id=1, source_target_pairs={{8,0},{16,8},{24,16},{9,1},{17,9},{25,17},{10,2},{18,10},{26,18},{... | collective-permute-start | bytes 786440 | tf_op jit(solution)/shard_map/ppermute | solution.py:18
  30.7 17.9 %copy-start.5 = (bf16[64,1024]{1,0:T(8,128)(2,1)S(1)}, bf16[64,1024]{1,0:T(8,128)(2,1)}, u32[]{:S(2)}) copy-start(bf16[64,1024]{1,0:T(8,128)(2,1)} %get-tuple-element.45) | copy-start | bytes 393220
  30.7 17.9 %copy-start.7 = (bf16[1,1024,2048]{2,1,0:T(8,128)(2,1)S(1)}, bf16[1,1024,2048]{2,1,0:T(8,128)(2,1)}, u32[]{:S(2)}) copy-start(bf16[1,1024,2048]{2,1,0:T(8,128)(2,1)} %param.7) | copy-start | bytes 12582916
  30.8 7.4 %collective-permute-start.7 = (bf16[64,2048]{1,0:T(8,128)(2,1)S(1)}, bf16[64,2048]{1,0:T(8,128)(2,1)S(1)}, u32[]{:S(2)}, u32[]{:S(2)}) collective-permute-start(bf16[64,2048]{1,0:T(8,128)(2,1)S(1)} %split.256), channel_id=1, source_target_pairs={{0,4},{1,3},{2,6},{3,1},{4,0},{5,7},{6,2},{7,5},{8,12},{9,11},{10,... | collective-permute-start | bytes 786440 | tf_op jit(solution)/shard_map/ppermute | solution.py:98
  38.1 5.5 %collective-permute-start.6 = (bf16[64,2048]{1,0:T(8,128)(2,1)S(1)}, bf16[64,2048]{1,0:T(8,128)(2,1)S(1)}, u32[]{:S(2)}, u32[]{:S(2)}) collective-permute-start(bf16[64,2048]{1,0:T(8,128)(2,1)S(1)} %split.257), channel_id=1, source_target_pairs={{0,4},{1,3},{2,6},{3,1},{4,0},{5,7},{6,2},{7,5},{8,12},{9,11},{10,... | collective-permute-start | bytes 786440 | tf_op jit(solution)/shard_map/ppermute | solution.py:98
  39.6 7.5 %collective-permute-start.9 = (bf16[64,2048]{1,0:T(8,128)(2,1)S(1)}, bf16[64,2048]{1,0:T(8,128)(2,1)S(1)}, u32[]{:S(2)}, u32[]{:S(2)}) collective-permute-start(bf16[64,2048]{1,0:T(8,128)(2,1)S(1)} %fusion.37), channel_id=1, source_target_pairs={{0,4},{1,3},{2,6},{3,1},{4,0},{5,7},{6,2},{7,5},{8,12},{9,11},{10,... | collective-permute-start | bytes 786440 | tf_op jit(solution)/shard_map/ppermute | solution.py:98
  43.9 13.0 %collective-permute-start.8 = (bf16[64,2048]{1,0:T(8,128)(2,1)S(1)}, bf16[64,2048]{1,0:T(8,128)(2,1)S(1)}, u32[]{:S(2)}, u32[]{:S(2)}) collective-permute-start(bf16[64,2048]{1,0:T(8,128)(2,1)S(1)} %add_convert_fusion.4), channel_id=1, source_target_pairs={{0,8},{8,16},{16,24},{1,9},{9,17},{17,25},{2,10},{10,18},{18,26},{... | collective-permute-start | bytes 786440 | tf_op jit(solution)/shard_map/ppermute | solution.py:18
  47.1 8.4 %collective-permute-start.10 = (bf16[128,2048]{1,0:T(8,128)(2,1)S(1)}, bf16[128,2048]{1,0:T(8,128)(2,1)S(1)}, u32[]{:S(2)}, u32[]{:S(2)}) collective-permute-start(bf16[128,2048]{1,0:T(8,128)(2,1)S(1)} %pad_maximum_fusion.2), channel_id=1, source_target_pairs={{0,2},{1,5},{2,0},{3,7},{4,6},{5,1},{6,4},{7,3},{8,10},{9,13},{10,... | collective-permute-start | bytes 1572872 | tf_op jit(solution)/shard_map/ppermute | solution.py:98
  49.9 6.9 %copy-start.3 = (bf16[64,2048]{1,0:T(8,128)(2,1)S(1)}, bf16[64,2048]{1,0:T(8,128)(2,1)}, u32[]{:S(2)}) copy-start(bf16[64,2048]{1,0:T(8,128)(2,1)} %param.10) | copy-start | bytes 786436
  50.0 11.2 %collective-permute-start.16 = (bf16[128,2048]{1,0:T(8,128)(2,1)S(1)}, bf16[128,2048]{1,0:T(8,128)(2,1)S(1)}, u32[]{:S(2)}, u32[]{:S(2)}) collective-permute-start(bf16[128,2048]{1,0:T(8,128)(2,1)S(1)} %split.191), channel_id=1, source_target_pairs={{0,2},{1,5},{2,0},{3,7},{4,6},{5,1},{6,4},{7,3},{8,10},{9,13},{10,... | collective-permute-start | bytes 1572872 | tf_op jit(solution)/shard_map/ppermute | solution.py:98
  56.8 18.4 %copy-start.2 = (bf16[64,2048]{1,0:T(8,128)(2,1)S(1)}, bf16[64,2048]{1,0:T(8,128)(2,1)}, u32[]{:S(2)}) copy-start(bf16[64,2048]{1,0:T(8,128)(2,1)} %param.12) | copy-start | bytes 786436
  57.1 5.5 %collective-permute-start.11 = (bf16[128,1024]{1,0:T(8,128)(2,1)S(1)}, bf16[128,1024]{1,0:T(8,128)(2,1)S(1)}, u32[]{:S(2)}, u32[]{:S(2)}) collective-permute-start(bf16[128,1024]{1,0:T(8,128)(2,1)S(1)} %get-tuple-element.50), channel_id=1, source_target_pairs={{0,1},{1,0},{2,3},{3,2},{4,5},{5,4},{6,7},{7,6},{8,9},{9,8},{10,11... | collective-permute-start | bytes 786440 | tf_op jit(solution)/shard_map/ppermute | solution.py:50
  61.3 5.3 %collective-permute-start.17 = (bf16[64,2048]{1,0:T(8,128)(2,1)S(1)}, bf16[64,2048]{1,0:T(8,128)(2,1)S(1)}, u32[]{:S(2)}, u32[]{:S(2)}) collective-permute-start(bf16[64,2048]{1,0:T(8,128)(2,1)S(1)} %split.255), channel_id=1, source_target_pairs={{0,4},{1,3},{2,6},{3,1},{4,0},{5,7},{6,2},{7,5},{8,12},{9,11},{10,... | collective-permute-start | bytes 786440 | tf_op jit(solution)/shard_map/ppermute | solution.py:98
  62.7 12.5 %collective-permute-start.14 = (bf16[64,1024]{1,0:T(8,128)(2,1)S(1)}, bf16[64,1024]{1,0:T(8,128)(2,1)S(1)}, u32[]{:S(2)}, u32[]{:S(2)}) collective-permute-start(bf16[64,1024]{1,0:T(8,128)(2,1)S(1)} %get-tuple-element.112), channel_id=1, source_target_pairs={{8,2},{9,6},{10,0},{11,4},{13,7},{12,3},{15,5},{14,1},{16,10},{17,... | collective-permute-start | bytes 393224 | tf_op jit(solution)/shard_map/ppermute | solution.py:119
  64.0 11.2 %collective-permute-start.15 = (bf16[64,1024]{1,0:T(8,128)(2,1)S(1)}, bf16[64,1024]{1,0:T(8,128)(2,1)S(1)}, u32[]{:S(2)}, u32[]{:S(2)}) collective-permute-start(bf16[64,1024]{1,0:T(8,128)(2,1)S(1)} %get-tuple-element.113), channel_id=1, source_target_pairs={{8,0},{9,4},{10,2},{11,6},{13,5},{12,1},{15,7},{14,3},{16,8},{17,1... | collective-permute-start | bytes 393224 | tf_op jit(solution)/shard_map/ppermute | solution.py:119
  66.6 9.9 %collective-permute-start.18 = (bf16[64,1024]{1,0:T(8,128)(2,1)S(1)}, bf16[64,1024]{1,0:T(8,128)(2,1)S(1)}, u32[]{:S(2)}, u32[]{:S(2)}) collective-permute-start(bf16[64,1024]{1,0:T(8,128)(2,1)S(1)} %get-tuple-element.108), channel_id=1, source_target_pairs={{0,2},{1,6},{2,0},{3,4},{5,7},{4,3},{7,5},{6,1},{8,10},{9,14},{10,... | collective-permute-start | bytes 393224 | tf_op jit(solution)/shard_map/ppermute | solution.py:111
  73.3 6.3 %collective-permute-start.12 = (bf16[64,1024]{1,0:T(8,128)(2,1)S(1)}, bf16[64,1024]{1,0:T(8,128)(2,1)S(1)}, u32[]{:S(2)}, u32[]{:S(2)}) collective-permute-start(bf16[64,1024]{1,0:T(8,128)(2,1)S(1)} %get-tuple-element.109), channel_id=1, source_target_pairs={{0,0},{1,4},{2,2},{3,6},{5,5},{4,1},{7,7},{6,3},{8,8},{9,12},{10,1... | collective-permute-start | bytes 393224 | tf_op jit(solution)/shard_map/ppermute | solution.py:111
  79.6 1.6 %collective-permute-start.19 = (bf16[128,1024]{1,0:T(8,128)(2,1)S(1)}, bf16[128,1024]{1,0:T(8,128)(2,1)S(1)}, u32[]{:S(2)}, u32[]{:S(2)}) collective-permute-start(bf16[128,1024]{1,0:T(8,128)(2,1)S(1)} %constant_dynamic-update-slice_fusion), channel_id=1, source_target_pairs={{0,1},{1,0},{2,3},{3,2},{4,5},{5,4},{6,7},{7,6},{8,9},{9,8},{10,11... | collective-permute-start | bytes 786440 | tf_op jit(solution)/shard_map/ppermute | solution.py:50
  79.6 7.6 %collective-permute-start.21 = (bf16[64,2048]{1,0:T(8,128)(2,1)S(1)}, bf16[64,2048]{1,0:T(8,128)(2,1)S(1)}, u32[]{:S(2)}, u32[]{:S(2)}) collective-permute-start(bf16[64,2048]{1,0:T(8,128)(2,1)S(1)} %get-tuple-element.64), channel_id=1, source_target_pairs={{0,4},{1,3},{2,6},{3,1},{4,0},{5,7},{6,2},{7,5},{8,12},{9,11},{10,... | collective-permute-start | bytes 786440 | tf_op jit(solution)/shard_map/ppermute | solution.py:98
  82.6 11.9 %collective-permute-start.20 = (bf16[128,2048]{1,0:T(8,128)(2,1)S(1)}, bf16[128,2048]{1,0:T(8,128)(2,1)S(1)}, u32[]{:S(2)}, u32[]{:S(2)}) collective-permute-start(bf16[128,2048]{1,0:T(8,128)(2,1)S(1)} %split.199), channel_id=1, source_target_pairs={{0,2},{1,5},{2,0},{3,7},{4,6},{5,1},{6,4},{7,3},{8,10},{9,13},{10,... | collective-permute-start | bytes 1572872 | tf_op jit(solution)/shard_map/ppermute | solution.py:98
  82.9 11.6 %collective-permute-start.25 = (bf16[64,1024]{1,0:T(8,128)(2,1)S(1)}, bf16[64,1024]{1,0:T(8,128)(2,1)S(1)}, u32[]{:S(2)}, u32[]{:S(2)}) collective-permute-start(bf16[64,1024]{1,0:T(8,128)(2,1)S(1)} %get-tuple-element.112), channel_id=1, source_target_pairs={{0,2},{1,6},{2,0},{3,4},{5,7},{4,3},{7,5},{6,1},{8,10},{9,14},{10,... | collective-permute-start | bytes 393224 | tf_op jit(solution)/shard_map/ppermute | solution.py:111
  84.7 9.8 %collective-permute-start.26 = (bf16[64,1024]{1,0:T(8,128)(2,1)S(1)}, bf16[64,1024]{1,0:T(8,128)(2,1)S(1)}, u32[]{:S(2)}, u32[]{:S(2)}) collective-permute-start(bf16[64,1024]{1,0:T(8,128)(2,1)S(1)} %get-tuple-element.113), channel_id=1, source_target_pairs={{0,0},{1,4},{2,2},{3,6},{5,5},{4,1},{7,7},{6,3},{8,8},{9,12},{10,1... | collective-permute-start | bytes 393224 | tf_op jit(solution)/shard_map/ppermute | solution.py:111
  87.3 12.7 %collective-permute-start.23 = (bf16[128,2048]{1,0:T(8,128)(2,1)S(1)}, bf16[128,2048]{1,0:T(8,128)(2,1)S(1)}, u32[]{:S(2)}, u32[]{:S(2)}) collective-permute-start(bf16[128,2048]{1,0:T(8,128)(2,1)S(1)} %pad_maximum_fusion.3), channel_id=1, source_target_pairs={{0,2},{1,5},{2,0},{3,7},{4,6},{5,1},{6,4},{7,3},{8,10},{9,13},{10,... | collective-permute-start | bytes 1572872 | tf_op jit(solution)/shard_map/ppermute | solution.py:98
  101.4 1.6 %collective-permute-start.24 = (bf16[128,1024]{1,0:T(8,128)(2,1)S(1)}, bf16[128,1024]{1,0:T(8,128)(2,1)S(1)}, u32[]{:S(2)}, u32[]{:S(2)}) collective-permute-start(bf16[128,1024]{1,0:T(8,128)(2,1)S(1)} %get-tuple-element.61), channel_id=1, source_target_pairs={{0,1},{1,0},{2,3},{3,2},{4,5},{5,4},{6,7},{7,6},{8,9},{9,8},{10,11... | collective-permute-start | bytes 786440 | tf_op jit(solution)/shard_map/ppermute | solution.py:50
  102.0 6.3 %collective-permute-start.22 = (bf16[64,2048]{1,0:T(8,128)(2,1)S(1)}, bf16[64,2048]{1,0:T(8,128)(2,1)S(1)}, u32[]{:S(2)}, u32[]{:S(2)}) collective-permute-start(bf16[64,2048]{1,0:T(8,128)(2,1)S(1)} %split.254), channel_id=1, source_target_pairs={{0,4},{1,3},{2,6},{3,1},{4,0},{5,7},{6,2},{7,5},{8,12},{9,11},{10,... | collective-permute-start | bytes 786440 | tf_op jit(solution)/shard_map/ppermute | solution.py:98
  103.1 6.8 %collective-permute-start.27 = (bf16[64,1024]{1,0:T(8,128)(2,1)S(1)}, bf16[64,1024]{1,0:T(8,128)(2,1)S(1)}, u32[]{:S(2)}, u32[]{:S(2)}) collective-permute-start(bf16[64,1024]{1,0:T(8,128)(2,1)S(1)} %get-tuple-element.104), channel_id=1, source_target_pairs={{0,2},{1,6},{2,0},{3,4},{5,7},{4,3},{7,5},{6,1},{8,10},{9,14},{10,... | collective-permute-start | bytes 393224 | tf_op jit(solution)/shard_map/ppermute | solution.py:111
  104.4 6.7 %collective-permute-start.28 = (bf16[64,1024]{1,0:T(8,128)(2,1)S(1)}, bf16[64,1024]{1,0:T(8,128)(2,1)S(1)}, u32[]{:S(2)}, u32[]{:S(2)}) collective-permute-start(bf16[64,1024]{1,0:T(8,128)(2,1)S(1)} %get-tuple-element.105), channel_id=1, source_target_pairs={{0,0},{1,4},{2,2},{3,6},{5,5},{4,1},{7,7},{6,3},{8,8},{9,12},{10,1... | collective-permute-start | bytes 393224 | tf_op jit(solution)/shard_map/ppermute | solution.py:111

commit v4 on v0

v4 whole, which is shorter than its diff:
```python
import jax
import jax.numpy as jnp
from jax import lax
from jax.sharding import PartitionSpec as P

F32 = jnp.float32
BF16 = jnp.bfloat16

TURNED = ("B0", "G1")
AT_ONCE = ("A0", "A1", "G0")
GATES = {
    "A0_o": ("weight",),
    "A1_a0": ("A0_x",),
    "A1_in": ("A0_m0",),
    "A1_s": ("B0_m0",),
    "A2_a0": ("B0_m1",),
    "A2_in": ("B0_m0",),
    "A2_o": ("A2_a0",),
    "A2_s": ("B0_m1",),
    "A3_a0": ("A3_m1",),
    "A3_a1": ("sc2",),
    "A3_in": ("zf_a",),
    "B0_a0": ("F1_t0",),
    "B0_a1": ("F1_m1",),
    "B1_a0": ("G0_h",),
    "B1_a1": ("G0_s",),
    "B1_x": ("out1",),
    "D0_a0": ("feed",),
    "F1_a1": ("sc1",),
    "F2_a0": ("G1_m1",),
    "F2_a1": ("G1_s",),
    "F2_x": ("A3_o",),
    "G0_a0": ("out1",),
    "G0_a1": ("B1_t0",),
    "G0_h": ("B1_t0", "feed"),
    "G1_a0": ("F2_t0",),
    "G1_a1": ("F2_m1",),
    "G1_h": ("G1_m1",),
    "W0_m": ("G0_m1",),
    "gr1": ("F2_t0",),
    "out2": ("G1_m1",),
    "zr_m": ("B0_m1",),
}


def silu_slope(values):
    sigma = jax.nn.sigmoid(values)
    return sigma * (1.0 + values * (1.0 - sigma))


def passed_along(value, steps):
    count = lax.axis_size("segment")
    first, last = (max(0, -steps), min(count, count - steps))
    return lax.ppermute(value, "segment", [(source, source + steps) for source in range(first, last)])


def fixed(value):
    return lax.optimization_barrier(value)


def bits_of(count):
    return count.bit_length() - 1


def cut(value, count, axis=0):
    return jnp.split(value, count, axis=axis)


def xor_order(blocks, index):
    for bit in range(bits_of(len(blocks))):
        flip = 1 << bit
        is_set = (index & flip) != 0
        blocks = [jnp.where(is_set, blocks[k ^ flip], blocks[k]) for k in range(len(blocks))]
    return blocks


def col_swap(value, flip):
    count = lax.axis_size("col")
    return lax.ppermute(value, "col", [(source, source ^ flip) for source in range(count)])


class Plane:
    def __init__(self):
        self.rows, self.cols = lax.axis_size("row"), lax.axis_size("col")
        self.row, self.col = lax.axis_index("row"), lax.axis_index("col")
        self.steps = bits_of(self.rows)
        self.per_col = self.rows // self.cols
        self.home = self.row // self.per_col

    def flips(self, col, turn):
        return [1 << ((col + turn + step) % self.steps) for step in range(self.steps)]

    def places(self, col, turn):
        flips = self.flips(col, turn)
        return [
            sum(flip for at, flip in enumerate(flips) if place >> (self.steps - 1 - at) & 1)
            for place in range(self.rows)
        ]

    def choose(self, orders):
        chosen = orders[0]
        for at in range(1, len(orders)):
            picked = self.col % len(orders) == at
            chosen = [
                old if old is new else jnp.where(picked, new, old)
                for old, new in zip(chosen, orders[at])
            ]
        return chosen

    def by_place(self, blocks, turn):
        kinds = range(max(self.steps, 1))
        return self.choose([[blocks[k] for k in self.places(col, turn)] for col in kinds])

    def by_k(self, blocks, turn):
        orders = []
        for col in range(max(self.steps, 1)):
            places = self.places(col, turn)
            orders.append([blocks[places.index(k)] for k in range(self.rows)])
        return self.choose(orders)

    def step_swap(self, value, step, turn):
        pairs = []
        for row in range(self.rows):
            for col in range(self.cols):
                other = row ^ self.flips(col, turn)[step]
                pairs.append((row * self.cols + col, other * self.cols + col))
        return lax.ppermute(value, ("row", "col"), pairs)

    def across(self, value, shift, onward=0):
        pairs = []
        for row in range(self.rows):
            home = row // self.per_col
            for j in range(self.cols):
                other = row ^ (j * self.per_col + shift)
                pairs.append((row * self.cols + (home ^ j), other * self.cols + home))
        if not onward:
            return lax.ppermute(value, ("row", "col"), pairs)
        sections, size = lax.axis_size("segment"), self.rows * self.cols
        pairs = [
            (at * size + source, (at + onward) * size + target)
            for at in range(sections)
            if 0 <= at + onward < sections
            for source, target in pairs
        ]
        return lax.ppermute(value, ("segment", "row", "col"), pairs)

    def joined(self, half, others, at_once):
        if at_once:
            halves = xor_order(others, self.home)
        else:
            halves = xor_order([half] + others, self.col ^ self.home)
        return [block for half in halves for block in cut(half, self.per_col)]

    def shares(self, partial, turn):
        ordered = jnp.concatenate(self.by_k(cut(partial, self.rows), turn), axis=0)
        return xor_order(cut(ordered, self.cols), self.col ^ self.home)

    def in_columns(self, arrived):
        return jnp.concatenate(xor_order(arrived, self.row % self.per_col), axis=1)


class Flow:
    def __init__(self, gates):
        self.gates, self.rules, self.values = gates, {}, {}

    def rule(self, name, make):
        self.rules[name] = make

    def __call__(self, name):
        if name not in self.values:
            value = self.rules[name]()
            others = [self(other) for other in self.gates.get(name, ()) if other in self.rules]
            if others:
                value = lax.optimization_barrier((value, others))[0]
            self.values[name] = value
        return self.values[name]


def shards(weights, layer_gains, incoming, fresh_batch, returning, fresh_cotangent, stashed_inputs):
    segment_index = lax.axis_index("segment")
    segment_count = lax.axis_size("segment")
    layer_gain = layer_gains[0][None, :]
    plane = Plane()
    steps, shifts = plane.steps, range(plane.per_col)
    flow = Flow(GATES)
    rule = flow.rule

    def advance(own_block, pre_act):
        return fixed((own_block.astype(F32) + layer_gain * jax.nn.silu(pre_act)).astype(BF16))

    def scale(upstream, pre_act):
        return fixed((upstream.astype(F32) * layer_gain * silu_slope(pre_act)).astype(BF16))

    def retreat(upstream, back_term):
        return (upstream.astype(F32) + back_term.astype(F32)).astype(BF16)

    def spread(name, block):
        def message(shift):
            pieces = cut(flow(f"{name}_in"), plane.per_col, axis=1)
            return xor_order(pieces, plane.row % plane.per_col)[shift]

        def others():
            half = flow(f"{name}_s")
            if name in AT_ONCE:
                halves = lax.all_gather(half, "col", axis=0, tiled=False)
                return [halves[col] for col in range(plane.cols)]
            return [col_swap(half, flip) for flip in range(1, plane.cols)]

        rule(f"{name}_in", block)
        for shift in shifts:
            rule(f"{name}_m{shift}", lambda shift=shift: message(shift))
            rule(f"{name}_a{shift}", lambda shift=shift: plane.across(flow(f"{name}_m{shift}"), shift))
        rule(f"{name}_s", lambda: jnp.concatenate([flow(f"{name}_a{at}") for at in shifts], axis=0))
        rule(f"{name}_o", others)
        rule(f"{name}_x", lambda: plane.joined(flow(f"{name}_s"), flow(f"{name}_o"), name in AT_ONCE))

    def product(name, source):
        turn = int(name in TURNED)

        def multiplied():
            full = jnp.concatenate(plane.by_place(flow(f"{name}_x"), turn), axis=0)
            return jnp.dot(full, flow("weight"), preferred_element_type=F32).astype(BF16)

        def message(step):
            return fixed(cut(flow(f"{name}_t{step}"), 2)[1].astype(BF16))

        def total(step):
            ours = cut(flow(f"{name}_t{step}"), 2)[0]
            return ours.astype(F32) + flow(f"{name}_a{step}").astype(F32)

        rule(f"{name}_x", lambda: flow(f"{source}_x"))
        rule(f"{name}_t0", multiplied)
        for step in range(steps):
            rule(f"{name}_m{step}", lambda step=step: message(step))
            rule(
                f"{name}_a{step}",
                lambda step=step: plane.step_swap(flow(f"{name}_m{step}"), step, turn),
            )
            rule(f"{name}_t{step + 1}", lambda step=step: total(step))
        return lambda: flow(f"{name}_t{steps}").astype(F32)

    def back(name, scaled):
        turn = int(name in TURNED)

        def doubled(at):
            block = jnp.concatenate([flow(f"{name}_m{at}"), flow(f"{name}_a{at}")], axis=0)
            return fixed(block) if at + 1 < steps else block

        def multiplied():
            return lax.dot_general(
                flow(f"{name}_m{steps}"),
                flow("weight"),
                (((1,), (1,)), ((), ())),
                preferred_element_type=F32,
            ).astype(BF16)

        def others():
            shares = flow(f"{name}_h")
            if name in AT_ONCE and plane.cols == 2:
                both = lax.all_gather(shares[1], "col", axis=0, tiled=False)
                return [jnp.where(plane.col == 0, both[1], both[0])]
            return [col_swap(shares[flip], flip) for flip in range(1, plane.cols)]

        def total():
            ours = flow(f"{name}_h")[0].astype(F32)
            return fixed(sum([o.astype(F32) for o in flow(f"{name}_o")], ours).astype(BF16))

        rule(f"{name}_m0", lambda: flow(scaled))
        for at in range(steps):
            step = steps - 1 - at
            rule(
                f"{name}_a{at}",
                lambda at=at, step=step: plane.step_swap(flow(f"{name}_m{at}"), step, turn),
            )
            rule(f"{name}_m{at + 1}", lambda at=at: doubled(at))
        rule(f"{name}_p", multiplied)
        rule(f"{name}_h", lambda: fixed(plane.shares(flow(f"{name}_p"), turn)))
        rule(f"{name}_o", others)
        rule(f"{name}_s", total)

    def deliver(name, source, onward=0):
        rule(f"{name}_m", lambda: cut(flow(source), plane.per_col))
        for shift in shifts:
            rule(
                f"{name}_a{shift}",
                lambda shift=shift: plane.across(flow(f"{name}_m")[shift], shift, onward),
            )
        return lambda: plane.in_columns([flow(f"{name}_a{shift}") for shift in shifts])

    rule("weight", lambda: weights[0])

    spread("A0", lambda: stashed_inputs[0, 0])
    spread("A1", lambda: incoming[0])
    spread("A2", lambda: stashed_inputs[0, 1])
    first_back, first_pre, second_back = product("B0", "A0"), product("F1", "A1"), product("B1", "A2")
    rule("sc1", lambda: scale(returning[0], first_back()))
    rule("out1", lambda: advance(incoming[0], first_pre()))
    back("G0", "sc1")
    own_back = deliver("W0", "G0_s")
    rule("gr1", lambda: retreat(returning[0], own_back()))

    rule("zf_a", lambda: passed_along(flow("out1"), 1))
    rule("feed", lambda: jnp.where(segment_index == 0, fresh_batch, flow("zf_a")))
    rule("zr_m", lambda: returning[0])
    rule("zr_a", lambda: passed_along(flow("zr_m"), -1))
    next_back = deliver("D0", "G0_s", -1)
    rule("ag", lambda: retreat(flow("zr_a"), next_back()))
    rule("up", lambda: jnp.where(segment_index == segment_count - 1, fresh_cotangent, flow("ag")))

    spread("A3", lambda: flow("feed"))
    second_pre = product("F2", "A3")
    rule("out2", lambda: advance(flow("feed"), second_pre()))
    rule("sc2", lambda: scale(flow("up"), second_back()))
    back("G1", "sc2")
    last_back = deliver("D1", "G1_s")
    rule("gr2", lambda: retreat(flow("up"), last_back()))

    layer_outputs = jnp.stack([flow("out1"), flow("out2")], axis=0)[None]
    input_grads = jnp.stack([flow("gr1"), flow("gr2")], axis=0)[None]
    return (layer_outputs, input_grads)


def solution(mesh):
    in_specs = (
        P("segment", "row", "col"),
        P("segment", "col"),
        P("segment", "row", "col"),
        P("row", "col"),
        P("segment", "row", "col"),
        P("row", "col"),
        P("segment", None, "row", "col"),
    )
    out_specs = (P("segment", None, "row", "col"), P("segment", None, "row", "col"))
    return jax.shard_map(shards, mesh=mesh, in_specs=in_specs, out_specs=out_specs, check_vma=False)
```

time: 246 us -> 106 us (0.43)
  waiting for transfers between devices: 161 us -> 36.5 us
  matrix products: 49.3 us -> 7.68 us
  starting transfers between devices: 4.5 us -> 45.5 us
  between operations: 13.8 us -> 1.32 us
  blocking collectives: 10.2 us -> 7.12 us
    all_gather x1 -> x0, waiting for transfers between devices: 156 us -> none  [shards(): weight_panel = lax.all_gather(weight_block, 'row', axis=0, tiled=True)]
    dot_general x4 -> x6, matrix products: 49.3 us -> 7.68 us  [the longest x4 5.11 us: multiplied(): jnp.dot(full, flow('weight'), preferred_element_type=F32).astype(BF16)]
    ppermute x2 -> x31, starting transfers between devices: 4.38 us -> 45.5 us  [the longest x12 27.2 us: across(): return lax.ppermute(value, ('row', 'col'), pairs)]
    ppermute x2 -> x31, waiting for transfers between devices: 4.52 us -> 36.5 us  [the longest x12 14.8 us: across(): return lax.ppermute(value, ('row', 'col'), pairs)]
    all_gather x4 -> x3, blocking collectives: 10.2 us -> 7.12 us  [the longest x2 4.94 us: others(): halves = lax.all_gather(half, 'col', axis=0, tiled=False)]
  transfers between devices with their start and end apart: 5 -> 31, of which waited for: 3 -> 18; matrix products, arithmetic and copies ran while one was open for 9% -> 11% of each run, Pallas kernels for 0% -> 0%
where the time goes in v4:
time: 106 us; the launch traced here: 105 us
  starting transfers between devices  45.5 us (43%)
  waiting for transfers between devices  36.5 us (34%)
  matrix products  7.68 us (7%)
  blocking collectives  7.12 us (7%)
  other arithmetic  5.32 us (5%)
  local copies, waits for them, and re-layouts  1.55 us (1%)
  between operations  1.32 us (1%)
    ppermute x12, starting transfers between devices, across(): return lax.ppermute(value, ('row', 'col'), pairs)  27.2 us
    ppermute x12, waiting for transfers between devices, across(): return lax.ppermute(value, ('row', 'col'), pairs)  14.8 us
    ppermute x12, waiting for transfers between devices, step_swap(): return lax.ppermute(value, ('row', 'col'), pairs)  10 us
    ppermute x12, starting transfers between devices, step_swap(): return lax.ppermute(value, ('row', 'col'), pairs)  9.96 us
    ppermute x2, waiting for transfers between devices, across(): return lax.ppermute(value, ('segment', 'row', 'col'), pairs)  8.24 us
    dot_general x4, matrix products, multiplied(): jnp.dot(full, flow('weight'), preferred_element_type=F32).astype(BF16)  5.11 us
    all_gather x2, blocking collectives, others(): halves = lax.all_gather(half, 'col', axis=0, tiled=False)  4.94 us
    ppermute x2, starting transfers between devices, passed_along(): lax.ppermute(value, 'segment', [(source, source + steps) for source in ra...  4.5 us
  transfers between devices with their start and end apart: 31, of which 18 were waited for; matrix products, arithmetic and copies ran while one was open for 11% of the time, Pallas kernels for 0%

profile of v4, /device:TPU:1, one launch (start us, length us, event | category | flops | bytes accessed | tf_op | source)
XLA Modules:
  0.0 104.9 jit_solution(4456579807612715738)
XLA Ops:
  0.6 1.1 %slice_bitcast_fusion = (bf16[64,2048]{1,0:T(8,128)(2,1)S(1)}, bf16[64,2048]{1,0:T(8,128)(2,1)S(1)}) fusion(bf16[1,2,64,2048]{3,2,1,0:T(8,128)(2,1)} %param.13), kind=kLoop, calls=%fused_computation.84 | loop fusion | bytes 1048576 | tf_op jit(solution)/shard_map/squeeze | solution.py:294
  1.7 4.5 %collective-permute-start.1 = (bf16[64,1024]{1,0:T(8,128)(2,1)S(1)}, bf16[64,1024]{1,0:T(8,128)(2,1)S(1)}, u32[]{:S(2)}, u32[]{:S(2)}) collective-permute-start(bf16[64,1024]{1,0:T(8,128)(2,1)S(1)} %get-tuple-element.153), channel_id=1, source_target_pairs={{0,0},{1,4},{2,2},{3,6},{5,5},{4,1},{7,7},{6,3},{8,8},{9,12},{10,1... | collective-permute-start | bytes 393224 | tf_op jit(solution)/shard_map/ppermute | solution.py:137
  6.3 1.0 collective-permute-start.2
  7.3 1.0 broadcast_select_fusion.33
  8.3 3.6 %collective-permute-start = (bf16[64,1024]{1,0:T(8,128)(2,1)S(1)}, bf16[64,1024]{1,0:T(8,128)(2,1)S(1)}, u32[]{:S(2)}, u32[]{:S(2)}) collective-permute-start(bf16[64,1024]{1,0:T(8,128)(2,1)S(1)} %get-tuple-element.154), channel_id=1, source_target_pairs={{0,0},{1,4},{2,2},{3,6},{5,5},{4,1},{7,7},{6,3},{8,8},{9,12},{10,1... | collective-permute-start | bytes 393224 | tf_op jit(solution)/shard_map/ppermute | solution.py:137
  12.5 2.3 %all-gather = bf16[256,1024]{1,0:T(8,128)(2,1)S(1)} all-gather(bf16[128,1024]{1,0:T(8,128)(2,1)S(1)} %pad_maximum_fusion.2), channel_id=2, replica_groups=mesh['segment'=4,'row'=4,'col'=2] {'col'}, dimensions={0}, use_global_device_ids=true | all-gather | bytes 786432 | tf_op jit(solution)/shard_map/all_gather | solution.py:205
  14.9 1.3 %convolution_convert_fusion.3 = bf16[256,2048]{1,0:T(8,128)(2,1)S(1)} fusion(bf16[64,1024]{1,0:T(8,128)(2,1)S(1)} %get-tuple-element.151, bf16[64,1024]{1,0:T(8,128)(2,1)S(1)} %get-tuple-element.117, bf16[64,1024]{1,0:T(8,128)(2,1)S(1)} %get-tuple-element.116, bf16[64,1024]{1,0:T(8,128)(2,1)S(1)} %get-tuple-element.150, bf16[1,1024,2048]{2,1,0:T(8,128)(2,1)S(1)} %copy-done.5), kind=kOutput, calls=%fused_computation.3 | convolution fusion | flops 1076363264 | bytes 5767168 | tf_op jit(solution)/shard_map/dot_general | solution.py:222
  16.3 0.8 collective-permute-start.6
  17.3 2.6 %all-gather.1 = bf16[256,1024]{1,0:T(8,128)(2,1)S(1)} all-gather(bf16[128,1024]{1,0:T(8,128)(2,1)S(1)} %pad_maximum_fusion.3), channel_id=3, replica_groups=mesh['segment'=4,'row'=4,'col'=2] {'col'}, dimensions={0}, use_global_device_ids=true | all-gather | bytes 786432 | tf_op jit(solution)/shard_map/all_gather | solution.py:205
  20.0 1.3 %convolution_convert_fusion.2 = bf16[256,2048]{1,0:T(8,128)(2,1)S(1)} fusion(bf16[64,1024]{1,0:T(8,128)(2,1)S(1)} %get-tuple-element.149, bf16[64,1024]{1,0:T(8,128)(2,1)S(1)} %get-tuple-element.113, bf16[64,1024]{1,0:T(8,128)(2,1)S(1)} %get-tuple-element.112, bf16[64,1024]{1,0:T(8,128)(2,1)S(1)} %get-tuple-element.148, bf16[1,1024,2048]{2,1,0:T(8,128)(2,1)S(1)} %copy-done.5), kind=kOutput, calls=%fused_computation.2 | convolution fusion | flops 1076363264 | bytes 5767168 | tf_op jit(solution)/shard_map/dot_general | solution.py:222
  21.4 0.9 collective-permute-start.4
  22.3 2.5 %collective-permute-start.14 = (bf16[64,1024]{1,0:T(8,128)(2,1)S(1)}, bf16[64,1024]{1,0:T(8,128)(2,1)S(1)}, u32[]{:S(2)}, u32[]{:S(2)}) collective-permute-start(bf16[64,1024]{1,0:T(8,128)(2,1)S(1)} %get-tuple-element.144), channel_id=1, source_target_pairs={{0,0},{1,4},{2,2},{3,6},{5,5},{4,1},{7,7},{6,3},{8,8},{9,12},{10,1... | collective-permute-start | bytes 393224 | tf_op jit(solution)/shard_map/ppermute | solution.py:137
  24.8 1.3 %collective-permute-start.15 = (bf16[64,1024]{1,0:T(8,128)(2,1)S(1)}, bf16[64,1024]{1,0:T(8,128)(2,1)S(1)}, u32[]{:S(2)}, u32[]{:S(2)}) collective-permute-start(bf16[64,1024]{1,0:T(8,128)(2,1)S(1)} %get-tuple-element.145), channel_id=1, source_target_pairs={{0,2},{1,6},{2,0},{3,4},{5,7},{4,3},{7,5},{6,1},{8,10},{9,14},{10,... | collective-permute-start | bytes 393224 | tf_op jit(solution)/shard_map/ppermute | solution.py:137
  26.3 5.9 %collective-permute-done.4 = bf16[128,2048]{1,0:T(8,128)(2,1)S(1)} collective-permute-done((bf16[128,2048]{1,0:T(8,128)(2,1)S(1)}, bf16[128,2048]{1,0:T(8,128)(2,1)S(1)}, u32[]{:S(2)}, u32[]{:S(2)}) %collective-permute-start.4) | collective-permute-done | bytes 524320 | tf_op jit(solution)/shard_map/ppermute | solution.py:127
  32.5 0.8 collective-permute-start.5
  33.9 1.3 %collective-permute-start.11 = (bf16[64,2048]{1,0:T(8,128)(2,1)S(1)}, bf16[64,2048]{1,0:T(8,128)(2,1)S(1)}, u32[]{:S(2)}, u32[]{:S(2)}) collective-permute-start(bf16[64,2048]{1,0:T(8,128)(2,1)S(1)} %bitcast.44), channel_id=1, source_target_pairs={{8,0},{16,8},{24,16},{9,1},{17,9},{25,17},{10,2},{18,10},{26,18},{... | collective-permute-start | bytes 786440 | tf_op jit(solution)/shard_map/ppermute | solution.py:54
  35.2 1.9 %collective-permute-done.7 = bf16[64,2048]{1,0:T(8,128)(2,1)S(1)} collective-permute-done((bf16[64,2048]{1,0:T(8,128)(2,1)S(1)}, bf16[64,2048]{1,0:T(8,128)(2,1)S(1)}, u32[]{:S(2)}, u32[]{:S(2)}) %collective-permute-start.7) | collective-permute-done | bytes 262176 | tf_op jit(solution)/shard_map/ppermute | solution.py:127
  37.3 0.9 collective-permute-start.12
  38.3 0.8 collective-permute-done.5
  39.3 3.2 %collective-permute-start.8 = (bf16[64,2048]{1,0:T(8,128)(2,1)S(1)}, bf16[64,2048]{1,0:T(8,128)(2,1)S(1)}, u32[]{:S(2)}, u32[]{:S(2)}) collective-permute-start(bf16[64,2048]{1,0:T(8,128)(2,1)S(1)} %add_convert_fusion.3), channel_id=1, source_target_pairs={{0,8},{8,16},{16,24},{1,9},{9,17},{17,25},{2,10},{10,18},{18,26},{... | collective-permute-start | bytes 786440 | tf_op jit(solution)/shard_map/ppermute | solution.py:54
  43.0 2.1 %collective-permute-start.13 = (bf16[128,2048]{1,0:T(8,128)(2,1)S(1)}, bf16[128,2048]{1,0:T(8,128)(2,1)S(1)}, u32[]{:S(2)}, u32[]{:S(2)}) collective-permute-start(bf16[128,2048]{1,0:T(8,128)(2,1)S(1)} %pad_maximum_fusion), channel_id=1, source_target_pairs={{0,2},{1,5},{2,0},{3,7},{4,6},{5,1},{6,4},{7,3},{8,10},{9,13},{10,... | collective-permute-start | bytes 1572872 | tf_op jit(solution)/shard_map/ppermute | solution.py:127
  45.0 2.4 %collective-permute-done.8 = bf16[64,2048]{1,0:T(8,128)(2,1)S(1)} collective-permute-done((bf16[64,2048]{1,0:T(8,128)(2,1)S(1)}, bf16[64,2048]{1,0:T(8,128)(2,1)S(1)}, u32[]{:S(2)}, u32[]{:S(2)}) %collective-permute-start.8) | collective-permute-done | bytes 262176 | tf_op jit(solution)/shard_map/ppermute | solution.py:54
  47.5 4.7 %collective-permute-start.9 = (bf16[64,1024]{1,0:T(8,128)(2,1)S(1)}, bf16[64,1024]{1,0:T(8,128)(2,1)S(1)}, u32[]{:S(2)}, u32[]{:S(2)}) collective-permute-start(bf16[64,1024]{1,0:T(8,128)(2,1)S(1)} %get-tuple-element.147), channel_id=1, source_target_pairs={{0,0},{1,4},{2,2},{3,6},{5,5},{4,1},{7,7},{6,3},{8,8},{9,12},{10,1... | collective-permute-start | bytes 393224 | tf_op jit(solution)/shard_map/ppermute | solution.py:137
  52.3 1.3 %convolution_convert_fusion.1 = bf16[256,2048]{1,0:T(8,128)(2,1)S(1)} fusion(bf16[64,1024]{1,0:T(8,128)(2,1)S(1)} %get-tuple-element.66, bf16[64,1024]{1,0:T(8,128)(2,1)S(1)} %get-tuple-element.139, bf16[64,1024]{1,0:T(8,128)(2,1)S(1)} %get-tuple-element.138, bf16[64,1024]{1,0:T(8,128)(2,1)S(1)} %get-tuple-element.63, bf16[1,1024,2048]{2,1,0:T(8,128)(2,1)S(1)} %copy-done.5), kind=kOutput, calls=%fused_computation.1 | convolution fusion | flops 1076363264 | bytes 5767168 | tf_op jit(solution)/shard_map/dot_general | solution.py:222
  53.7 1.5 %collective-permute-start.10 = (bf16[64,1024]{1,0:T(8,128)(2,1)S(1)}, bf16[64,1024]{1,0:T(8,128)(2,1)S(1)}, u32[]{:S(2)}, u32[]{:S(2)}) collective-permute-start(bf16[64,1024]{1,0:T(8,128)(2,1)S(1)} %get-tuple-element.146), channel_id=1, source_target_pairs={{0,2},{1,6},{2,0},{3,4},{5,7},{4,3},{7,5},{6,1},{8,10},{9,14},{10,... | collective-permute-start | bytes 393224 | tf_op jit(solution)/shard_map/ppermute | solution.py:137
  55.2 1.3 %convolution_convert_fusion.5 = bf16[256,1024]{1,0:T(8,128)(2,1)S(1)} fusion(bf16[128,2048]{1,0:T(8,128)(2,1)S(1)} %collective-permute-done.13, bf16[128,2048]{1,0:T(8,128)(2,1)S(1)} %pad_maximum_fusion, bf16[1,1024,2048]{2,1,0:T(8,128)(2,1)S(1)} %copy-done.5), kind=kOutput, calls=%fused_computation.5 | convolution fusion | flops 1076101120 | bytes 5767168 | tf_op jit(solution)/shard_map/dot_general | solution.py:250
  56.6 2.2 %all-gather.2 = bf16[256,1024]{1,0:T(8,128)(2,1)S(1)} all-gather(bf16[128,1024]{1,0:T(8,128)(2,1)S(1)} %get-tuple-element.71), channel_id=4, replica_groups=mesh['segment'=4,'row'=4,'col'=2] {'col'}, dimensions={0}, use_global_device_ids=true | all-gather | bytes 786432 | tf_op jit(solution)/shard_map/all_gather | solution.py:260
  59.0 1.3 %collective-permute-start.18 = (bf16[64,1024]{1,0:T(8,128)(2,1)S(1)}, bf16[64,1024]{1,0:T(8,128)(2,1)S(1)}, u32[]{:S(2)}, u32[]{:S(2)}) collective-permute-start(bf16[64,1024]{1,0:T(8,128)(2,1)S(1)} %get-tuple-element.90), channel_id=1, source_target_pairs={{8,0},{9,4},{10,2},{11,6},{13,5},{12,1},{15,7},{14,3},{16,8},{17,1... | collective-permute-start | bytes 393224 | tf_op jit(solution)/shard_map/ppermute | solution.py:145
  60.3 1.3 %collective-permute-start.17 = (bf16[64,1024]{1,0:T(8,128)(2,1)S(1)}, bf16[64,1024]{1,0:T(8,128)(2,1)S(1)}, u32[]{:S(2)}, u32[]{:S(2)}) collective-permute-start(bf16[64,1024]{1,0:T(8,128)(2,1)S(1)} %get-tuple-element.89), channel_id=1, source_target_pairs={{8,2},{9,6},{10,0},{11,4},{13,7},{12,3},{15,5},{14,1},{16,10},{17,... | collective-permute-start | bytes 393224 | tf_op jit(solution)/shard_map/ppermute | solution.py:145
  62.8 5.8 %collective-permute-done.18 = bf16[64,1024]{1,0:T(8,128)(2,1)S(1)} collective-permute-done((bf16[64,1024]{1,0:T(8,128)(2,1)S(1)}, bf16[64,1024]{1,0:T(8,128)(2,1)S(1)}, u32[]{:S(2)}, u32[]{:S(2)}) %collective-permute-start.18) | collective-permute-done | bytes 131104 | tf_op jit(solution)/shard_map/ppermute | solution.py:145
  68.5 2.5 %collective-permute-done.17 = bf16[64,1024]{1,0:T(8,128)(2,1)S(1)} collective-permute-done((bf16[64,1024]{1,0:T(8,128)(2,1)S(1)}, bf16[64,1024]{1,0:T(8,128)(2,1)S(1)}, u32[]{:S(2)}, u32[]{:S(2)}) %collective-permute-start.17) | collective-permute-done | bytes 131104 | tf_op jit(solution)/shard_map/ppermute | solution.py:145
  71.4 0.9 collective-permute-start.21
  72.3 1.0 collective-permute-start.23
  73.6 1.3 %convolution_convert_fusion = bf16[256,2048]{1,0:T(8,128)(2,1)S(1)} fusion(bf16[64,1024]{1,0:T(8,128)(2,1)S(1)} %get-tuple-element.79, bf16[64,1024]{1,0:T(8,128)(2,1)S(1)} %get-tuple-element.129, bf16[64,1024]{1,0:T(8,128)(2,1)S(1)} %get-tuple-element.128, bf16[64,1024]{1,0:T(8,128)(2,1)S(1)} %get-tuple-element.76, bf16[1,1024,2048]{2,1,0:T(8,128)(2,1)S(1)} %copy-done.5), kind=kOutput, calls=%fused_computation | convolution fusion | flops 1076363264 | bytes 5767168 | tf_op jit(solution)/shard_map/dot_general | solution.py:222
  74.9 1.0 collective-permute-start.22
  76.0 1.7 %collective-permute-start.27 = (bf16[64,1024]{1,0:T(8,128)(2,1)S(1)}, bf16[64,1024]{1,0:T(8,128)(2,1)S(1)}, u32[]{:S(2)}, u32[]{:S(2)}) collective-permute-start(bf16[64,1024]{1,0:T(8,128)(2,1)S(1)} %get-tuple-element.89), channel_id=1, source_target_pairs={{0,2},{1,6},{2,0},{3,4},{5,7},{4,3},{7,5},{6,1},{8,10},{9,14},{10,... | collective-permute-start | bytes 393224 | tf_op jit(solution)/shard_map/ppermute | solution.py:137
  77.7 2.3 %collective-permute-start.28 = (bf16[64,1024]{1,0:T(8,128)(2,1)S(1)}, bf16[64,1024]{1,0:T(8,128)(2,1)S(1)}, u32[]{:S(2)}, u32[]{:S(2)}) collective-permute-start(bf16[64,1024]{1,0:T(8,128)(2,1)S(1)} %get-tuple-element.90), channel_id=1, source_target_pairs={{0,0},{1,4},{2,2},{3,6},{5,5},{4,1},{7,7},{6,3},{8,8},{9,12},{10,1... | collective-permute-start | bytes 393224 | tf_op jit(solution)/shard_map/ppermute | solution.py:137
  80.1 1.0 collective-permute-start.25
  81.1 11.7 %collective-permute-done.27 = bf16[64,1024]{1,0:T(8,128)(2,1)S(1)} collective-permute-done((bf16[64,1024]{1,0:T(8,128)(2,1)S(1)}, bf16[64,1024]{1,0:T(8,128)(2,1)S(1)}, u32[]{:S(2)}, u32[]{:S(2)}) %collective-permute-start.27) | collective-permute-done | bytes 131104 | tf_op jit(solution)/shard_map/ppermute | solution.py:137
  93.0 1.3 %convolution_convert_fusion.4 = bf16[256,1024]{1,0:T(8,128)(2,1)S(1)} fusion(bf16[128,2048]{1,0:T(8,128)(2,1)S(1)} %collective-permute-done.25, bf16[128,2048]{1,0:T(8,128)(2,1)S(1)} %pad_maximum_fusion.1, bf16[1,1024,2048]{2,1,0:T(8,128)(2,1)S(1)} %copy-done.5), kind=kOutput, calls=%fused_computation.4 | convolution fusion | flops 1076101120 | bytes 5767168 | tf_op jit(solution)/shard_map/dot_general | solution.py:250
  95.2 0.9 collective-permute-done.26
  96.2 1.1 %collective-permute-start.29 = (bf16[64,1024]{1,0:T(8,128)(2,1)S(1)}, bf16[64,1024]{1,0:T(8,128)(2,1)S(1)}, u32[]{:S(2)}, u32[]{:S(2)}) collective-permute-start(bf16[64,1024]{1,0:T(8,128)(2,1)S(1)} %get-tuple-element.126), channel_id=1, source_target_pairs={{0,2},{1,6},{2,0},{3,4},{5,7},{4,3},{7,5},{6,1},{8,10},{9,14},{10,... | collective-permute-start | bytes 393224 | tf_op jit(solution)/shard_map/ppermute | solution.py:137
  97.2 2.9 %collective-permute-start.30 = (bf16[64,1024]{1,0:T(8,128)(2,1)S(1)}, bf16[64,1024]{1,0:T(8,128)(2,1)S(1)}, u32[]{:S(2)}, u32[]{:S(2)}) collective-permute-start(bf16[64,1024]{1,0:T(8,128)(2,1)S(1)} %get-tuple-element.127), channel_id=1, source_target_pairs={{0,0},{1,4},{2,2},{3,6},{5,5},{4,1},{7,7},{6,3},{8,8},{9,12},{10,1... | collective-permute-start | bytes 393224 | tf_op jit(solution)/shard_map/ppermute | solution.py:137
  100.2 0.7 collective-permute-done.24
  101.0 0.8 maximum_bitcast_fusion
  101.9 0.9 collective-permute-done.29
  102.7 1.2 %collective-permute-done.30 = bf16[64,1024]{1,0:T(8,128)(2,1)S(1)} collective-permute-done((bf16[64,1024]{1,0:T(8,128)(2,1)S(1)}, bf16[64,1024]{1,0:T(8,128)(2,1)S(1)}, u32[]{:S(2)}, u32[]{:S(2)}) %collective-permute-start.30) | collective-permute-done | bytes 131104 | tf_op jit(solution)/shard_map/ppermute | solution.py:137
  104.1 0.8 maximum_bitcast_fusion.1
  (91 shorter events, 6.7 us)
Async XLA Ops:
  1.7 10.3 %collective-permute-start.1 = (bf16[64,1024]{1,0:T(8,128)(2,1)S(1)}, bf16[64,1024]{1,0:T(8,128)(2,1)S(1)}, u32[]{:S(2)}, u32[]{:S(2)}) collective-permute-start(bf16[64,1024]{1,0:T(8,128)(2,1)S(1)} %get-tuple-element.153), channel_id=1, source_target_pairs={{0,0},{1,4},{2,2},{3,6},{5,5},{4,1},{7,7},{6,3},{8,8},{9,12},{10,1... | collective-permute-start | bytes 393224 | tf_op jit(solution)/shard_map/ppermute | solution.py:137
  6.3 6.1 %collective-permute-start.2 = (bf16[64,1024]{1,0:T(8,128)(2,1)S(1)}, bf16[64,1024]{1,0:T(8,128)(2,1)S(1)}, u32[]{:S(2)}, u32[]{:S(2)}) collective-permute-start(bf16[64,1024]{1,0:T(8,128)(2,1)S(1)} %get-tuple-element.152), channel_id=1, source_target_pairs={{0,2},{1,6},{2,0},{3,4},{5,7},{4,3},{7,5},{6,1},{8,10},{9,14},{10,... | collective-permute-start | bytes 393224 | tf_op jit(solution)/shard_map/ppermute | solution.py:137
  8.3 8.0 %collective-permute-start = (bf16[64,1024]{1,0:T(8,128)(2,1)S(1)}, bf16[64,1024]{1,0:T(8,128)(2,1)S(1)}, u32[]{:S(2)}, u32[]{:S(2)}) collective-permute-start(bf16[64,1024]{1,0:T(8,128)(2,1)S(1)} %get-tuple-element.154), channel_id=1, source_target_pairs={{0,0},{1,4},{2,2},{3,6},{5,5},{4,1},{7,7},{6,3},{8,8},{9,12},{10,1... | collective-permute-start | bytes 393224 | tf_op jit(solution)/shard_map/ppermute | solution.py:137
  11.9 5.4 %collective-permute-start.3 = (bf16[64,1024]{1,0:T(8,128)(2,1)S(1)}, bf16[64,1024]{1,0:T(8,128)(2,1)S(1)}, u32[]{:S(2)}, u32[]{:S(2)}) collective-permute-start(bf16[64,1024]{1,0:T(8,128)(2,1)S(1)} %get-tuple-element.155), channel_id=1, source_target_pairs={{0,2},{1,6},{2,0},{3,4},{5,7},{4,3},{7,5},{6,1},{8,10},{9,14},{10,... | collective-permute-start | bytes 393224 | tf_op jit(solution)/shard_map/ppermute | solution.py:137
  12.1 2.9 %copy-start.5 = (bf16[1,1024,2048]{2,1,0:T(8,128)(2,1)S(1)}, bf16[1,1024,2048]{2,1,0:T(8,128)(2,1)}, u32[]{:S(2)}) copy-start(bf16[1,1024,2048]{2,1,0:T(8,128)(2,1)} %param.7) | copy-start | bytes 12582916
  16.3 9.8 %collective-permute-start.6 = (bf16[128,2048]{1,0:T(8,128)(2,1)S(1)}, bf16[128,2048]{1,0:T(8,128)(2,1)S(1)}, u32[]{:S(2)}, u32[]{:S(2)}) collective-permute-start(bf16[128,2048]{1,0:T(8,128)(2,1)S(1)} %split.238), channel_id=1, source_target_pairs={{0,4},{1,3},{2,6},{3,1},{4,0},{5,7},{6,2},{7,5},{8,12},{9,11},{10,... | collective-permute-start | bytes 1572872 | tf_op jit(solution)/shard_map/ppermute | solution.py:127
  21.3 12.6 %copy-start = (bf16[1,64,2048]{2,1,0:T(8,128)(2,1)S(1)}, bf16[1,64,2048]{2,1,0:T(8,128)(2,1)}, u32[]{:S(2)}) copy-start(bf16[1,64,2048]{2,1,0:T(8,128)(2,1)} %param.11) | copy-start | bytes 786436
  21.3 15.8 %copy-start.4 = (f32[1,2048]{1,0:T(1,128)S(1)}, f32[1,2048]{1,0:T(1,128)}, u32[]{:S(2)}) copy-start(f32[1,2048]{1,0:T(1,128)} %param.8) | copy-start | bytes 24580
  21.3 17.7 %copy-start.1 = (bf16[1,64,2048]{2,1,0:T(8,128)(2,1)S(1)}, bf16[1,64,2048]{2,1,0:T(8,128)(2,1)}, u32[]{:S(2)}) copy-start(bf16[1,64,2048]{2,1,0:T(8,128)(2,1)} %param.9) | copy-start | bytes 786436
  21.4 10.9 %collective-permute-start.4 = (bf16[128,2048]{1,0:T(8,128)(2,1)S(1)}, bf16[128,2048]{1,0:T(8,128)(2,1)S(1)}, u32[]{:S(2)}, u32[]{:S(2)}) collective-permute-start(bf16[128,2048]{1,0:T(8,128)(2,1)S(1)} %split.244), channel_id=1, source_target_pairs={{0,2},{1,5},{2,0},{3,7},{4,6},{5,1},{6,4},{7,3},{8,10},{9,13},{10,... | collective-permute-start | bytes 1572872 | tf_op jit(solution)/shard_map/ppermute | solution.py:127
  22.3 11.0 %collective-permute-start.14 = (bf16[64,1024]{1,0:T(8,128)(2,1)S(1)}, bf16[64,1024]{1,0:T(8,128)(2,1)S(1)}, u32[]{:S(2)}, u32[]{:S(2)}) collective-permute-start(bf16[64,1024]{1,0:T(8,128)(2,1)S(1)} %get-tuple-element.144), channel_id=1, source_target_pairs={{0,0},{1,4},{2,2},{3,6},{5,5},{4,1},{7,7},{6,3},{8,8},{9,12},{10,1... | collective-permute-start | bytes 393224 | tf_op jit(solution)/shard_map/ppermute | solution.py:137
  24.8 8.8 %collective-permute-start.15 = (bf16[64,1024]{1,0:T(8,128)(2,1)S(1)}, bf16[64,1024]{1,0:T(8,128)(2,1)S(1)}, u32[]{:S(2)}, u32[]{:S(2)}) collective-permute-start(bf16[64,1024]{1,0:T(8,128)(2,1)S(1)} %get-tuple-element.145), channel_id=1, source_target_pairs={{0,2},{1,6},{2,0},{3,4},{5,7},{4,3},{7,5},{6,1},{8,10},{9,14},{10,... | collective-permute-start | bytes 393224 | tf_op jit(solution)/shard_map/ppermute | solution.py:137
  26.3 10.8 %collective-permute-start.7 = (bf16[64,2048]{1,0:T(8,128)(2,1)S(1)}, bf16[64,2048]{1,0:T(8,128)(2,1)S(1)}, u32[]{:S(2)}, u32[]{:S(2)}) collective-permute-start(bf16[64,2048]{1,0:T(8,128)(2,1)S(1)} %split.334), channel_id=1, source_target_pairs={{0,2},{1,5},{2,0},{3,7},{4,6},{5,1},{6,4},{7,3},{8,10},{9,13},{10,... | collective-permute-start | bytes 786440 | tf_op jit(solution)/shard_map/ppermute | solution.py:127
  32.4 15.0 %copy-start.3 = (bf16[64,2048]{1,0:T(8,128)(2,1)S(1)}, bf16[64,2048]{1,0:T(8,128)(2,1)}, u32[]{:S(2)}) copy-start(bf16[64,2048]{1,0:T(8,128)(2,1)} %param.10) | copy-start | bytes 786436
  32.5 6.6 %collective-permute-start.5 = (bf16[64,2048]{1,0:T(8,128)(2,1)S(1)}, bf16[64,2048]{1,0:T(8,128)(2,1)S(1)}, u32[]{:S(2)}, u32[]{:S(2)}) collective-permute-start(bf16[64,2048]{1,0:T(8,128)(2,1)S(1)} %split.335), channel_id=1, source_target_pairs={{0,4},{1,3},{2,6},{3,1},{4,0},{5,7},{6,2},{7,5},{8,12},{9,11},{10,... | collective-permute-start | bytes 786440 | tf_op jit(solution)/shard_map/ppermute | solution.py:127
  33.7 5.6 %collective-permute-start.16 = (bf16[128,1024]{1,0:T(8,128)(2,1)S(1)}, bf16[128,1024]{1,0:T(8,128)(2,1)S(1)}, u32[]{:S(2)}, u32[]{:S(2)}) collective-permute-start(bf16[128,1024]{1,0:T(8,128)(2,1)S(1)} %pad_maximum_fusion.4), channel_id=1, source_target_pairs={{0,1},{1,0},{2,3},{3,2},{4,5},{5,4},{6,7},{7,6},{8,9},{9,8},{10,11... | collective-permute-start | bytes 786440 | tf_op jit(solution)/shard_map/ppermute | solution.py:79
  33.9 37.1 %collective-permute-start.11 = (bf16[64,2048]{1,0:T(8,128)(2,1)S(1)}, bf16[64,2048]{1,0:T(8,128)(2,1)S(1)}, u32[]{:S(2)}, u32[]{:S(2)}) collective-permute-start(bf16[64,2048]{1,0:T(8,128)(2,1)S(1)} %bitcast.44), channel_id=1, source_target_pairs={{8,0},{16,8},{24,16},{9,1},{17,9},{25,17},{10,2},{18,10},{26,18},{... | collective-permute-start | bytes 786440 | tf_op jit(solution)/shard_map/ppermute | solution.py:54
  37.3 5.6 %collective-permute-start.12 = (bf16[64,2048]{1,0:T(8,128)(2,1)S(1)}, bf16[64,2048]{1,0:T(8,128)(2,1)S(1)}, u32[]{:S(2)}, u32[]{:S(2)}) collective-permute-start(bf16[64,2048]{1,0:T(8,128)(2,1)S(1)} %fusion.7), channel_id=1, source_target_pairs={{0,4},{1,3},{2,6},{3,1},{4,0},{5,7},{6,2},{7,5},{8,12},{9,11},{10,... | collective-permute-start | bytes 786440 | tf_op jit(solution)/shard_map/ppermute | solution.py:127
  39.3 8.2 %collective-permute-start.8 = (bf16[64,2048]{1,0:T(8,128)(2,1)S(1)}, bf16[64,2048]{1,0:T(8,128)(2,1)S(1)}, u32[]{:S(2)}, u32[]{:S(2)}) collective-permute-start(bf16[64,2048]{1,0:T(8,128)(2,1)S(1)} %add_convert_fusion.3), channel_id=1, source_target_pairs={{0,8},{8,16},{16,24},{1,9},{9,17},{17,25},{2,10},{10,18},{18,26},{... | collective-permute-start | bytes 786440 | tf_op jit(solution)/shard_map/ppermute | solution.py:54
  43.0 12.2 %collective-permute-start.13 = (bf16[128,2048]{1,0:T(8,128)(2,1)S(1)}, bf16[128,2048]{1,0:T(8,128)(2,1)S(1)}, u32[]{:S(2)}, u32[]{:S(2)}) collective-permute-start(bf16[128,2048]{1,0:T(8,128)(2,1)S(1)} %pad_maximum_fusion), channel_id=1, source_target_pairs={{0,2},{1,5},{2,0},{3,7},{4,6},{5,1},{6,4},{7,3},{8,10},{9,13},{10,... | collective-permute-start | bytes 1572872 | tf_op jit(solution)/shard_map/ppermute | solution.py:127
  47.5 7.7 %collective-permute-start.9 = (bf16[64,1024]{1,0:T(8,128)(2,1)S(1)}, bf16[64,1024]{1,0:T(8,128)(2,1)S(1)}, u32[]{:S(2)}, u32[]{:S(2)}) collective-permute-start(bf16[64,1024]{1,0:T(8,128)(2,1)S(1)} %get-tuple-element.147), channel_id=1, source_target_pairs={{0,0},{1,4},{2,2},{3,6},{5,5},{4,1},{7,7},{6,3},{8,8},{9,12},{10,1... | collective-permute-start | bytes 393224 | tf_op jit(solution)/shard_map/ppermute | solution.py:137
  53.6 8.4 %collective-permute-start.19 = (bf16[128,2048]{1,0:T(8,128)(2,1)S(1)}, bf16[128,2048]{1,0:T(8,128)(2,1)S(1)}, u32[]{:S(2)}, u32[]{:S(2)}) collective-permute-start(bf16[128,2048]{1,0:T(8,128)(2,1)S(1)} %split.261), channel_id=1, source_target_pairs={{0,2},{1,5},{2,0},{3,7},{4,6},{5,1},{6,4},{7,3},{8,10},{9,13},{10,... | collective-permute-start | bytes 1572872 | tf_op jit(solution)/shard_map/ppermute | solution.py:127
  53.7 17.7 %collective-permute-start.10 = (bf16[64,1024]{1,0:T(8,128)(2,1)S(1)}, bf16[64,1024]{1,0:T(8,128)(2,1)S(1)}, u32[]{:S(2)}, u32[]{:S(2)}) collective-permute-start(bf16[64,1024]{1,0:T(8,128)(2,1)S(1)} %get-tuple-element.146), channel_id=1, source_target_pairs={{0,2},{1,6},{2,0},{3,4},{5,7},{4,3},{7,5},{6,1},{8,10},{9,14},{10,... | collective-permute-start | bytes 393224 | tf_op jit(solution)/shard_map/ppermute | solution.py:137
  56.5 14.6 %copy-start.2 = (bf16[64,2048]{1,0:T(8,128)(2,1)S(1)}, bf16[64,2048]{1,0:T(8,128)(2,1)}, u32[]{:S(2)}) copy-start(bf16[64,2048]{1,0:T(8,128)(2,1)} %param.12) | copy-start | bytes 786436
  59.0 9.5 %collective-permute-start.18 = (bf16[64,1024]{1,0:T(8,128)(2,1)S(1)}, bf16[64,1024]{1,0:T(8,128)(2,1)S(1)}, u32[]{:S(2)}, u32[]{:S(2)}) collective-permute-start(bf16[64,1024]{1,0:T(8,128)(2,1)S(1)} %get-tuple-element.90), channel_id=1, source_target_pairs={{8,0},{9,4},{10,2},{11,6},{13,5},{12,1},{15,7},{14,3},{16,8},{17,1... | collective-permute-start | bytes 393224 | tf_op jit(solution)/shard_map/ppermute | solution.py:145
  60.3 10.7 %collective-permute-start.17 = (bf16[64,1024]{1,0:T(8,128)(2,1)S(1)}, bf16[64,1024]{1,0:T(8,128)(2,1)S(1)}, u32[]{:S(2)}, u32[]{:S(2)}) collective-permute-start(bf16[64,1024]{1,0:T(8,128)(2,1)S(1)} %get-tuple-element.89), channel_id=1, source_target_pairs={{8,2},{9,6},{10,0},{11,4},{13,7},{12,3},{15,5},{14,1},{16,10},{17,... | collective-permute-start | bytes 393224 | tf_op jit(solution)/shard_map/ppermute | solution.py:145
  62.2 8.9 %collective-permute-start.20 = (bf16[64,2048]{1,0:T(8,128)(2,1)S(1)}, bf16[64,2048]{1,0:T(8,128)(2,1)S(1)}, u32[]{:S(2)}, u32[]{:S(2)}) collective-permute-start(bf16[64,2048]{1,0:T(8,128)(2,1)S(1)} %split.333), channel_id=1, source_target_pairs={{0,4},{1,3},{2,6},{3,1},{4,0},{5,7},{6,2},{7,5},{8,12},{9,11},{10,... | collective-permute-start | bytes 786440 | tf_op jit(solution)/shard_map/ppermute | solution.py:127
  71.4 2.1 %collective-permute-start.21 = (bf16[128,1024]{1,0:T(8,128)(2,1)S(1)}, bf16[128,1024]{1,0:T(8,128)(2,1)S(1)}, u32[]{:S(2)}, u32[]{:S(2)}) collective-permute-start(bf16[128,1024]{1,0:T(8,128)(2,1)S(1)} %constant_dynamic-update-slice_fusion), channel_id=1, source_target_pairs={{0,1},{1,0},{2,3},{3,2},{4,5},{5,4},{6,7},{7,6},{8,9},{9,8},{10,11... | collective-permute-start | bytes 786440 | tf_op jit(solution)/shard_map/ppermute | solution.py:79
  72.3 7.7 %collective-permute-start.23 = (bf16[64,2048]{1,0:T(8,128)(2,1)S(1)}, bf16[64,2048]{1,0:T(8,128)(2,1)S(1)}, u32[]{:S(2)}, u32[]{:S(2)}) collective-permute-start(bf16[64,2048]{1,0:T(8,128)(2,1)S(1)} %get-tuple-element.92), channel_id=1, source_target_pairs={{0,2},{1,5},{2,0},{3,7},{4,6},{5,1},{6,4},{7,3},{8,10},{9,13},{10,... | collective-permute-start | bytes 786440 | tf_op jit(solution)/shard_map/ppermute | solution.py:127
  74.9 17.9 %collective-permute-start.22 = (bf16[128,2048]{1,0:T(8,128)(2,1)S(1)}, bf16[128,2048]{1,0:T(8,128)(2,1)S(1)}, u32[]{:S(2)}, u32[]{:S(2)}) collective-permute-start(bf16[128,2048]{1,0:T(8,128)(2,1)S(1)} %split.269), channel_id=1, source_target_pairs={{0,2},{1,5},{2,0},{3,7},{4,6},{5,1},{6,4},{7,3},{8,10},{9,13},{10,... | collective-permute-start | bytes 1572872 | tf_op jit(solution)/shard_map/ppermute | solution.py:127
  76.0 16.8 %collective-permute-start.27 = (bf16[64,1024]{1,0:T(8,128)(2,1)S(1)}, bf16[64,1024]{1,0:T(8,128)(2,1)S(1)}, u32[]{:S(2)}, u32[]{:S(2)}) collective-permute-start(bf16[64,1024]{1,0:T(8,128)(2,1)S(1)} %get-tuple-element.89), channel_id=1, source_target_pairs={{0,2},{1,6},{2,0},{3,4},{5,7},{4,3},{7,5},{6,1},{8,10},{9,14},{10,... | collective-permute-start | bytes 393224 | tf_op jit(solution)/shard_map/ppermute | solution.py:137
  77.7 15.1 %collective-permute-start.28 = (bf16[64,1024]{1,0:T(8,128)(2,1)S(1)}, bf16[64,1024]{1,0:T(8,128)(2,1)S(1)}, u32[]{:S(2)}, u32[]{:S(2)}) collective-permute-start(bf16[64,1024]{1,0:T(8,128)(2,1)S(1)} %get-tuple-element.90), channel_id=1, source_target_pairs={{0,0},{1,4},{2,2},{3,6},{5,5},{4,1},{7,7},{6,3},{8,8},{9,12},{10,1... | collective-permute-start | bytes 393224 | tf_op jit(solution)/shard_map/ppermute | solution.py:137
  80.1 12.9 %collective-permute-start.25 = (bf16[128,2048]{1,0:T(8,128)(2,1)S(1)}, bf16[128,2048]{1,0:T(8,128)(2,1)S(1)}, u32[]{:S(2)}, u32[]{:S(2)}) collective-permute-start(bf16[128,2048]{1,0:T(8,128)(2,1)S(1)} %pad_maximum_fusion.1), channel_id=1, source_target_pairs={{0,4},{1,3},{2,6},{3,1},{4,0},{5,7},{6,2},{7,5},{8,12},{9,11},{10,... | collective-permute-start | bytes 1572872 | tf_op jit(solution)/shard_map/ppermute | solution.py:127
  94.5 1.6 %collective-permute-start.26 = (bf16[128,1024]{1,0:T(8,128)(2,1)S(1)}, bf16[128,1024]{1,0:T(8,128)(2,1)S(1)}, u32[]{:S(2)}, u32[]{:S(2)}) collective-permute-start(bf16[128,1024]{1,0:T(8,128)(2,1)S(1)} %get-tuple-element.86), channel_id=1, source_target_pairs={{0,1},{1,0},{2,3},{3,2},{4,5},{5,4},{6,7},{7,6},{8,9},{9,8},{10,11... | collective-permute-start | bytes 786440 | tf_op jit(solution)/shard_map/ppermute | solution.py:79
  94.6 6.2 %collective-permute-start.24 = (bf16[64,2048]{1,0:T(8,128)(2,1)S(1)}, bf16[64,2048]{1,0:T(8,128)(2,1)S(1)}, u32[]{:S(2)}, u32[]{:S(2)}) collective-permute-start(bf16[64,2048]{1,0:T(8,128)(2,1)S(1)} %split.332), channel_id=1, source_target_pairs={{0,4},{1,3},{2,6},{3,1},{4,0},{5,7},{6,2},{7,5},{8,12},{9,11},{10,... | collective-permute-start | bytes 786440 | tf_op jit(solution)/shard_map/ppermute | solution.py:127
  96.2 6.6 %collective-permute-start.29 = (bf16[64,1024]{1,0:T(8,128)(2,1)S(1)}, bf16[64,1024]{1,0:T(8,128)(2,1)S(1)}, u32[]{:S(2)}, u32[]{:S(2)}) collective-permute-start(bf16[64,1024]{1,0:T(8,128)(2,1)S(1)} %get-tuple-element.126), channel_id=1, source_target_pairs={{0,2},{1,6},{2,0},{3,4},{5,7},{4,3},{7,5},{6,1},{8,10},{9,14},{10,... | collective-permute-start | bytes 393224 | tf_op jit(solution)/shard_map/ppermute | solution.py:137
  97.2 6.7 %collective-permute-start.30 = (bf16[64,1024]{1,0:T(8,128)(2,1)S(1)}, bf16[64,1024]{1,0:T(8,128)(2,1)S(1)}, u32[]{:S(2)}, u32[]{:S(2)}) collective-permute-start(bf16[64,1024]{1,0:T(8,128)(2,1)S(1)} %get-tuple-element.127), channel_id=1, source_target_pairs={{0,0},{1,4},{2,2},{3,6},{5,5},{4,1},{7,7},{6,3},{8,8},{9,12},{10,1... | collective-permute-start | bytes 393224 | tf_op jit(solution)/shard_map/ppermute | solution.py:137

commit v5 on v4

--- a/solution.py
+++ b/solution.py
@@ -6,14 +6,14 @@
 F32 = jnp.float32
 BF16 = jnp.bfloat16
 
-TURNED = ("B0", "G1")
+TURNED = ("B0", "G0")
 AT_ONCE = ("A0", "A1", "G0")
 GATES = {
     "A0_o": ("weight",),
     "A1_a0": ("A0_x",),
     "A1_in": ("A0_m0",),
     "A1_s": ("B0_m0",),
-    "A2_a0": ("B0_m1",),
+    "A2_a0": ("A1_a1", "B0_m1"),
     "A2_in": ("B0_m0",),
     "A2_o": ("A2_a0",),
     "A2_s": ("B0_m1",),
@@ -27,6 +27,7 @@
     "B1_x": ("out1",),
     "D0_a0": ("feed",),
     "F1_a1": ("sc1",),
+    "F1_m0": ("weight",),
     "F2_a0": ("G1_m1",),
     "F2_a1": ("G1_s",),
     "F2_x": ("A3_o",),
@@ -36,10 +37,11 @@
     "G1_a0": ("F2_t0",),
     "G1_a1": ("F2_m1",),
     "G1_h": ("G1_m1",),
-    "W0_m": ("G0_m1",),
-    "gr1": ("F2_t0",),
+    "G1_o": ("zt_a",),
     "out2": ("G1_m1",),
+    "zr_a": ("F1_m1",),
     "zr_m": ("B0_m1",),
+    "zt_m": ("F2_m1",),
 }
 
 
@@ -126,20 +128,20 @@
                 pairs.append((row * self.cols + col, other * self.cols + col))
         return lax.ppermute(value, ("row", "col"), pairs)
 
-    def across(self, value, shift, onward=0):
+    def across(self, value, shift, onward=0, only=None):
         pairs = []
         for row in range(self.rows):
             home = row // self.per_col
             for j in range(self.cols):
                 other = row ^ (j * self.per_col + shift)
                 pairs.append((row * self.cols + (home ^ j), other * self.cols + home))
-        if not onward:
+        if not onward and only is None:
             return lax.ppermute(value, ("row", "col"), pairs)
         sections, size = lax.axis_size("segment"), self.rows * self.cols
         pairs = [
             (at * size + source, (at + onward) * size + target)
             for at in range(sections)
-            if 0 <= at + onward < sections
+            if 0 <= at + onward < sections and only in (None, at)
             for source, target in pairs
         ]
         return lax.ppermute(value, ("segment", "row", "col"), pairs)
@@ -278,12 +280,12 @@
         rule(f"{name}_o", others)
         rule(f"{name}_s", total)
 
-    def deliver(name, source, onward=0):
+    def deliver(name, source, onward=0, only=None):
         rule(f"{name}_m", lambda: cut(flow(source), plane.per_col))
         for shift in shifts:
             rule(
                 f"{name}_a{shift}",
-                lambda shift=shift: plane.across(flow(f"{name}_m")[shift], shift, onward),
+                lambda shift=shift: plane.across(flow(f"{name}_m")[shift], shift, onward, only),
             )
         return lambda: plane.in_columns([flow(f"{name}_a{shift}") for shift in shifts])
 
@@ -296,8 +298,6 @@
     rule("sc1", lambda: scale(returning[0], first_back()))
     rule("out1", lambda: advance(incoming[0], first_pre()))
     back("G0", "sc1")
-    own_back = deliver("W0", "G0_s")
-    rule("gr1", lambda: retreat(returning[0], own_back()))
 
     rule("zf_a", lambda: passed_along(flow("out1"), 1))
     rule("feed", lambda: jnp.where(segment_index == 0, fresh_batch, flow("zf_a")))
@@ -305,6 +305,11 @@
     rule("zr_a", lambda: passed_along(flow("zr_m"), -1))
     next_back = deliver("D0", "G0_s", -1)
     rule("ag", lambda: retreat(flow("zr_a"), next_back()))
+    own_back = deliver("W0", "G0_s", 0, 0)
+    rule("zt_m", lambda: flow("ag"))
+    rule("zt_a", lambda: passed_along(flow("zt_m"), 1))
+    rule("gw", lambda: fixed(retreat(returning[0], own_back())))
+    rule("gr1", lambda: jnp.where(segment_index == 0, flow("gw"), flow("zt_a")))
     rule("up", lambda: jnp.where(segment_index == segment_count - 1, fresh_cotangent, flow("ag")))
 
     spread("A3", lambda: flow("feed"))

time: 106 us -> 105 us (level)
  waiting for transfers between devices: 36.5 us -> 32.2 us
  starting transfers between devices: 45.5 us -> 49.5 us
    ppermute x12 -> x10, waiting for transfers between devices: 14.8 us -> 3.58 us  [across(): return lax.ppermute(value, ('row', 'col'), pairs)]
    ppermute x2 -> x4, starting transfers between devices: 2.58 us -> 9.01 us  [across(): return lax.ppermute(value, ('segment', 'row', 'col'), pairs)]
    ppermute x2 -> x4, waiting for transfers between devices: 8.24 us -> 13.5 us  [across(): return lax.ppermute(value, ('segment', 'row', 'col'), pairs)]
    ppermute x12 -> x10, starting transfers between devices: 27.2 us -> 22.5 us  [across(): return lax.ppermute(value, ('row', 'col'), pairs)]
    ppermute x12, starting transfers between devices: 9.96 us -> 11.4 us  [step_swap(): return lax.ppermute(value, ('row', 'col'), pairs)]
    ppermute x12, waiting for transfers between devices: 10 us -> 11.5 us  [step_swap(): return lax.ppermute(value, ('row', 'col'), pairs)]
    ppermute x2 -> x3, starting transfers between devices: 4.5 us -> 5.8 us  [passed_along(): lax.ppermute(value, 'segment', [(source, source + steps) for source in ra...]
    ppermute x2 -> x3, waiting for transfers between devices: 2.41 us -> 3.62 us  [passed_along(): lax.ppermute(value, 'segment', [(source, source + steps) for source in ra...]
  transfers between devices with their start and end apart: 31 -> 32, of which waited for: 18 -> 16; matrix products, arithmetic and copies ran while one was open for 11% -> 12% of each run, Pallas kernels for 0% -> 0%
where the time goes in v5:
time: 105 us
  starting transfers between devices  49.5 us (47%)
  waiting for transfers between devices  32.2 us (31%)
  matrix products  7.68 us (7%)
  blocking collectives  7.12 us (7%)
  other arithmetic  5.39 us (5%)
  local copies, waits for them, and re-layouts  1.55 us (1%)
  between operations  1.35 us (1%)
    ppermute x10, starting transfers between devices, across(): return lax.ppermute(value, ('row', 'col'), pairs)  22.5 us
    ppermute x4, waiting for transfers between devices, across(): return lax.ppermute(value, ('segment', 'row', 'col'), pairs)  13.5 us
    ppermute x12, waiting for transfers between devices, step_swap(): return lax.ppermute(value, ('row', 'col'), pairs)  11.5 us
    ppermute x12, starting transfers between devices, step_swap(): return lax.ppermute(value, ('row', 'col'), pairs)  11.4 us
    ppermute x4, starting transfers between devices, across(): return lax.ppermute(value, ('segment', 'row', 'col'), pairs)  9.01 us
    ppermute x3, starting transfers between devices, passed_along(): lax.ppermute(value, 'segment', [(source, source + steps) for source in ra...  5.8 us
    dot_general x4, matrix products, multiplied(): jnp.dot(full, flow('weight'), preferred_element_type=F32).astype(BF16)  5.11 us
    all_gather x2, blocking collectives, others(): halves = lax.all_gather(half, 'col', axis=0, tiled=False)  4.94 us
  transfers between devices with their start and end apart: 32, of which 16 were waited for; matrix products, arithmetic and copies ran while one was open for 12% of the time, Pallas kernels for 0%

profile of v5, /device:TPU:1, one launch (start us, length us, event | category | flops | bytes accessed | tf_op | source)
XLA Modules:
  0.0 104.8 jit_solution(12874585598412007705)
XLA Ops:
  0.6 1.1 %slice_bitcast_fusion = (bf16[64,2048]{1,0:T(8,128)(2,1)S(1)}, bf16[64,2048]{1,0:T(8,128)(2,1)S(1)}) fusion(bf16[1,2,64,2048]{3,2,1,0:T(8,128)(2,1)} %param.13), kind=kLoop, calls=%fused_computation.84 | loop fusion | bytes 1048576 | tf_op jit(solution)/shard_map/squeeze | solution.py:296
  1.7 4.5 %collective-permute-start.1 = (bf16[64,1024]{1,0:T(8,128)(2,1)S(1)}, bf16[64,1024]{1,0:T(8,128)(2,1)S(1)}, u32[]{:S(2)}, u32[]{:S(2)}) collective-permute-start(bf16[64,1024]{1,0:T(8,128)(2,1)S(1)} %get-tuple-element.155), channel_id=1, source_target_pairs={{0,0},{1,4},{2,2},{3,6},{5,5},{4,1},{7,7},{6,3},{8,8},{9,12},{10,1... | collective-permute-start | bytes 393224 | tf_op jit(solution)/shard_map/ppermute | solution.py:139
  6.3 1.0 collective-permute-start.2
  7.3 1.0 broadcast_select_fusion.34
  8.3 3.6 %collective-permute-start = (bf16[64,1024]{1,0:T(8,128)(2,1)S(1)}, bf16[64,1024]{1,0:T(8,128)(2,1)S(1)}, u32[]{:S(2)}, u32[]{:S(2)}) collective-permute-start(bf16[64,1024]{1,0:T(8,128)(2,1)S(1)} %get-tuple-element.156), channel_id=1, source_target_pairs={{0,0},{1,4},{2,2},{3,6},{5,5},{4,1},{7,7},{6,3},{8,8},{9,12},{10,1... | collective-permute-start | bytes 393224 | tf_op jit(solution)/shard_map/ppermute | solution.py:139
  12.5 2.3 %all-gather = bf16[256,1024]{1,0:T(8,128)(2,1)S(1)} all-gather(bf16[128,1024]{1,0:T(8,128)(2,1)S(1)} %pad_maximum_fusion.2), channel_id=2, replica_groups=mesh['segment'=4,'row'=4,'col'=2] {'col'}, dimensions={0}, use_global_device_ids=true | all-gather | bytes 786432 | tf_op jit(solution)/shard_map/all_gather | solution.py:207
  14.9 1.3 %convolution_convert_fusion.3 = bf16[256,2048]{1,0:T(8,128)(2,1)S(1)} fusion(bf16[64,1024]{1,0:T(8,128)(2,1)S(1)} %get-tuple-element.153, bf16[64,1024]{1,0:T(8,128)(2,1)S(1)} %get-tuple-element.119, bf16[64,1024]{1,0:T(8,128)(2,1)S(1)} %get-tuple-element.118, bf16[64,1024]{1,0:T(8,128)(2,1)S(1)} %get-tuple-element.152, bf16[1,1024,2048]{2,1,0:T(8,128)(2,1)S(1)} %copy-done.5), kind=kOutput, calls=%fused_computation.3 | convolution fusion | flops 1076363264 | bytes 5767168 | tf_op jit(solution)/shard_map/dot_general | solution.py:224
  16.3 0.8 collective-permute-start.6
  17.3 2.6 %all-gather.1 = bf16[256,1024]{1,0:T(8,128)(2,1)S(1)} all-gather(bf16[128,1024]{1,0:T(8,128)(2,1)S(1)} %pad_maximum_fusion.3), channel_id=3, replica_groups=mesh['segment'=4,'row'=4,'col'=2] {'col'}, dimensions={0}, use_global_device_ids=true | all-gather | bytes 786432 | tf_op jit(solution)/shard_map/all_gather | solution.py:207
  20.0 1.3 %convolution_convert_fusion.2 = bf16[256,2048]{1,0:T(8,128)(2,1)S(1)} fusion(bf16[64,1024]{1,0:T(8,128)(2,1)S(1)} %get-tuple-element.151, bf16[64,1024]{1,0:T(8,128)(2,1)S(1)} %get-tuple-element.115, bf16[64,1024]{1,0:T(8,128)(2,1)S(1)} %get-tuple-element.114, bf16[64,1024]{1,0:T(8,128)(2,1)S(1)} %get-tuple-element.150, bf16[1,1024,2048]{2,1,0:T(8,128)(2,1)S(1)} %copy-done.5), kind=kOutput, calls=%fused_computation.2 | convolution fusion | flops 1076363264 | bytes 5767168 | tf_op jit(solution)/shard_map/dot_general | solution.py:224
  21.4 0.9 collective-permute-start.4
  22.3 2.5 %collective-permute-start.14 = (bf16[64,1024]{1,0:T(8,128)(2,1)S(1)}, bf16[64,1024]{1,0:T(8,128)(2,1)S(1)}, u32[]{:S(2)}, u32[]{:S(2)}) collective-permute-start(bf16[64,1024]{1,0:T(8,128)(2,1)S(1)} %get-tuple-element.146), channel_id=1, source_target_pairs={{0,0},{1,4},{2,2},{3,6},{5,5},{4,1},{7,7},{6,3},{8,8},{9,12},{10,1... | collective-permute-start | bytes 393224 | tf_op jit(solution)/shard_map/ppermute | solution.py:139
  24.8 1.3 %collective-permute-start.15 = (bf16[64,1024]{1,0:T(8,128)(2,1)S(1)}, bf16[64,1024]{1,0:T(8,128)(2,1)S(1)}, u32[]{:S(2)}, u32[]{:S(2)}) collective-permute-start(bf16[64,1024]{1,0:T(8,128)(2,1)S(1)} %get-tuple-element.147), channel_id=1, source_target_pairs={{0,2},{1,6},{2,0},{3,4},{5,7},{4,3},{7,5},{6,1},{8,10},{9,14},{10,... | collective-permute-start | bytes 393224 | tf_op jit(solution)/shard_map/ppermute | solution.py:139
  26.3 5.9 %collective-permute-done.4 = bf16[128,2048]{1,0:T(8,128)(2,1)S(1)} collective-permute-done((bf16[128,2048]{1,0:T(8,128)(2,1)S(1)}, bf16[128,2048]{1,0:T(8,128)(2,1)S(1)}, u32[]{:S(2)}, u32[]{:S(2)}) %collective-permute-start.4) | collective-permute-done | bytes 524320 | tf_op jit(solution)/shard_map/ppermute | solution.py:129
  32.5 0.8 collective-permute-start.5
  33.9 1.3 %collective-permute-start.11 = (bf16[64,2048]{1,0:T(8,128)(2,1)S(1)}, bf16[64,2048]{1,0:T(8,128)(2,1)S(1)}, u32[]{:S(2)}, u32[]{:S(2)}) collective-permute-start(bf16[64,2048]{1,0:T(8,128)(2,1)S(1)} %bitcast.45), channel_id=1, source_target_pairs={{8,0},{16,8},{24,16},{9,1},{17,9},{25,17},{10,2},{18,10},{26,18},{... | collective-permute-start | bytes 786440 | tf_op jit(solution)/shard_map/ppermute | solution.py:56
  35.2 1.9 %collective-permute-done.7 = bf16[64,2048]{1,0:T(8,128)(2,1)S(1)} collective-permute-done((bf16[64,2048]{1,0:T(8,128)(2,1)S(1)}, bf16[64,2048]{1,0:T(8,128)(2,1)S(1)}, u32[]{:S(2)}, u32[]{:S(2)}) %collective-permute-start.7) | collective-permute-done | bytes 262176 | tf_op jit(solution)/shard_map/ppermute | solution.py:129
  37.3 2.1 %collective-permute-start.12 = (bf16[64,2048]{1,0:T(8,128)(2,1)S(1)}, bf16[64,2048]{1,0:T(8,128)(2,1)S(1)}, u32[]{:S(2)}, u32[]{:S(2)}) collective-permute-start(bf16[64,2048]{1,0:T(8,128)(2,1)S(1)} %fusion.7), channel_id=1, source_target_pairs={{0,2},{1,5},{2,0},{3,7},{4,6},{5,1},{6,4},{7,3},{8,10},{9,13},{10,... | collective-permute-start | bytes 786440 | tf_op jit(solution)/shard_map/ppermute | solution.py:129
  39.6 3.2 %collective-permute-start.8 = (bf16[64,2048]{1,0:T(8,128)(2,1)S(1)}, bf16[64,2048]{1,0:T(8,128)(2,1)S(1)}, u32[]{:S(2)}, u32[]{:S(2)}) collective-permute-start(bf16[64,2048]{1,0:T(8,128)(2,1)S(1)} %add_convert_fusion.3), channel_id=1, source_target_pairs={{0,8},{8,16},{16,24},{1,9},{9,17},{17,25},{2,10},{10,18},{18,26},{... | collective-permute-start | bytes 786440 | tf_op jit(solution)/shard_map/ppermute | solution.py:56
  43.5 1.1 %collective-permute-start.13 = (bf16[128,2048]{1,0:T(8,128)(2,1)S(1)}, bf16[128,2048]{1,0:T(8,128)(2,1)S(1)}, u32[]{:S(2)}, u32[]{:S(2)}) collective-permute-start(bf16[128,2048]{1,0:T(8,128)(2,1)S(1)} %pad_maximum_fusion), channel_id=1, source_target_pairs={{0,4},{1,3},{2,6},{3,1},{4,0},{5,7},{6,2},{7,5},{8,12},{9,11},{10,... | collective-permute-start | bytes 1572872 | tf_op jit(solution)/shard_map/ppermute | solution.py:129
  44.6 3.6 %collective-permute-done.8 = bf16[64,2048]{1,0:T(8,128)(2,1)S(1)} collective-permute-done((bf16[64,2048]{1,0:T(8,128)(2,1)S(1)}, bf16[64,2048]{1,0:T(8,128)(2,1)S(1)}, u32[]{:S(2)}, u32[]{:S(2)}) %collective-permute-start.8) | collective-permute-done | bytes 262176 | tf_op jit(solution)/shard_map/ppermute | solution.py:56
  48.3 3.2 %collective-permute-start.9 = (bf16[64,1024]{1,0:T(8,128)(2,1)S(1)}, bf16[64,1024]{1,0:T(8,128)(2,1)S(1)}, u32[]{:S(2)}, u32[]{:S(2)}) collective-permute-start(bf16[64,1024]{1,0:T(8,128)(2,1)S(1)} %get-tuple-element.149), channel_id=1, source_target_pairs={{0,0},{1,4},{2,2},{3,6},{5,5},{4,1},{7,7},{6,3},{8,8},{9,12},{10,1... | collective-permute-start | bytes 393224 | tf_op jit(solution)/shard_map/ppermute | solution.py:139
  51.6 1.3 %convolution_convert_fusion.1 = bf16[256,2048]{1,0:T(8,128)(2,1)S(1)} fusion(bf16[64,1024]{1,0:T(8,128)(2,1)S(1)} %get-tuple-element.69, bf16[64,1024]{1,0:T(8,128)(2,1)S(1)} %get-tuple-element.141, bf16[64,1024]{1,0:T(8,128)(2,1)S(1)} %get-tuple-element.140, bf16[64,1024]{1,0:T(8,128)(2,1)S(1)} %get-tuple-element.66, bf16[1,1024,2048]{2,1,0:T(8,128)(2,1)S(1)} %copy-done.5), kind=kOutput, calls=%fused_computation.1 | convolution fusion | flops 1076363264 | bytes 5767168 | tf_op jit(solution)/shard_map/dot_general | solution.py:224
  53.0 1.8 %collective-permute-start.10 = (bf16[64,1024]{1,0:T(8,128)(2,1)S(1)}, bf16[64,1024]{1,0:T(8,128)(2,1)S(1)}, u32[]{:S(2)}, u32[]{:S(2)}) collective-permute-start(bf16[64,1024]{1,0:T(8,128)(2,1)S(1)} %get-tuple-element.148), channel_id=1, source_target_pairs={{0,2},{1,6},{2,0},{3,4},{5,7},{4,3},{7,5},{6,1},{8,10},{9,14},{10,... | collective-permute-start | bytes 393224 | tf_op jit(solution)/shard_map/ppermute | solution.py:139
  54.9 1.3 %convolution_convert_fusion.5 = bf16[256,1024]{1,0:T(8,128)(2,1)S(1)} fusion(bf16[128,2048]{1,0:T(8,128)(2,1)S(1)} %collective-permute-done.13, bf16[128,2048]{1,0:T(8,128)(2,1)S(1)} %pad_maximum_fusion, bf16[1,1024,2048]{2,1,0:T(8,128)(2,1)S(1)} %copy-done.5), kind=kOutput, calls=%fused_computation.5 | convolution fusion | flops 1076101120 | bytes 5767168 | tf_op jit(solution)/shard_map/dot_general | solution.py:252
  56.4 2.2 %all-gather.2 = bf16[256,1024]{1,0:T(8,128)(2,1)S(1)} all-gather(bf16[128,1024]{1,0:T(8,128)(2,1)S(1)} %get-tuple-element.74), channel_id=4, replica_groups=mesh['segment'=4,'row'=4,'col'=2] {'col'}, dimensions={0}, use_global_device_ids=true | all-gather | bytes 786432 | tf_op jit(solution)/shard_map/all_gather | solution.py:262
  58.7 1.3 %collective-permute-start.18 = (bf16[64,1024]{1,0:T(8,128)(2,1)S(1)}, bf16[64,1024]{1,0:T(8,128)(2,1)S(1)}, u32[]{:S(2)}, u32[]{:S(2)}) collective-permute-start(bf16[64,1024]{1,0:T(8,128)(2,1)S(1)} %get-tuple-element.139), channel_id=1, source_target_pairs={{8,0},{9,4},{10,2},{11,6},{13,5},{12,1},{15,7},{14,3},{16,8},{17,1... | collective-permute-start | bytes 393224 | tf_op jit(solution)/shard_map/ppermute | solution.py:147
  60.0 1.3 %collective-permute-start.17 = (bf16[64,1024]{1,0:T(8,128)(2,1)S(1)}, bf16[64,1024]{1,0:T(8,128)(2,1)S(1)}, u32[]{:S(2)}, u32[]{:S(2)}) collective-permute-start(bf16[64,1024]{1,0:T(8,128)(2,1)S(1)} %get-tuple-element.138), channel_id=1, source_target_pairs={{8,2},{9,6},{10,0},{11,4},{13,7},{12,3},{15,5},{14,1},{16,10},{17,... | collective-permute-start | bytes 393224 | tf_op jit(solution)/shard_map/ppermute | solution.py:147
  61.5 1.4 %collective-permute-start.20 = (bf16[64,2048]{1,0:T(8,128)(2,1)S(1)}, bf16[64,2048]{1,0:T(8,128)(2,1)S(1)}, u32[]{:S(2)}, u32[]{:S(2)}) collective-permute-start(bf16[64,2048]{1,0:T(8,128)(2,1)S(1)} %split.333), channel_id=1, source_target_pairs={{0,4},{1,3},{2,6},{3,1},{4,0},{5,7},{6,2},{7,5},{8,12},{9,11},{10,... | collective-permute-start | bytes 786440 | tf_op jit(solution)/shard_map/ppermute | solution.py:129
  62.9 4.6 %collective-permute-done.18 = bf16[64,1024]{1,0:T(8,128)(2,1)S(1)} collective-permute-done((bf16[64,1024]{1,0:T(8,128)(2,1)S(1)}, bf16[64,1024]{1,0:T(8,128)(2,1)S(1)}, u32[]{:S(2)}, u32[]{:S(2)}) %collective-permute-start.18) | collective-permute-done | bytes 131104 | tf_op jit(solution)/shard_map/ppermute | solution.py:147
  67.6 3.2 %collective-permute-done.17 = bf16[64,1024]{1,0:T(8,128)(2,1)S(1)} collective-permute-done((bf16[64,1024]{1,0:T(8,128)(2,1)S(1)}, bf16[64,1024]{1,0:T(8,128)(2,1)S(1)}, u32[]{:S(2)}, u32[]{:S(2)}) %collective-permute-start.17) | collective-permute-done | bytes 131104 | tf_op jit(solution)/shard_map/ppermute | solution.py:147
  71.6 1.5 %collective-permute-start.23 = (bf16[64,2048]{1,0:T(8,128)(2,1)S(1)}, bf16[64,2048]{1,0:T(8,128)(2,1)S(1)}, u32[]{:S(2)}, u32[]{:S(2)}) collective-permute-start(bf16[64,2048]{1,0:T(8,128)(2,1)S(1)} %get-tuple-element.94), channel_id=1, source_target_pairs={{0,4},{1,3},{2,6},{3,1},{4,0},{5,7},{6,2},{7,5},{8,12},{9,11},{10,... | collective-permute-start | bytes 786440 | tf_op jit(solution)/shard_map/ppermute | solution.py:129
  73.3 1.3 %convolution_convert_fusion = bf16[256,2048]{1,0:T(8,128)(2,1)S(1)} fusion(bf16[64,1024]{1,0:T(8,128)(2,1)S(1)} %get-tuple-element.82, bf16[64,1024]{1,0:T(8,128)(2,1)S(1)} %get-tuple-element.131, bf16[64,1024]{1,0:T(8,128)(2,1)S(1)} %get-tuple-element.130, bf16[64,1024]{1,0:T(8,128)(2,1)S(1)} %get-tuple-element.79, bf16[1,1024,2048]{2,1,0:T(8,128)(2,1)S(1)} %copy-done.5), kind=kOutput, calls=%fused_computation | convolution fusion | flops 1076363264 | bytes 5767168 | tf_op jit(solution)/shard_map/dot_general | solution.py:224
  74.6 0.9 collective-permute-start.22
  75.5 3.4 %collective-permute-start.28 = (bf16[64,1024]{1,0:T(8,128)(2,1)S(1)}, bf16[64,1024]{1,0:T(8,128)(2,1)S(1)}, u32[]{:S(2)}, u32[]{:S(2)}) collective-permute-start(bf16[64,1024]{1,0:T(8,128)(2,1)S(1)} %get-tuple-element.138), channel_id=1, source_target_pairs={{0,2},{1,6},{2,0},{3,4},{5,7},{4,3},{7,5},{6,1}} | collective-permute-start | bytes 393224 | tf_op jit(solution)/shard_map/ppermute | solution.py:147
  79.0 3.0 %collective-permute-start.29 = (bf16[64,1024]{1,0:T(8,128)(2,1)S(1)}, bf16[64,1024]{1,0:T(8,128)(2,1)S(1)}, u32[]{:S(2)}, u32[]{:S(2)}) collective-permute-start(bf16[64,1024]{1,0:T(8,128)(2,1)S(1)} %get-tuple-element.139), channel_id=1, source_target_pairs={{0,0},{1,4},{2,2},{3,6},{5,5},{4,1},{7,7},{6,3}} | collective-permute-start | bytes 393224 | tf_op jit(solution)/shard_map/ppermute | solution.py:147
  82.1 4.7 %collective-permute-done.28 = bf16[64,1024]{1,0:T(8,128)(2,1)S(1)} collective-permute-done((bf16[64,1024]{1,0:T(8,128)(2,1)S(1)}, bf16[64,1024]{1,0:T(8,128)(2,1)S(1)}, u32[]{:S(2)}, u32[]{:S(2)}) %collective-permute-start.28) | collective-permute-done | bytes 131104 | tf_op jit(solution)/shard_map/ppermute | solution.py:147
  86.8 0.9 collective-permute-done.29
  88.0 1.3 %collective-permute-start.27 = (bf16[64,2048]{1,0:T(8,128)(2,1)S(1)}, bf16[64,2048]{1,0:T(8,128)(2,1)S(1)}, u32[]{:S(2)}, u32[]{:S(2)}) collective-permute-start(bf16[64,2048]{1,0:T(8,128)(2,1)S(1)} %get-tuple-element.90), channel_id=1, source_target_pairs={{0,8},{8,16},{16,24},{1,9},{9,17},{17,25},{2,10},{10,18},{18,26},{... | collective-permute-start | bytes 786440 | tf_op jit(solution)/shard_map/ppermute | solution.py:56
  89.3 3.0 %collective-permute-done.25 = bf16[128,2048]{1,0:T(8,128)(2,1)S(1)} collective-permute-done((bf16[128,2048]{1,0:T(8,128)(2,1)S(1)}, bf16[128,2048]{1,0:T(8,128)(2,1)S(1)}, u32[]{:S(2)}, u32[]{:S(2)}) %collective-permute-start.25) | collective-permute-done | bytes 524320 | tf_op jit(solution)/shard_map/ppermute | solution.py:129
  92.3 1.3 %convolution_convert_fusion.4 = bf16[256,1024]{1,0:T(8,128)(2,1)S(1)} fusion(bf16[128,2048]{1,0:T(8,128)(2,1)S(1)} %collective-permute-done.25, bf16[128,2048]{1,0:T(8,128)(2,1)S(1)} %pad_maximum_fusion.1, bf16[1,1024,2048]{2,1,0:T(8,128)(2,1)S(1)} %copy-done.5), kind=kOutput, calls=%fused_computation.4 | convolution fusion | flops 1076101120 | bytes 5767168 | tf_op jit(solution)/shard_map/dot_general | solution.py:252
  93.9 1.6 %collective-permute-start.24 = (bf16[64,2048]{1,0:T(8,128)(2,1)S(1)}, bf16[64,2048]{1,0:T(8,128)(2,1)S(1)}, u32[]{:S(2)}, u32[]{:S(2)}) collective-permute-start(bf16[64,2048]{1,0:T(8,128)(2,1)S(1)} %split.332), channel_id=1, source_target_pairs={{0,4},{1,3},{2,6},{3,1},{4,0},{5,7},{6,2},{7,5},{8,12},{9,11},{10,... | collective-permute-start | bytes 786440 | tf_op jit(solution)/shard_map/ppermute | solution.py:129
  95.5 2.0 %collective-permute-start.30 = (bf16[64,1024]{1,0:T(8,128)(2,1)S(1)}, bf16[64,1024]{1,0:T(8,128)(2,1)S(1)}, u32[]{:S(2)}, u32[]{:S(2)}) collective-permute-start(bf16[64,1024]{1,0:T(8,128)(2,1)S(1)} %get-tuple-element.128), channel_id=1, source_target_pairs={{0,2},{1,6},{2,0},{3,4},{5,7},{4,3},{7,5},{6,1},{8,10},{9,14},{10,... | collective-permute-start | bytes 393224 | tf_op jit(solution)/shard_map/ppermute | solution.py:139
  97.5 2.5 %collective-permute-start.31 = (bf16[64,1024]{1,0:T(8,128)(2,1)S(1)}, bf16[64,1024]{1,0:T(8,128)(2,1)S(1)}, u32[]{:S(2)}, u32[]{:S(2)}) collective-permute-start(bf16[64,1024]{1,0:T(8,128)(2,1)S(1)} %get-tuple-element.129), channel_id=1, source_target_pairs={{0,0},{1,4},{2,2},{3,6},{5,5},{4,1},{7,7},{6,3},{8,8},{9,12},{10,1... | collective-permute-start | bytes 393224 | tf_op jit(solution)/shard_map/ppermute | solution.py:139
  100.4 0.8 maximum_bitcast_fusion
  101.2 1.2 %collective-permute-done.30 = bf16[64,1024]{1,0:T(8,128)(2,1)S(1)} collective-permute-done((bf16[64,1024]{1,0:T(8,128)(2,1)S(1)}, bf16[64,1024]{1,0:T(8,128)(2,1)S(1)}, u32[]{:S(2)}, u32[]{:S(2)}) %collective-permute-start.30) | collective-permute-done | bytes 131104 | tf_op jit(solution)/shard_map/ppermute | solution.py:139
  102.4 1.4 %collective-permute-done.31 = bf16[64,1024]{1,0:T(8,128)(2,1)S(1)} collective-permute-done((bf16[64,1024]{1,0:T(8,128)(2,1)S(1)}, bf16[64,1024]{1,0:T(8,128)(2,1)S(1)}, u32[]{:S(2)}, u32[]{:S(2)}) %collective-permute-start.31) | collective-permute-done | bytes 131104 | tf_op jit(solution)/shard_map/ppermute | solution.py:139
  104.0 0.8 maximum_bitcast_fusion.1
  (94 shorter events, 5.8 us)
Async XLA Ops:
  1.7 10.3 %collective-permute-start.1 = (bf16[64,1024]{1,0:T(8,128)(2,1)S(1)}, bf16[64,1024]{1,0:T(8,128)(2,1)S(1)}, u32[]{:S(2)}, u32[]{:S(2)}) collective-permute-start(bf16[64,1024]{1,0:T(8,128)(2,1)S(1)} %get-tuple-element.155), channel_id=1, source_target_pairs={{0,0},{1,4},{2,2},{3,6},{5,5},{4,1},{7,7},{6,3},{8,8},{9,12},{10,1... | collective-permute-start | bytes 393224 | tf_op jit(solution)/shard_map/ppermute | solution.py:139
  6.3 6.1 %collective-permute-start.2 = (bf16[64,1024]{1,0:T(8,128)(2,1)S(1)}, bf16[64,1024]{1,0:T(8,128)(2,1)S(1)}, u32[]{:S(2)}, u32[]{:S(2)}) collective-permute-start(bf16[64,1024]{1,0:T(8,128)(2,1)S(1)} %get-tuple-element.154), channel_id=1, source_target_pairs={{0,2},{1,6},{2,0},{3,4},{5,7},{4,3},{7,5},{6,1},{8,10},{9,14},{10,... | collective-permute-start | bytes 393224 | tf_op jit(solution)/shard_map/ppermute | solution.py:139
  8.3 8.0 %collective-permute-start = (bf16[64,1024]{1,0:T(8,128)(2,1)S(1)}, bf16[64,1024]{1,0:T(8,128)(2,1)S(1)}, u32[]{:S(2)}, u32[]{:S(2)}) collective-permute-start(bf16[64,1024]{1,0:T(8,128)(2,1)S(1)} %get-tuple-element.156), channel_id=1, source_target_pairs={{0,0},{1,4},{2,2},{3,6},{5,5},{4,1},{7,7},{6,3},{8,8},{9,12},{10,1... | collective-permute-start | bytes 393224 | tf_op jit(solution)/shard_map/ppermute | solution.py:139
  11.9 5.4 %collective-permute-start.3 = (bf16[64,1024]{1,0:T(8,128)(2,1)S(1)}, bf16[64,1024]{1,0:T(8,128)(2,1)S(1)}, u32[]{:S(2)}, u32[]{:S(2)}) collective-permute-start(bf16[64,1024]{1,0:T(8,128)(2,1)S(1)} %get-tuple-element.157), channel_id=1, source_target_pairs={{0,2},{1,6},{2,0},{3,4},{5,7},{4,3},{7,5},{6,1},{8,10},{9,14},{10,... | collective-permute-start | bytes 393224 | tf_op jit(solution)/shard_map/ppermute | solution.py:139
  12.1 2.9 %copy-start.5 = (bf16[1,1024,2048]{2,1,0:T(8,128)(2,1)S(1)}, bf16[1,1024,2048]{2,1,0:T(8,128)(2,1)}, u32[]{:S(2)}) copy-start(bf16[1,1024,2048]{2,1,0:T(8,128)(2,1)} %param.7) | copy-start | bytes 12582916
  16.3 9.8 %collective-permute-start.6 = (bf16[128,2048]{1,0:T(8,128)(2,1)S(1)}, bf16[128,2048]{1,0:T(8,128)(2,1)S(1)}, u32[]{:S(2)}, u32[]{:S(2)}) collective-permute-start(bf16[128,2048]{1,0:T(8,128)(2,1)S(1)} %split.238), channel_id=1, source_target_pairs={{0,4},{1,3},{2,6},{3,1},{4,0},{5,7},{6,2},{7,5},{8,12},{9,11},{10,... | collective-permute-start | bytes 1572872 | tf_op jit(solution)/shard_map/ppermute | solution.py:129
  21.3 12.6 %copy-start = (bf16[1,64,2048]{2,1,0:T(8,128)(2,1)S(1)}, bf16[1,64,2048]{2,1,0:T(8,128)(2,1)}, u32[]{:S(2)}) copy-start(bf16[1,64,2048]{2,1,0:T(8,128)(2,1)} %param.11) | copy-start | bytes 786436
  21.3 15.8 %copy-start.4 = (f32[1,2048]{1,0:T(1,128)S(1)}, f32[1,2048]{1,0:T(1,128)}, u32[]{:S(2)}) copy-start(f32[1,2048]{1,0:T(1,128)} %param.8) | copy-start | bytes 24580
  21.3 18.1 %copy-start.1 = (bf16[1,64,2048]{2,1,0:T(8,128)(2,1)S(1)}, bf16[1,64,2048]{2,1,0:T(8,128)(2,1)}, u32[]{:S(2)}) copy-start(bf16[1,64,2048]{2,1,0:T(8,128)(2,1)} %param.9) | copy-start | bytes 786436
  21.4 10.9 %collective-permute-start.4 = (bf16[128,2048]{1,0:T(8,128)(2,1)S(1)}, bf16[128,2048]{1,0:T(8,128)(2,1)S(1)}, u32[]{:S(2)}, u32[]{:S(2)}) collective-permute-start(bf16[128,2048]{1,0:T(8,128)(2,1)S(1)} %split.244), channel_id=1, source_target_pairs={{0,2},{1,5},{2,0},{3,7},{4,6},{5,1},{6,4},{7,3},{8,10},{9,13},{10,... | collective-permute-start | bytes 1572872 | tf_op jit(solution)/shard_map/ppermute | solution.py:129
  22.3 11.0 %collective-permute-start.14 = (bf16[64,1024]{1,0:T(8,128)(2,1)S(1)}, bf16[64,1024]{1,0:T(8,128)(2,1)S(1)}, u32[]{:S(2)}, u32[]{:S(2)}) collective-permute-start(bf16[64,1024]{1,0:T(8,128)(2,1)S(1)} %get-tuple-element.146), channel_id=1, source_target_pairs={{0,0},{1,4},{2,2},{3,6},{5,5},{4,1},{7,7},{6,3},{8,8},{9,12},{10,1... | collective-permute-start | bytes 393224 | tf_op jit(solution)/shard_map/ppermute | solution.py:139
  24.8 8.8 %collective-permute-start.15 = (bf16[64,1024]{1,0:T(8,128)(2,1)S(1)}, bf16[64,1024]{1,0:T(8,128)(2,1)S(1)}, u32[]{:S(2)}, u32[]{:S(2)}) collective-permute-start(bf16[64,1024]{1,0:T(8,128)(2,1)S(1)} %get-tuple-element.147), channel_id=1, source_target_pairs={{0,2},{1,6},{2,0},{3,4},{5,7},{4,3},{7,5},{6,1},{8,10},{9,14},{10,... | collective-permute-start | bytes 393224 | tf_op jit(solution)/shard_map/ppermute | solution.py:139
  26.3 10.8 %collective-permute-start.7 = (bf16[64,2048]{1,0:T(8,128)(2,1)S(1)}, bf16[64,2048]{1,0:T(8,128)(2,1)S(1)}, u32[]{:S(2)}, u32[]{:S(2)}) collective-permute-start(bf16[64,2048]{1,0:T(8,128)(2,1)S(1)} %split.334), channel_id=1, source_target_pairs={{0,2},{1,5},{2,0},{3,7},{4,6},{5,1},{6,4},{7,3},{8,10},{9,13},{10,... | collective-permute-start | bytes 786440 | tf_op jit(solution)/shard_map/ppermute | solution.py:129
  32.4 15.8 %copy-start.3 = (bf16[64,2048]{1,0:T(8,128)(2,1)S(1)}, bf16[64,2048]{1,0:T(8,128)(2,1)}, u32[]{:S(2)}) copy-start(bf16[64,2048]{1,0:T(8,128)(2,1)} %param.10) | copy-start | bytes 786436
  32.5 7.0 %collective-permute-start.5 = (bf16[64,2048]{1,0:T(8,128)(2,1)S(1)}, bf16[64,2048]{1,0:T(8,128)(2,1)S(1)}, u32[]{:S(2)}, u32[]{:S(2)}) collective-permute-start(bf16[64,2048]{1,0:T(8,128)(2,1)S(1)} %split.335), channel_id=1, source_target_pairs={{0,4},{1,3},{2,6},{3,1},{4,0},{5,7},{6,2},{7,5},{8,12},{9,11},{10,... | collective-permute-start | bytes 786440 | tf_op jit(solution)/shard_map/ppermute | solution.py:129
  33.7 5.9 %collective-permute-start.16 = (bf16[128,1024]{1,0:T(8,128)(2,1)S(1)}, bf16[128,1024]{1,0:T(8,128)(2,1)S(1)}, u32[]{:S(2)}, u32[]{:S(2)}) collective-permute-start(bf16[128,1024]{1,0:T(8,128)(2,1)S(1)} %pad_maximum_fusion.4), channel_id=1, source_target_pairs={{0,1},{1,0},{2,3},{3,2},{4,5},{5,4},{6,7},{7,6},{8,9},{9,8},{10,11... | collective-permute-start | bytes 786440 | tf_op jit(solution)/shard_map/ppermute | solution.py:81
  33.9 19.1 %collective-permute-start.11 = (bf16[64,2048]{1,0:T(8,128)(2,1)S(1)}, bf16[64,2048]{1,0:T(8,128)(2,1)S(1)}, u32[]{:S(2)}, u32[]{:S(2)}) collective-permute-start(bf16[64,2048]{1,0:T(8,128)(2,1)S(1)} %bitcast.45), channel_id=1, source_target_pairs={{8,0},{16,8},{24,16},{9,1},{17,9},{25,17},{10,2},{18,10},{26,18},{... | collective-permute-start | bytes 786440 | tf_op jit(solution)/shard_map/ppermute | solution.py:56
  37.3 6.1 %collective-permute-start.12 = (bf16[64,2048]{1,0:T(8,128)(2,1)S(1)}, bf16[64,2048]{1,0:T(8,128)(2,1)S(1)}, u32[]{:S(2)}, u32[]{:S(2)}) collective-permute-start(bf16[64,2048]{1,0:T(8,128)(2,1)S(1)} %fusion.7), channel_id=1, source_target_pairs={{0,2},{1,5},{2,0},{3,7},{4,6},{5,1},{6,4},{7,3},{8,10},{9,13},{10,... | collective-permute-start | bytes 786440 | tf_op jit(solution)/shard_map/ppermute | solution.py:129
  39.6 8.6 %collective-permute-start.8 = (bf16[64,2048]{1,0:T(8,128)(2,1)S(1)}, bf16[64,2048]{1,0:T(8,128)(2,1)S(1)}, u32[]{:S(2)}, u32[]{:S(2)}) collective-permute-start(bf16[64,2048]{1,0:T(8,128)(2,1)S(1)} %add_convert_fusion.3), channel_id=1, source_target_pairs={{0,8},{8,16},{16,24},{1,9},{9,17},{17,25},{2,10},{10,18},{18,26},{... | collective-permute-start | bytes 786440 | tf_op jit(solution)/shard_map/ppermute | solution.py:56
  43.5 11.4 %collective-permute-start.13 = (bf16[128,2048]{1,0:T(8,128)(2,1)S(1)}, bf16[128,2048]{1,0:T(8,128)(2,1)S(1)}, u32[]{:S(2)}, u32[]{:S(2)}) collective-permute-start(bf16[128,2048]{1,0:T(8,128)(2,1)S(1)} %pad_maximum_fusion), channel_id=1, source_target_pairs={{0,4},{1,3},{2,6},{3,1},{4,0},{5,7},{6,2},{7,5},{8,12},{9,11},{10,... | collective-permute-start | bytes 1572872 | tf_op jit(solution)/shard_map/ppermute | solution.py:129
  48.3 6.6 %collective-permute-start.9 = (bf16[64,1024]{1,0:T(8,128)(2,1)S(1)}, bf16[64,1024]{1,0:T(8,128)(2,1)S(1)}, u32[]{:S(2)}, u32[]{:S(2)}) collective-permute-start(bf16[64,1024]{1,0:T(8,128)(2,1)S(1)} %get-tuple-element.149), channel_id=1, source_target_pairs={{0,0},{1,4},{2,2},{3,6},{5,5},{4,1},{7,7},{6,3},{8,8},{9,12},{10,1... | collective-permute-start | bytes 393224 | tf_op jit(solution)/shard_map/ppermute | solution.py:139
  52.9 8.4 %collective-permute-start.19 = (bf16[128,2048]{1,0:T(8,128)(2,1)S(1)}, bf16[128,2048]{1,0:T(8,128)(2,1)S(1)}, u32[]{:S(2)}, u32[]{:S(2)}) collective-permute-start(bf16[128,2048]{1,0:T(8,128)(2,1)S(1)} %split.261), channel_id=1, source_target_pairs={{0,2},{1,5},{2,0},{3,7},{4,6},{5,1},{6,4},{7,3},{8,10},{9,13},{10,... | collective-permute-start | bytes 1572872 | tf_op jit(solution)/shard_map/ppermute | solution.py:129
  53.0 18.2 %collective-permute-start.10 = (bf16[64,1024]{1,0:T(8,128)(2,1)S(1)}, bf16[64,1024]{1,0:T(8,128)(2,1)S(1)}, u32[]{:S(2)}, u32[]{:S(2)}) collective-permute-start(bf16[64,1024]{1,0:T(8,128)(2,1)S(1)} %get-tuple-element.148), channel_id=1, source_target_pairs={{0,2},{1,6},{2,0},{3,4},{5,7},{4,3},{7,5},{6,1},{8,10},{9,14},{10,... | collective-permute-start | bytes 393224 | tf_op jit(solution)/shard_map/ppermute | solution.py:139
  56.2 14.7 %copy-start.2 = (bf16[64,2048]{1,0:T(8,128)(2,1)S(1)}, bf16[64,2048]{1,0:T(8,128)(2,1)}, u32[]{:S(2)}) copy-start(bf16[64,2048]{1,0:T(8,128)(2,1)} %param.12) | copy-start | bytes 786436
  58.7 8.9 %collective-permute-start.18 = (bf16[64,1024]{1,0:T(8,128)(2,1)S(1)}, bf16[64,1024]{1,0:T(8,128)(2,1)S(1)}, u32[]{:S(2)}, u32[]{:S(2)}) collective-permute-start(bf16[64,1024]{1,0:T(8,128)(2,1)S(1)} %get-tuple-element.139), channel_id=1, source_target_pairs={{8,0},{9,4},{10,2},{11,6},{13,5},{12,1},{15,7},{14,3},{16,8},{17,1... | collective-permute-start | bytes 393224 | tf_op jit(solution)/shard_map/ppermute | solution.py:147
  60.0 10.8 %collective-permute-start.17 = (bf16[64,1024]{1,0:T(8,128)(2,1)S(1)}, bf16[64,1024]{1,0:T(8,128)(2,1)S(1)}, u32[]{:S(2)}, u32[]{:S(2)}) collective-permute-start(bf16[64,1024]{1,0:T(8,128)(2,1)S(1)} %get-tuple-element.138), channel_id=1, source_target_pairs={{8,2},{9,6},{10,0},{11,4},{13,7},{12,3},{15,5},{14,1},{16,10},{17,... | collective-permute-start | bytes 393224 | tf_op jit(solution)/shard_map/ppermute | solution.py:147
  61.5 9.3 %collective-permute-start.20 = (bf16[64,2048]{1,0:T(8,128)(2,1)S(1)}, bf16[64,2048]{1,0:T(8,128)(2,1)S(1)}, u32[]{:S(2)}, u32[]{:S(2)}) collective-permute-start(bf16[64,2048]{1,0:T(8,128)(2,1)S(1)} %split.333), channel_id=1, source_target_pairs={{0,4},{1,3},{2,6},{3,1},{4,0},{5,7},{6,2},{7,5},{8,12},{9,11},{10,... | collective-permute-start | bytes 786440 | tf_op jit(solution)/shard_map/ppermute | solution.py:129
  71.2 1.9 %collective-permute-start.21 = (bf16[128,1024]{1,0:T(8,128)(2,1)S(1)}, bf16[128,1024]{1,0:T(8,128)(2,1)S(1)}, u32[]{:S(2)}, u32[]{:S(2)}) collective-permute-start(bf16[128,1024]{1,0:T(8,128)(2,1)S(1)} %constant_dynamic-update-slice_fusion), channel_id=1, source_target_pairs={{0,1},{1,0},{2,3},{3,2},{4,5},{5,4},{6,7},{7,6},{8,9},{9,8},{10,11... | collective-permute-start | bytes 786440 | tf_op jit(solution)/shard_map/ppermute | solution.py:81
  71.6 10.4 %collective-permute-start.23 = (bf16[64,2048]{1,0:T(8,128)(2,1)S(1)}, bf16[64,2048]{1,0:T(8,128)(2,1)S(1)}, u32[]{:S(2)}, u32[]{:S(2)}) collective-permute-start(bf16[64,2048]{1,0:T(8,128)(2,1)S(1)} %get-tuple-element.94), channel_id=1, source_target_pairs={{0,4},{1,3},{2,6},{3,1},{4,0},{5,7},{6,2},{7,5},{8,12},{9,11},{10,... | collective-permute-start | bytes 786440 | tf_op jit(solution)/shard_map/ppermute | solution.py:129
  74.6 13.2 %collective-permute-start.22 = (bf16[128,2048]{1,0:T(8,128)(2,1)S(1)}, bf16[128,2048]{1,0:T(8,128)(2,1)S(1)}, u32[]{:S(2)}, u32[]{:S(2)}) collective-permute-start(bf16[128,2048]{1,0:T(8,128)(2,1)S(1)} %split.269), channel_id=1, source_target_pairs={{0,2},{1,5},{2,0},{3,7},{4,6},{5,1},{6,4},{7,3},{8,10},{9,13},{10,... | collective-permute-start | bytes 1572872 | tf_op jit(solution)/shard_map/ppermute | solution.py:129
  75.5 11.3 %collective-permute-start.28 = (bf16[64,1024]{1,0:T(8,128)(2,1)S(1)}, bf16[64,1024]{1,0:T(8,128)(2,1)S(1)}, u32[]{:S(2)}, u32[]{:S(2)}) collective-permute-start(bf16[64,1024]{1,0:T(8,128)(2,1)S(1)} %get-tuple-element.138), channel_id=1, source_target_pairs={{0,2},{1,6},{2,0},{3,4},{5,7},{4,3},{7,5},{6,1}} | collective-permute-start | bytes 393224 | tf_op jit(solution)/shard_map/ppermute | solution.py:147
  79.0 8.8 %collective-permute-start.29 = (bf16[64,1024]{1,0:T(8,128)(2,1)S(1)}, bf16[64,1024]{1,0:T(8,128)(2,1)S(1)}, u32[]{:S(2)}, u32[]{:S(2)}) collective-permute-start(bf16[64,1024]{1,0:T(8,128)(2,1)S(1)} %get-tuple-element.139), channel_id=1, source_target_pairs={{0,0},{1,4},{2,2},{3,6},{5,5},{4,1},{7,7},{6,3}} | collective-permute-start | bytes 393224 | tf_op jit(solution)/shard_map/ppermute | solution.py:147
  82.0 10.2 %collective-permute-start.25 = (bf16[128,2048]{1,0:T(8,128)(2,1)S(1)}, bf16[128,2048]{1,0:T(8,128)(2,1)S(1)}, u32[]{:S(2)}, u32[]{:S(2)}) collective-permute-start(bf16[128,2048]{1,0:T(8,128)(2,1)S(1)} %pad_maximum_fusion.1), channel_id=1, source_target_pairs={{0,2},{1,5},{2,0},{3,7},{4,6},{5,1},{6,4},{7,3},{8,10},{9,13},{10,... | collective-permute-start | bytes 1572872 | tf_op jit(solution)/shard_map/ppermute | solution.py:129
  88.0 7.5 %collective-permute-start.27 = (bf16[64,2048]{1,0:T(8,128)(2,1)S(1)}, bf16[64,2048]{1,0:T(8,128)(2,1)S(1)}, u32[]{:S(2)}, u32[]{:S(2)}) collective-permute-start(bf16[64,2048]{1,0:T(8,128)(2,1)S(1)} %get-tuple-element.90), channel_id=1, source_target_pairs={{0,8},{8,16},{16,24},{1,9},{9,17},{17,25},{2,10},{10,18},{18,26},{... | collective-permute-start | bytes 786440 | tf_op jit(solution)/shard_map/ppermute | solution.py:56
  93.7 1.7 %collective-permute-start.26 = (bf16[128,1024]{1,0:T(8,128)(2,1)S(1)}, bf16[128,1024]{1,0:T(8,128)(2,1)S(1)}, u32[]{:S(2)}, u32[]{:S(2)}) collective-permute-start(bf16[128,1024]{1,0:T(8,128)(2,1)S(1)} %get-tuple-element.89), channel_id=1, source_target_pairs={{0,1},{1,0},{2,3},{3,2},{4,5},{5,4},{6,7},{7,6},{8,9},{9,8},{10,11... | collective-permute-start | bytes 786440 | tf_op jit(solution)/shard_map/ppermute | solution.py:81
  93.9 6.2 %collective-permute-start.24 = (bf16[64,2048]{1,0:T(8,128)(2,1)S(1)}, bf16[64,2048]{1,0:T(8,128)(2,1)S(1)}, u32[]{:S(2)}, u32[]{:S(2)}) collective-permute-start(bf16[64,2048]{1,0:T(8,128)(2,1)S(1)} %split.332), channel_id=1, source_target_pairs={{0,4},{1,3},{2,6},{3,1},{4,0},{5,7},{6,2},{7,5},{8,12},{9,11},{10,... | collective-permute-start | bytes 786440 | tf_op jit(solution)/shard_map/ppermute | solution.py:129
  95.5 6.8 %collective-permute-start.30 = (bf16[64,1024]{1,0:T(8,128)(2,1)S(1)}, bf16[64,1024]{1,0:T(8,128)(2,1)S(1)}, u32[]{:S(2)}, u32[]{:S(2)}) collective-permute-start(bf16[64,1024]{1,0:T(8,128)(2,1)S(1)} %get-tuple-element.128), channel_id=1, source_target_pairs={{0,2},{1,6},{2,0},{3,4},{5,7},{4,3},{7,5},{6,1},{8,10},{9,14},{10,... | collective-permute-start | bytes 393224 | tf_op jit(solution)/shard_map/ppermute | solution.py:139
  97.5 6.3 %collective-permute-start.31 = (bf16[64,1024]{1,0:T(8,128)(2,1)S(1)}, bf16[64,1024]{1,0:T(8,128)(2,1)S(1)}, u32[]{:S(2)}, u32[]{:S(2)}) collective-permute-start(bf16[64,1024]{1,0:T(8,128)(2,1)S(1)} %get-tuple-element.129), channel_id=1, source_target_pairs={{0,0},{1,4},{2,2},{3,6},{5,5},{4,1},{7,7},{6,3},{8,8},{9,12},{10,1... | collective-permute-start | bytes 393224 | tf_op jit(solution)/shard_map/ppermute | solution.py:139

commit v6 on v5

--- a/solution.py
+++ b/solution.py
@@ -321,7 +321,8 @@
     rule("gr2", lambda: retreat(flow("up"), last_back()))
 
     layer_outputs = jnp.stack([flow("out1"), flow("out2")], axis=0)[None]
-    input_grads = jnp.stack([flow("gr1"), flow("gr2")], axis=0)[None]
+    first_half = fixed(jnp.stack([flow("gr1"), flow("up")], axis=0))
+    input_grads = lax.dynamic_update_index_in_dim(first_half, flow("gr2"), 1, 0)[None]
     return (layer_outputs, input_grads)
 
 

time: 105 us -> 105 us (level)
  transfers between devices with their start and end apart: 32 -> 32, of which waited for: 16 -> 15; matrix products, arithmetic and copies ran while one was open for 12% -> 12% of each run, Pallas kernels for 0% -> 0%
where the time goes in v6:
time: 105 us
  starting transfers between devices  49.5 us (47%)
  waiting for transfers between devices  32.1 us (31%)
  matrix products  7.68 us (7%)
  blocking collectives  7.12 us (7%)
  other arithmetic  4.56 us (4%)
  local copies, waits for them, and re-layouts  2.34 us (2%)
  between operations  1.36 us (1%)
    ppermute x10, starting transfers between devices, across(): return lax.ppermute(value, ('row', 'col'), pairs)  22.5 us
    ppermute x4, waiting for transfers between devices, across(): return lax.ppermute(value, ('segment', 'row', 'col'), pairs)  13.5 us
    ppermute x12, starting transfers between devices, step_swap(): return lax.ppermute(value, ('row', 'col'), pairs)  11.5 us
    ppermute x12, waiting for transfers between devices, step_swap(): return lax.ppermute(value, ('row', 'col'), pairs)  11.4 us
    ppermute x4, starting transfers between devices, across(): return lax.ppermute(value, ('segment', 'row', 'col'), pairs)  9.01 us
    ppermute x3, starting transfers between devices, passed_along(): lax.ppermute(value, 'segment', [(source, source + steps) for source in ra...  5.8 us
    dot_general x4, matrix products, multiplied(): jnp.dot(full, flow('weight'), preferred_element_type=F32).astype(BF16)  5.11 us
    all_gather x2, blocking collectives, others(): halves = lax.all_gather(half, 'col', axis=0, tiled=False)  4.94 us
  transfers between devices with their start and end apart: 32, of which 15 were waited for; matrix products, arithmetic and copies ran while one was open for 12% of the time, Pallas kernels for 0%

profile of v6, /device:TPU:1, one launch (start us, length us, event | category | flops | bytes accessed | tf_op | source)
XLA Modules:
  0.0 104.7 jit_solution(6890031799790514796)
XLA Ops:
  0.6 1.1 %slice_bitcast_fusion = (bf16[64,2048]{1,0:T(8,128)(2,1)S(1)}, bf16[64,2048]{1,0:T(8,128)(2,1)S(1)}) fusion(bf16[1,2,64,2048]{3,2,1,0:T(8,128)(2,1)} %param.13), kind=kLoop, calls=%fused_computation.85 | loop fusion | bytes 1048576 | tf_op jit(solution)/shard_map/squeeze | solution.py:296
  1.7 4.5 %collective-permute-start.1 = (bf16[64,1024]{1,0:T(8,128)(2,1)S(1)}, bf16[64,1024]{1,0:T(8,128)(2,1)S(1)}, u32[]{:S(2)}, u32[]{:S(2)}) collective-permute-start(bf16[64,1024]{1,0:T(8,128)(2,1)S(1)} %get-tuple-element.156), channel_id=1, source_target_pairs={{0,0},{1,4},{2,2},{3,6},{5,5},{4,1},{7,7},{6,3},{8,8},{9,12},{10,1... | collective-permute-start | bytes 393224 | tf_op jit(solution)/shard_map/ppermute | solution.py:139
  6.3 1.0 collective-permute-start.2
  7.3 1.0 broadcast_select_fusion.34
  8.3 3.6 %collective-permute-start = (bf16[64,1024]{1,0:T(8,128)(2,1)S(1)}, bf16[64,1024]{1,0:T(8,128)(2,1)S(1)}, u32[]{:S(2)}, u32[]{:S(2)}) collective-permute-start(bf16[64,1024]{1,0:T(8,128)(2,1)S(1)} %get-tuple-element.157), channel_id=1, source_target_pairs={{0,0},{1,4},{2,2},{3,6},{5,5},{4,1},{7,7},{6,3},{8,8},{9,12},{10,1... | collective-permute-start | bytes 393224 | tf_op jit(solution)/shard_map/ppermute | solution.py:139
  12.5 2.3 %all-gather = bf16[256,1024]{1,0:T(8,128)(2,1)S(1)} all-gather(bf16[128,1024]{1,0:T(8,128)(2,1)S(1)} %pad_maximum_fusion.3), channel_id=2, replica_groups=mesh['segment'=4,'row'=4,'col'=2] {'col'}, dimensions={0}, use_global_device_ids=true | all-gather | bytes 786432 | tf_op jit(solution)/shard_map/all_gather | solution.py:207
  14.9 1.3 %convolution_convert_fusion.3 = bf16[256,2048]{1,0:T(8,128)(2,1)S(1)} fusion(bf16[64,1024]{1,0:T(8,128)(2,1)S(1)} %get-tuple-element.154, bf16[64,1024]{1,0:T(8,128)(2,1)S(1)} %get-tuple-element.120, bf16[64,1024]{1,0:T(8,128)(2,1)S(1)} %get-tuple-element.119, bf16[64,1024]{1,0:T(8,128)(2,1)S(1)} %get-tuple-element.153, bf16[1,1024,2048]{2,1,0:T(8,128)(2,1)S(1)} %copy-done.6), kind=kOutput, calls=%fused_computation.3 | convolution fusion | flops 1076363264 | bytes 5767168 | tf_op jit(solution)/shard_map/dot_general | solution.py:224
  16.3 0.8 collective-permute-start.6
  17.3 2.6 %all-gather.1 = bf16[256,1024]{1,0:T(8,128)(2,1)S(1)} all-gather(bf16[128,1024]{1,0:T(8,128)(2,1)S(1)} %pad_maximum_fusion.4), channel_id=3, replica_groups=mesh['segment'=4,'row'=4,'col'=2] {'col'}, dimensions={0}, use_global_device_ids=true | all-gather | bytes 786432 | tf_op jit(solution)/shard_map/all_gather | solution.py:207
  20.0 1.3 %convolution_convert_fusion.2 = bf16[256,2048]{1,0:T(8,128)(2,1)S(1)} fusion(bf16[64,1024]{1,0:T(8,128)(2,1)S(1)} %get-tuple-element.152, bf16[64,1024]{1,0:T(8,128)(2,1)S(1)} %get-tuple-element.116, bf16[64,1024]{1,0:T(8,128)(2,1)S(1)} %get-tuple-element.115, bf16[64,1024]{1,0:T(8,128)(2,1)S(1)} %get-tuple-element.151, bf16[1,1024,2048]{2,1,0:T(8,128)(2,1)S(1)} %copy-done.6), kind=kOutput, calls=%fused_computation.2 | convolution fusion | flops 1076363264 | bytes 5767168 | tf_op jit(solution)/shard_map/dot_general | solution.py:224
  21.4 0.9 collective-permute-start.4
  22.3 2.5 %collective-permute-start.14 = (bf16[64,1024]{1,0:T(8,128)(2,1)S(1)}, bf16[64,1024]{1,0:T(8,128)(2,1)S(1)}, u32[]{:S(2)}, u32[]{:S(2)}) collective-permute-start(bf16[64,1024]{1,0:T(8,128)(2,1)S(1)} %get-tuple-element.147), channel_id=1, source_target_pairs={{0,0},{1,4},{2,2},{3,6},{5,5},{4,1},{7,7},{6,3},{8,8},{9,12},{10,1... | collective-permute-start | bytes 393224 | tf_op jit(solution)/shard_map/ppermute | solution.py:139
  24.8 1.3 %collective-permute-start.15 = (bf16[64,1024]{1,0:T(8,128)(2,1)S(1)}, bf16[64,1024]{1,0:T(8,128)(2,1)S(1)}, u32[]{:S(2)}, u32[]{:S(2)}) collective-permute-start(bf16[64,1024]{1,0:T(8,128)(2,1)S(1)} %get-tuple-element.148), channel_id=1, source_target_pairs={{0,2},{1,6},{2,0},{3,4},{5,7},{4,3},{7,5},{6,1},{8,10},{9,14},{10,... | collective-permute-start | bytes 393224 | tf_op jit(solution)/shard_map/ppermute | solution.py:139
  26.3 5.9 %collective-permute-done.4 = bf16[128,2048]{1,0:T(8,128)(2,1)S(1)} collective-permute-done((bf16[128,2048]{1,0:T(8,128)(2,1)S(1)}, bf16[128,2048]{1,0:T(8,128)(2,1)S(1)}, u32[]{:S(2)}, u32[]{:S(2)}) %collective-permute-start.4) | collective-permute-done | bytes 524320 | tf_op jit(solution)/shard_map/ppermute | solution.py:129
  32.5 0.8 collective-permute-start.5
  33.9 1.3 %collective-permute-start.11 = (bf16[64,2048]{1,0:T(8,128)(2,1)S(1)}, bf16[64,2048]{1,0:T(8,128)(2,1)S(1)}, u32[]{:S(2)}, u32[]{:S(2)}) collective-permute-start(bf16[64,2048]{1,0:T(8,128)(2,1)S(1)} %bitcast.48), channel_id=1, source_target_pairs={{8,0},{16,8},{24,16},{9,1},{17,9},{25,17},{10,2},{18,10},{26,18},{... | collective-permute-start | bytes 786440 | tf_op jit(solution)/shard_map/ppermute | solution.py:56
  35.2 1.9 %collective-permute-done.7 = bf16[64,2048]{1,0:T(8,128)(2,1)S(1)} collective-permute-done((bf16[64,2048]{1,0:T(8,128)(2,1)S(1)}, bf16[64,2048]{1,0:T(8,128)(2,1)S(1)}, u32[]{:S(2)}, u32[]{:S(2)}) %collective-permute-start.7) | collective-permute-done | bytes 262176 | tf_op jit(solution)/shard_map/ppermute | solution.py:129
  37.3 2.1 %collective-permute-start.12 = (bf16[64,2048]{1,0:T(8,128)(2,1)S(1)}, bf16[64,2048]{1,0:T(8,128)(2,1)S(1)}, u32[]{:S(2)}, u32[]{:S(2)}) collective-permute-start(bf16[64,2048]{1,0:T(8,128)(2,1)S(1)} %fusion.7), channel_id=1, source_target_pairs={{0,2},{1,5},{2,0},{3,7},{4,6},{5,1},{6,4},{7,3},{8,10},{9,13},{10,... | collective-permute-start | bytes 786440 | tf_op jit(solution)/shard_map/ppermute | solution.py:129
  39.6 3.2 %collective-permute-start.8 = (bf16[64,2048]{1,0:T(8,128)(2,1)S(1)}, bf16[64,2048]{1,0:T(8,128)(2,1)S(1)}, u32[]{:S(2)}, u32[]{:S(2)}) collective-permute-start(bf16[64,2048]{1,0:T(8,128)(2,1)S(1)} %add_convert_fusion.3), channel_id=1, source_target_pairs={{0,8},{8,16},{16,24},{1,9},{9,17},{17,25},{2,10},{10,18},{18,26},{... | collective-permute-start | bytes 786440 | tf_op jit(solution)/shard_map/ppermute | solution.py:56
  43.5 1.1 %collective-permute-start.13 = (bf16[128,2048]{1,0:T(8,128)(2,1)S(1)}, bf16[128,2048]{1,0:T(8,128)(2,1)S(1)}, u32[]{:S(2)}, u32[]{:S(2)}) collective-permute-start(bf16[128,2048]{1,0:T(8,128)(2,1)S(1)} %pad_maximum_fusion), channel_id=1, source_target_pairs={{0,4},{1,3},{2,6},{3,1},{4,0},{5,7},{6,2},{7,5},{8,12},{9,11},{10,... | collective-permute-start | bytes 1572872 | tf_op jit(solution)/shard_map/ppermute | solution.py:129
  44.6 3.6 %collective-permute-done.8 = bf16[64,2048]{1,0:T(8,128)(2,1)S(1)} collective-permute-done((bf16[64,2048]{1,0:T(8,128)(2,1)S(1)}, bf16[64,2048]{1,0:T(8,128)(2,1)S(1)}, u32[]{:S(2)}, u32[]{:S(2)}) %collective-permute-start.8) | collective-permute-done | bytes 262176 | tf_op jit(solution)/shard_map/ppermute | solution.py:56
  48.3 3.2 %collective-permute-start.9 = (bf16[64,1024]{1,0:T(8,128)(2,1)S(1)}, bf16[64,1024]{1,0:T(8,128)(2,1)S(1)}, u32[]{:S(2)}, u32[]{:S(2)}) collective-permute-start(bf16[64,1024]{1,0:T(8,128)(2,1)S(1)} %get-tuple-element.150), channel_id=1, source_target_pairs={{0,0},{1,4},{2,2},{3,6},{5,5},{4,1},{7,7},{6,3},{8,8},{9,12},{10,1... | collective-permute-start | bytes 393224 | tf_op jit(solution)/shard_map/ppermute | solution.py:139
  51.6 1.3 %convolution_convert_fusion.1 = bf16[256,2048]{1,0:T(8,128)(2,1)S(1)} fusion(bf16[64,1024]{1,0:T(8,128)(2,1)S(1)} %get-tuple-element.69, bf16[64,1024]{1,0:T(8,128)(2,1)S(1)} %get-tuple-element.142, bf16[64,1024]{1,0:T(8,128)(2,1)S(1)} %get-tuple-element.141, bf16[64,1024]{1,0:T(8,128)(2,1)S(1)} %get-tuple-element.66, bf16[1,1024,2048]{2,1,0:T(8,128)(2,1)S(1)} %copy-done.6), kind=kOutput, calls=%fused_computation.1 | convolution fusion | flops 1076363264 | bytes 5767168 | tf_op jit(solution)/shard_map/dot_general | solution.py:224
  53.0 1.8 %collective-permute-start.10 = (bf16[64,1024]{1,0:T(8,128)(2,1)S(1)}, bf16[64,1024]{1,0:T(8,128)(2,1)S(1)}, u32[]{:S(2)}, u32[]{:S(2)}) collective-permute-start(bf16[64,1024]{1,0:T(8,128)(2,1)S(1)} %get-tuple-element.149), channel_id=1, source_target_pairs={{0,2},{1,6},{2,0},{3,4},{5,7},{4,3},{7,5},{6,1},{8,10},{9,14},{10,... | collective-permute-start | bytes 393224 | tf_op jit(solution)/shard_map/ppermute | solution.py:139
  54.9 1.3 %convolution_convert_fusion.5 = bf16[256,1024]{1,0:T(8,128)(2,1)S(1)} fusion(bf16[128,2048]{1,0:T(8,128)(2,1)S(1)} %collective-permute-done.13, bf16[128,2048]{1,0:T(8,128)(2,1)S(1)} %pad_maximum_fusion, bf16[1,1024,2048]{2,1,0:T(8,128)(2,1)S(1)} %copy-done.6), kind=kOutput, calls=%fused_computation.5 | convolution fusion | flops 1076101120 | bytes 5767168 | tf_op jit(solution)/shard_map/dot_general | solution.py:252
  56.4 2.2 %all-gather.2 = bf16[256,1024]{1,0:T(8,128)(2,1)S(1)} all-gather(bf16[128,1024]{1,0:T(8,128)(2,1)S(1)} %get-tuple-element.74), channel_id=4, replica_groups=mesh['segment'=4,'row'=4,'col'=2] {'col'}, dimensions={0}, use_global_device_ids=true | all-gather | bytes 786432 | tf_op jit(solution)/shard_map/all_gather | solution.py:262
  58.7 1.3 %collective-permute-start.18 = (bf16[64,1024]{1,0:T(8,128)(2,1)S(1)}, bf16[64,1024]{1,0:T(8,128)(2,1)S(1)}, u32[]{:S(2)}, u32[]{:S(2)}) collective-permute-start(bf16[64,1024]{1,0:T(8,128)(2,1)S(1)} %get-tuple-element.140), channel_id=1, source_target_pairs={{8,0},{9,4},{10,2},{11,6},{13,5},{12,1},{15,7},{14,3},{16,8},{17,1... | collective-permute-start | bytes 393224 | tf_op jit(solution)/shard_map/ppermute | solution.py:147
  60.0 1.3 %collective-permute-start.17 = (bf16[64,1024]{1,0:T(8,128)(2,1)S(1)}, bf16[64,1024]{1,0:T(8,128)(2,1)S(1)}, u32[]{:S(2)}, u32[]{:S(2)}) collective-permute-start(bf16[64,1024]{1,0:T(8,128)(2,1)S(1)} %get-tuple-element.139), channel_id=1, source_target_pairs={{8,2},{9,6},{10,0},{11,4},{13,7},{12,3},{15,5},{14,1},{16,10},{17,... | collective-permute-start | bytes 393224 | tf_op jit(solution)/shard_map/ppermute | solution.py:147
  61.5 1.4 %collective-permute-start.20 = (bf16[64,2048]{1,0:T(8,128)(2,1)S(1)}, bf16[64,2048]{1,0:T(8,128)(2,1)S(1)}, u32[]{:S(2)}, u32[]{:S(2)}) collective-permute-start(bf16[64,2048]{1,0:T(8,128)(2,1)S(1)} %split.333), channel_id=1, source_target_pairs={{0,4},{1,3},{2,6},{3,1},{4,0},{5,7},{6,2},{7,5},{8,12},{9,11},{10,... | collective-permute-start | bytes 786440 | tf_op jit(solution)/shard_map/ppermute | solution.py:129
  62.9 4.6 %collective-permute-done.18 = bf16[64,1024]{1,0:T(8,128)(2,1)S(1)} collective-permute-done((bf16[64,1024]{1,0:T(8,128)(2,1)S(1)}, bf16[64,1024]{1,0:T(8,128)(2,1)S(1)}, u32[]{:S(2)}, u32[]{:S(2)}) %collective-permute-start.18) | collective-permute-done | bytes 131104 | tf_op jit(solution)/shard_map/ppermute | solution.py:147
  67.5 3.2 %collective-permute-done.17 = bf16[64,1024]{1,0:T(8,128)(2,1)S(1)} collective-permute-done((bf16[64,1024]{1,0:T(8,128)(2,1)S(1)}, bf16[64,1024]{1,0:T(8,128)(2,1)S(1)}, u32[]{:S(2)}, u32[]{:S(2)}) %collective-permute-start.17) | collective-permute-done | bytes 131104 | tf_op jit(solution)/shard_map/ppermute | solution.py:147
  71.6 1.5 %collective-permute-start.23 = (bf16[64,2048]{1,0:T(8,128)(2,1)S(1)}, bf16[64,2048]{1,0:T(8,128)(2,1)S(1)}, u32[]{:S(2)}, u32[]{:S(2)}) collective-permute-start(bf16[64,2048]{1,0:T(8,128)(2,1)S(1)} %get-tuple-element.94), channel_id=1, source_target_pairs={{0,4},{1,3},{2,6},{3,1},{4,0},{5,7},{6,2},{7,5},{8,12},{9,11},{10,... | collective-permute-start | bytes 786440 | tf_op jit(solution)/shard_map/ppermute | solution.py:129
  73.3 1.3 %convolution_convert_fusion = bf16[256,2048]{1,0:T(8,128)(2,1)S(1)} fusion(bf16[64,1024]{1,0:T(8,128)(2,1)S(1)} %get-tuple-element.82, bf16[64,1024]{1,0:T(8,128)(2,1)S(1)} %get-tuple-element.132, bf16[64,1024]{1,0:T(8,128)(2,1)S(1)} %get-tuple-element.131, bf16[64,1024]{1,0:T(8,128)(2,1)S(1)} %get-tuple-element.79, bf16[1,1024,2048]{2,1,0:T(8,128)(2,1)S(1)} %copy-done.6), kind=kOutput, calls=%fused_computation | convolution fusion | flops 1076363264 | bytes 5767168 | tf_op jit(solution)/shard_map/dot_general | solution.py:224
  74.6 0.9 collective-permute-start.22
  75.5 3.4 %collective-permute-start.28 = (bf16[64,1024]{1,0:T(8,128)(2,1)S(1)}, bf16[64,1024]{1,0:T(8,128)(2,1)S(1)}, u32[]{:S(2)}, u32[]{:S(2)}) collective-permute-start(bf16[64,1024]{1,0:T(8,128)(2,1)S(1)} %get-tuple-element.139), channel_id=1, source_target_pairs={{0,2},{1,6},{2,0},{3,4},{5,7},{4,3},{7,5},{6,1}} | collective-permute-start | bytes 393224 | tf_op jit(solution)/shard_map/ppermute | solution.py:147
  79.0 3.0 %collective-permute-start.29 = (bf16[64,1024]{1,0:T(8,128)(2,1)S(1)}, bf16[64,1024]{1,0:T(8,128)(2,1)S(1)}, u32[]{:S(2)}, u32[]{:S(2)}) collective-permute-start(bf16[64,1024]{1,0:T(8,128)(2,1)S(1)} %get-tuple-element.140), channel_id=1, source_target_pairs={{0,0},{1,4},{2,2},{3,6},{5,5},{4,1},{7,7},{6,3}} | collective-permute-start | bytes 393224 | tf_op jit(solution)/shard_map/ppermute | solution.py:147
  82.1 4.7 %collective-permute-done.28 = bf16[64,1024]{1,0:T(8,128)(2,1)S(1)} collective-permute-done((bf16[64,1024]{1,0:T(8,128)(2,1)S(1)}, bf16[64,1024]{1,0:T(8,128)(2,1)S(1)}, u32[]{:S(2)}, u32[]{:S(2)}) %collective-permute-start.28) | collective-permute-done | bytes 131104 | tf_op jit(solution)/shard_map/ppermute | solution.py:147
  86.9 0.9 collective-permute-done.29
  88.0 1.3 %collective-permute-start.27 = (bf16[64,2048]{1,0:T(8,128)(2,1)S(1)}, bf16[64,2048]{1,0:T(8,128)(2,1)S(1)}, u32[]{:S(2)}, u32[]{:S(2)}) collective-permute-start(bf16[64,2048]{1,0:T(8,128)(2,1)S(1)} %get-tuple-element.90), channel_id=1, source_target_pairs={{0,8},{8,16},{16,24},{1,9},{9,17},{17,25},{2,10},{10,18},{18,26},{... | collective-permute-start | bytes 786440 | tf_op jit(solution)/shard_map/ppermute | solution.py:56
  89.3 3.0 %collective-permute-done.25 = bf16[128,2048]{1,0:T(8,128)(2,1)S(1)} collective-permute-done((bf16[128,2048]{1,0:T(8,128)(2,1)S(1)}, bf16[128,2048]{1,0:T(8,128)(2,1)S(1)}, u32[]{:S(2)}, u32[]{:S(2)}) %collective-permute-start.25) | collective-permute-done | bytes 524320 | tf_op jit(solution)/shard_map/ppermute | solution.py:129
  92.3 1.3 %convolution_convert_fusion.4 = bf16[256,1024]{1,0:T(8,128)(2,1)S(1)} fusion(bf16[128,2048]{1,0:T(8,128)(2,1)S(1)} %collective-permute-done.25, bf16[128,2048]{1,0:T(8,128)(2,1)S(1)} %pad_maximum_fusion.1, bf16[1,1024,2048]{2,1,0:T(8,128)(2,1)S(1)} %copy-done.6), kind=kOutput, calls=%fused_computation.4 | convolution fusion | flops 1076101120 | bytes 5767168 | tf_op jit(solution)/shard_map/dot_general | solution.py:252
  93.9 1.6 %collective-permute-start.24 = (bf16[64,2048]{1,0:T(8,128)(2,1)S(1)}, bf16[64,2048]{1,0:T(8,128)(2,1)S(1)}, u32[]{:S(2)}, u32[]{:S(2)}) collective-permute-start(bf16[64,2048]{1,0:T(8,128)(2,1)S(1)} %split.332), channel_id=1, source_target_pairs={{0,4},{1,3},{2,6},{3,1},{4,0},{5,7},{6,2},{7,5},{8,12},{9,11},{10,... | collective-permute-start | bytes 786440 | tf_op jit(solution)/shard_map/ppermute | solution.py:129
  95.6 2.0 %collective-permute-start.30 = (bf16[64,1024]{1,0:T(8,128)(2,1)S(1)}, bf16[64,1024]{1,0:T(8,128)(2,1)S(1)}, u32[]{:S(2)}, u32[]{:S(2)}) collective-permute-start(bf16[64,1024]{1,0:T(8,128)(2,1)S(1)} %get-tuple-element.127), channel_id=1, source_target_pairs={{0,2},{1,6},{2,0},{3,4},{5,7},{4,3},{7,5},{6,1},{8,10},{9,14},{10,... | collective-permute-start | bytes 393224 | tf_op jit(solution)/shard_map/ppermute | solution.py:139
  97.5 2.5 %collective-permute-start.31 = (bf16[64,1024]{1,0:T(8,128)(2,1)S(1)}, bf16[64,1024]{1,0:T(8,128)(2,1)S(1)}, u32[]{:S(2)}, u32[]{:S(2)}) collective-permute-start(bf16[64,1024]{1,0:T(8,128)(2,1)S(1)} %get-tuple-element.128), channel_id=1, source_target_pairs={{0,0},{1,4},{2,2},{3,6},{5,5},{4,1},{7,7},{6,3},{8,8},{9,12},{10,1... | collective-permute-start | bytes 393224 | tf_op jit(solution)/shard_map/ppermute | solution.py:139
  100.3 0.8 maximum_bitcast_fusion
  101.2 1.2 %collective-permute-done.30 = bf16[64,1024]{1,0:T(8,128)(2,1)S(1)} collective-permute-done((bf16[64,1024]{1,0:T(8,128)(2,1)S(1)}, bf16[64,1024]{1,0:T(8,128)(2,1)S(1)}, u32[]{:S(2)}, u32[]{:S(2)}) %collective-permute-start.30) | collective-permute-done | bytes 131104 | tf_op jit(solution)/shard_map/ppermute | solution.py:139
  102.4 1.4 %collective-permute-done.31 = bf16[64,1024]{1,0:T(8,128)(2,1)S(1)} collective-permute-done((bf16[64,1024]{1,0:T(8,128)(2,1)S(1)}, bf16[64,1024]{1,0:T(8,128)(2,1)S(1)}, u32[]{:S(2)}, u32[]{:S(2)}) %collective-permute-start.31) | collective-permute-done | bytes 131104 | tf_op jit(solution)/shard_map/ppermute | solution.py:139
  103.9 0.8 copy-done.2
  (96 shorter events, 5.8 us)
Async XLA Ops:
  1.7 10.3 %collective-permute-start.1 = (bf16[64,1024]{1,0:T(8,128)(2,1)S(1)}, bf16[64,1024]{1,0:T(8,128)(2,1)S(1)}, u32[]{:S(2)}, u32[]{:S(2)}) collective-permute-start(bf16[64,1024]{1,0:T(8,128)(2,1)S(1)} %get-tuple-element.156), channel_id=1, source_target_pairs={{0,0},{1,4},{2,2},{3,6},{5,5},{4,1},{7,7},{6,3},{8,8},{9,12},{10,1... | collective-permute-start | bytes 393224 | tf_op jit(solution)/shard_map/ppermute | solution.py:139
  6.3 6.1 %collective-permute-start.2 = (bf16[64,1024]{1,0:T(8,128)(2,1)S(1)}, bf16[64,1024]{1,0:T(8,128)(2,1)S(1)}, u32[]{:S(2)}, u32[]{:S(2)}) collective-permute-start(bf16[64,1024]{1,0:T(8,128)(2,1)S(1)} %get-tuple-element.155), channel_id=1, source_target_pairs={{0,2},{1,6},{2,0},{3,4},{5,7},{4,3},{7,5},{6,1},{8,10},{9,14},{10,... | collective-permute-start | bytes 393224 | tf_op jit(solution)/shard_map/ppermute | solution.py:139
  8.3 8.0 %collective-permute-start = (bf16[64,1024]{1,0:T(8,128)(2,1)S(1)}, bf16[64,1024]{1,0:T(8,128)(2,1)S(1)}, u32[]{:S(2)}, u32[]{:S(2)}) collective-permute-start(bf16[64,1024]{1,0:T(8,128)(2,1)S(1)} %get-tuple-element.157), channel_id=1, source_target_pairs={{0,0},{1,4},{2,2},{3,6},{5,5},{4,1},{7,7},{6,3},{8,8},{9,12},{10,1... | collective-permute-start | bytes 393224 | tf_op jit(solution)/shard_map/ppermute | solution.py:139
  11.9 5.4 %collective-permute-start.3 = (bf16[64,1024]{1,0:T(8,128)(2,1)S(1)}, bf16[64,1024]{1,0:T(8,128)(2,1)S(1)}, u32[]{:S(2)}, u32[]{:S(2)}) collective-permute-start(bf16[64,1024]{1,0:T(8,128)(2,1)S(1)} %get-tuple-element.158), channel_id=1, source_target_pairs={{0,2},{1,6},{2,0},{3,4},{5,7},{4,3},{7,5},{6,1},{8,10},{9,14},{10,... | collective-permute-start | bytes 393224 | tf_op jit(solution)/shard_map/ppermute | solution.py:139
  12.1 2.9 %copy-start.6 = (bf16[1,1024,2048]{2,1,0:T(8,128)(2,1)S(1)}, bf16[1,1024,2048]{2,1,0:T(8,128)(2,1)}, u32[]{:S(2)}) copy-start(bf16[1,1024,2048]{2,1,0:T(8,128)(2,1)} %param.7) | copy-start | bytes 12582916
  16.3 9.8 %collective-permute-start.6 = (bf16[128,2048]{1,0:T(8,128)(2,1)S(1)}, bf16[128,2048]{1,0:T(8,128)(2,1)S(1)}, u32[]{:S(2)}, u32[]{:S(2)}) collective-permute-start(bf16[128,2048]{1,0:T(8,128)(2,1)S(1)} %split.238), channel_id=1, source_target_pairs={{0,4},{1,3},{2,6},{3,1},{4,0},{5,7},{6,2},{7,5},{8,12},{9,11},{10,... | collective-permute-start | bytes 1572872 | tf_op jit(solution)/shard_map/ppermute | solution.py:129
  21.3 12.6 %copy-start = (bf16[1,64,2048]{2,1,0:T(8,128)(2,1)S(1)}, bf16[1,64,2048]{2,1,0:T(8,128)(2,1)}, u32[]{:S(2)}) copy-start(bf16[1,64,2048]{2,1,0:T(8,128)(2,1)} %param.11) | copy-start | bytes 786436
  21.3 15.8 %copy-start.5 = (f32[1,2048]{1,0:T(1,128)S(1)}, f32[1,2048]{1,0:T(1,128)}, u32[]{:S(2)}) copy-start(f32[1,2048]{1,0:T(1,128)} %param.8) | copy-start | bytes 24580
  21.3 18.1 %copy-start.1 = (bf16[1,64,2048]{2,1,0:T(8,128)(2,1)S(1)}, bf16[1,64,2048]{2,1,0:T(8,128)(2,1)}, u32[]{:S(2)}) copy-start(bf16[1,64,2048]{2,1,0:T(8,128)(2,1)} %param.9) | copy-start | bytes 786436
  21.4 10.9 %collective-permute-start.4 = (bf16[128,2048]{1,0:T(8,128)(2,1)S(1)}, bf16[128,2048]{1,0:T(8,128)(2,1)S(1)}, u32[]{:S(2)}, u32[]{:S(2)}) collective-permute-start(bf16[128,2048]{1,0:T(8,128)(2,1)S(1)} %split.244), channel_id=1, source_target_pairs={{0,2},{1,5},{2,0},{3,7},{4,6},{5,1},{6,4},{7,3},{8,10},{9,13},{10,... | collective-permute-start | bytes 1572872 | tf_op jit(solution)/shard_map/ppermute | solution.py:129
  22.3 11.0 %collective-permute-start.14 = (bf16[64,1024]{1,0:T(8,128)(2,1)S(1)}, bf16[64,1024]{1,0:T(8,128)(2,1)S(1)}, u32[]{:S(2)}, u32[]{:S(2)}) collective-permute-start(bf16[64,1024]{1,0:T(8,128)(2,1)S(1)} %get-tuple-element.147), channel_id=1, source_target_pairs={{0,0},{1,4},{2,2},{3,6},{5,5},{4,1},{7,7},{6,3},{8,8},{9,12},{10,1... | collective-permute-start | bytes 393224 | tf_op jit(solution)/shard_map/ppermute | solution.py:139
  24.8 8.8 %collective-permute-start.15 = (bf16[64,1024]{1,0:T(8,128)(2,1)S(1)}, bf16[64,1024]{1,0:T(8,128)(2,1)S(1)}, u32[]{:S(2)}, u32[]{:S(2)}) collective-permute-start(bf16[64,1024]{1,0:T(8,128)(2,1)S(1)} %get-tuple-element.148), channel_id=1, source_target_pairs={{0,2},{1,6},{2,0},{3,4},{5,7},{4,3},{7,5},{6,1},{8,10},{9,14},{10,... | collective-permute-start | bytes 393224 | tf_op jit(solution)/shard_map/ppermute | solution.py:139
  26.3 10.8 %collective-permute-start.7 = (bf16[64,2048]{1,0:T(8,128)(2,1)S(1)}, bf16[64,2048]{1,0:T(8,128)(2,1)S(1)}, u32[]{:S(2)}, u32[]{:S(2)}) collective-permute-start(bf16[64,2048]{1,0:T(8,128)(2,1)S(1)} %split.334), channel_id=1, source_target_pairs={{0,2},{1,5},{2,0},{3,7},{4,6},{5,1},{6,4},{7,3},{8,10},{9,13},{10,... | collective-permute-start | bytes 786440 | tf_op jit(solution)/shard_map/ppermute | solution.py:129
  32.4 15.8 %copy-start.3 = (bf16[64,2048]{1,0:T(8,128)(2,1)S(1)}, bf16[64,2048]{1,0:T(8,128)(2,1)}, u32[]{:S(2)}) copy-start(bf16[64,2048]{1,0:T(8,128)(2,1)} %param.10) | copy-start | bytes 786436
  32.5 7.0 %collective-permute-start.5 = (bf16[64,2048]{1,0:T(8,128)(2,1)S(1)}, bf16[64,2048]{1,0:T(8,128)(2,1)S(1)}, u32[]{:S(2)}, u32[]{:S(2)}) collective-permute-start(bf16[64,2048]{1,0:T(8,128)(2,1)S(1)} %split.335), channel_id=1, source_target_pairs={{0,4},{1,3},{2,6},{3,1},{4,0},{5,7},{6,2},{7,5},{8,12},{9,11},{10,... | collective-permute-start | bytes 786440 | tf_op jit(solution)/shard_map/ppermute | solution.py:129
  33.7 5.9 %collective-permute-start.16 = (bf16[128,1024]{1,0:T(8,128)(2,1)S(1)}, bf16[128,1024]{1,0:T(8,128)(2,1)S(1)}, u32[]{:S(2)}, u32[]{:S(2)}) collective-permute-start(bf16[128,1024]{1,0:T(8,128)(2,1)S(1)} %pad_maximum_fusion.5), channel_id=1, source_target_pairs={{0,1},{1,0},{2,3},{3,2},{4,5},{5,4},{6,7},{7,6},{8,9},{9,8},{10,11... | collective-permute-start | bytes 786440 | tf_op jit(solution)/shard_map/ppermute | solution.py:81
  33.9 19.1 %collective-permute-start.11 = (bf16[64,2048]{1,0:T(8,128)(2,1)S(1)}, bf16[64,2048]{1,0:T(8,128)(2,1)S(1)}, u32[]{:S(2)}, u32[]{:S(2)}) collective-permute-start(bf16[64,2048]{1,0:T(8,128)(2,1)S(1)} %bitcast.48), channel_id=1, source_target_pairs={{8,0},{16,8},{24,16},{9,1},{17,9},{25,17},{10,2},{18,10},{26,18},{... | collective-permute-start | bytes 786440 | tf_op jit(solution)/shard_map/ppermute | solution.py:56
  37.3 6.1 %collective-permute-start.12 = (bf16[64,2048]{1,0:T(8,128)(2,1)S(1)}, bf16[64,2048]{1,0:T(8,128)(2,1)S(1)}, u32[]{:S(2)}, u32[]{:S(2)}) collective-permute-start(bf16[64,2048]{1,0:T(8,128)(2,1)S(1)} %fusion.7), channel_id=1, source_target_pairs={{0,2},{1,5},{2,0},{3,7},{4,6},{5,1},{6,4},{7,3},{8,10},{9,13},{10,... | collective-permute-start | bytes 786440 | tf_op jit(solution)/shard_map/ppermute | solution.py:129
  39.6 8.6 %collective-permute-start.8 = (bf16[64,2048]{1,0:T(8,128)(2,1)S(1)}, bf16[64,2048]{1,0:T(8,128)(2,1)S(1)}, u32[]{:S(2)}, u32[]{:S(2)}) collective-permute-start(bf16[64,2048]{1,0:T(8,128)(2,1)S(1)} %add_convert_fusion.3), channel_id=1, source_target_pairs={{0,8},{8,16},{16,24},{1,9},{9,17},{17,25},{2,10},{10,18},{18,26},{... | collective-permute-start | bytes 786440 | tf_op jit(solution)/shard_map/ppermute | solution.py:56
  43.5 11.4 %collective-permute-start.13 = (bf16[128,2048]{1,0:T(8,128)(2,1)S(1)}, bf16[128,2048]{1,0:T(8,128)(2,1)S(1)}, u32[]{:S(2)}, u32[]{:S(2)}) collective-permute-start(bf16[128,2048]{1,0:T(8,128)(2,1)S(1)} %pad_maximum_fusion), channel_id=1, source_target_pairs={{0,4},{1,3},{2,6},{3,1},{4,0},{5,7},{6,2},{7,5},{8,12},{9,11},{10,... | collective-permute-start | bytes 1572872 | tf_op jit(solution)/shard_map/ppermute | solution.py:129
  48.3 6.6 %collective-permute-start.9 = (bf16[64,1024]{1,0:T(8,128)(2,1)S(1)}, bf16[64,1024]{1,0:T(8,128)(2,1)S(1)}, u32[]{:S(2)}, u32[]{:S(2)}) collective-permute-start(bf16[64,1024]{1,0:T(8,128)(2,1)S(1)} %get-tuple-element.150), channel_id=1, source_target_pairs={{0,0},{1,4},{2,2},{3,6},{5,5},{4,1},{7,7},{6,3},{8,8},{9,12},{10,1... | collective-permute-start | bytes 393224 | tf_op jit(solution)/shard_map/ppermute | solution.py:139
  52.9 8.4 %collective-permute-start.19 = (bf16[128,2048]{1,0:T(8,128)(2,1)S(1)}, bf16[128,2048]{1,0:T(8,128)(2,1)S(1)}, u32[]{:S(2)}, u32[]{:S(2)}) collective-permute-start(bf16[128,2048]{1,0:T(8,128)(2,1)S(1)} %split.261), channel_id=1, source_target_pairs={{0,2},{1,5},{2,0},{3,7},{4,6},{5,1},{6,4},{7,3},{8,10},{9,13},{10,... | collective-permute-start | bytes 1572872 | tf_op jit(solution)/shard_map/ppermute | solution.py:129
  53.0 18.2 %collective-permute-start.10 = (bf16[64,1024]{1,0:T(8,128)(2,1)S(1)}, bf16[64,1024]{1,0:T(8,128)(2,1)S(1)}, u32[]{:S(2)}, u32[]{:S(2)}) collective-permute-start(bf16[64,1024]{1,0:T(8,128)(2,1)S(1)} %get-tuple-element.149), channel_id=1, source_target_pairs={{0,2},{1,6},{2,0},{3,4},{5,7},{4,3},{7,5},{6,1},{8,10},{9,14},{10,... | collective-permute-start | bytes 393224 | tf_op jit(solution)/shard_map/ppermute | solution.py:139
  56.2 14.6 %copy-start.4 = (bf16[64,2048]{1,0:T(8,128)(2,1)S(1)}, bf16[64,2048]{1,0:T(8,128)(2,1)}, u32[]{:S(2)}) copy-start(bf16[64,2048]{1,0:T(8,128)(2,1)} %param.12) | copy-start | bytes 786436
  58.7 8.9 %collective-permute-start.18 = (bf16[64,1024]{1,0:T(8,128)(2,1)S(1)}, bf16[64,1024]{1,0:T(8,128)(2,1)S(1)}, u32[]{:S(2)}, u32[]{:S(2)}) collective-permute-start(bf16[64,1024]{1,0:T(8,128)(2,1)S(1)} %get-tuple-element.140), channel_id=1, source_target_pairs={{8,0},{9,4},{10,2},{11,6},{13,5},{12,1},{15,7},{14,3},{16,8},{17,1... | collective-permute-start | bytes 393224 | tf_op jit(solution)/shard_map/ppermute | solution.py:147
  60.0 10.8 %collective-permute-start.17 = (bf16[64,1024]{1,0:T(8,128)(2,1)S(1)}, bf16[64,1024]{1,0:T(8,128)(2,1)S(1)}, u32[]{:S(2)}, u32[]{:S(2)}) collective-permute-start(bf16[64,1024]{1,0:T(8,128)(2,1)S(1)} %get-tuple-element.139), channel_id=1, source_target_pairs={{8,2},{9,6},{10,0},{11,4},{13,7},{12,3},{15,5},{14,1},{16,10},{17,... | collective-permute-start | bytes 393224 | tf_op jit(solution)/shard_map/ppermute | solution.py:147
  61.5 9.3 %collective-permute-start.20 = (bf16[64,2048]{1,0:T(8,128)(2,1)S(1)}, bf16[64,2048]{1,0:T(8,128)(2,1)S(1)}, u32[]{:S(2)}, u32[]{:S(2)}) collective-permute-start(bf16[64,2048]{1,0:T(8,128)(2,1)S(1)} %split.333), channel_id=1, source_target_pairs={{0,4},{1,3},{2,6},{3,1},{4,0},{5,7},{6,2},{7,5},{8,12},{9,11},{10,... | collective-permute-start | bytes 786440 | tf_op jit(solution)/shard_map/ppermute | solution.py:129
  71.2 1.9 %collective-permute-start.21 = (bf16[128,1024]{1,0:T(8,128)(2,1)S(1)}, bf16[128,1024]{1,0:T(8,128)(2,1)S(1)}, u32[]{:S(2)}, u32[]{:S(2)}) collective-permute-start(bf16[128,1024]{1,0:T(8,128)(2,1)S(1)} %constant_dynamic-update-slice_fusion), channel_id=1, source_target_pairs={{0,1},{1,0},{2,3},{3,2},{4,5},{5,4},{6,7},{7,6},{8,9},{9,8},{10,11... | collective-permute-start | bytes 786440 | tf_op jit(solution)/shard_map/ppermute | solution.py:81
  71.6 10.4 %collective-permute-start.23 = (bf16[64,2048]{1,0:T(8,128)(2,1)S(1)}, bf16[64,2048]{1,0:T(8,128)(2,1)S(1)}, u32[]{:S(2)}, u32[]{:S(2)}) collective-permute-start(bf16[64,2048]{1,0:T(8,128)(2,1)S(1)} %get-tuple-element.94), channel_id=1, source_target_pairs={{0,4},{1,3},{2,6},{3,1},{4,0},{5,7},{6,2},{7,5},{8,12},{9,11},{10,... | collective-permute-start | bytes 786440 | tf_op jit(solution)/shard_map/ppermute | solution.py:129
  74.6 13.2 %collective-permute-start.22 = (bf16[128,2048]{1,0:T(8,128)(2,1)S(1)}, bf16[128,2048]{1,0:T(8,128)(2,1)S(1)}, u32[]{:S(2)}, u32[]{:S(2)}) collective-permute-start(bf16[128,2048]{1,0:T(8,128)(2,1)S(1)} %split.269), channel_id=1, source_target_pairs={{0,2},{1,5},{2,0},{3,7},{4,6},{5,1},{6,4},{7,3},{8,10},{9,13},{10,... | collective-permute-start | bytes 1572872 | tf_op jit(solution)/shard_map/ppermute | solution.py:129
  75.5 11.3 %collective-permute-start.28 = (bf16[64,1024]{1,0:T(8,128)(2,1)S(1)}, bf16[64,1024]{1,0:T(8,128)(2,1)S(1)}, u32[]{:S(2)}, u32[]{:S(2)}) collective-permute-start(bf16[64,1024]{1,0:T(8,128)(2,1)S(1)} %get-tuple-element.139), channel_id=1, source_target_pairs={{0,2},{1,6},{2,0},{3,4},{5,7},{4,3},{7,5},{6,1}} | collective-permute-start | bytes 393224 | tf_op jit(solution)/shard_map/ppermute | solution.py:147
  79.0 8.8 %collective-permute-start.29 = (bf16[64,1024]{1,0:T(8,128)(2,1)S(1)}, bf16[64,1024]{1,0:T(8,128)(2,1)S(1)}, u32[]{:S(2)}, u32[]{:S(2)}) collective-permute-start(bf16[64,1024]{1,0:T(8,128)(2,1)S(1)} %get-tuple-element.140), channel_id=1, source_target_pairs={{0,0},{1,4},{2,2},{3,6},{5,5},{4,1},{7,7},{6,3}} | collective-permute-start | bytes 393224 | tf_op jit(solution)/shard_map/ppermute | solution.py:147
  82.0 10.2 %collective-permute-start.25 = (bf16[128,2048]{1,0:T(8,128)(2,1)S(1)}, bf16[128,2048]{1,0:T(8,128)(2,1)S(1)}, u32[]{:S(2)}, u32[]{:S(2)}) collective-permute-start(bf16[128,2048]{1,0:T(8,128)(2,1)S(1)} %pad_maximum_fusion.1), channel_id=1, source_target_pairs={{0,2},{1,5},{2,0},{3,7},{4,6},{5,1},{6,4},{7,3},{8,10},{9,13},{10,... | collective-permute-start | bytes 1572872 | tf_op jit(solution)/shard_map/ppermute | solution.py:129
  88.0 7.5 %collective-permute-start.27 = (bf16[64,2048]{1,0:T(8,128)(2,1)S(1)}, bf16[64,2048]{1,0:T(8,128)(2,1)S(1)}, u32[]{:S(2)}, u32[]{:S(2)}) collective-permute-start(bf16[64,2048]{1,0:T(8,128)(2,1)S(1)} %get-tuple-element.90), channel_id=1, source_target_pairs={{0,8},{8,16},{16,24},{1,9},{9,17},{17,25},{2,10},{10,18},{18,26},{... | collective-permute-start | bytes 786440 | tf_op jit(solution)/shard_map/ppermute | solution.py:56
  93.7 1.7 %collective-permute-start.26 = (bf16[128,1024]{1,0:T(8,128)(2,1)S(1)}, bf16[128,1024]{1,0:T(8,128)(2,1)S(1)}, u32[]{:S(2)}, u32[]{:S(2)}) collective-permute-start(bf16[128,1024]{1,0:T(8,128)(2,1)S(1)} %get-tuple-element.89), channel_id=1, source_target_pairs={{0,1},{1,0},{2,3},{3,2},{4,5},{5,4},{6,7},{7,6},{8,9},{9,8},{10,11... | collective-permute-start | bytes 786440 | tf_op jit(solution)/shard_map/ppermute | solution.py:81
  93.9 6.3 %collective-permute-start.24 = (bf16[64,2048]{1,0:T(8,128)(2,1)S(1)}, bf16[64,2048]{1,0:T(8,128)(2,1)S(1)}, u32[]{:S(2)}, u32[]{:S(2)}) collective-permute-start(bf16[64,2048]{1,0:T(8,128)(2,1)S(1)} %split.332), channel_id=1, source_target_pairs={{0,4},{1,3},{2,6},{3,1},{4,0},{5,7},{6,2},{7,5},{8,12},{9,11},{10,... | collective-permute-start | bytes 786440 | tf_op jit(solution)/shard_map/ppermute | solution.py:129
  95.6 6.8 %collective-permute-start.30 = (bf16[64,1024]{1,0:T(8,128)(2,1)S(1)}, bf16[64,1024]{1,0:T(8,128)(2,1)S(1)}, u32[]{:S(2)}, u32[]{:S(2)}) collective-permute-start(bf16[64,1024]{1,0:T(8,128)(2,1)S(1)} %get-tuple-element.127), channel_id=1, source_target_pairs={{0,2},{1,6},{2,0},{3,4},{5,7},{4,3},{7,5},{6,1},{8,10},{9,14},{10,... | collective-permute-start | bytes 393224 | tf_op jit(solution)/shard_map/ppermute | solution.py:139
  97.5 6.3 %collective-permute-start.31 = (bf16[64,1024]{1,0:T(8,128)(2,1)S(1)}, bf16[64,1024]{1,0:T(8,128)(2,1)S(1)}, u32[]{:S(2)}, u32[]{:S(2)}) collective-permute-start(bf16[64,1024]{1,0:T(8,128)(2,1)S(1)} %get-tuple-element.128), channel_id=1, source_target_pairs={{0,0},{1,4},{2,2},{3,6},{5,5},{4,1},{7,7},{6,3},{8,8},{9,12},{10,1... | collective-permute-start | bytes 393224 | tf_op jit(solution)/shard_map/ppermute | solution.py:139
  103.9 0.8 copy-start.2

commit v7 on v6

--- a/solution.py
+++ b/solution.py
@@ -320,7 +320,8 @@
     last_back = deliver("D1", "G1_s")
     rule("gr2", lambda: retreat(flow("up"), last_back()))
 
-    layer_outputs = jnp.stack([flow("out1"), flow("out2")], axis=0)[None]
+    first_outputs = fixed(jnp.stack([flow("out1"), flow("feed")], axis=0))
+    layer_outputs = lax.dynamic_update_index_in_dim(first_outputs, flow("out2"), 1, 0)[None]
     first_half = fixed(jnp.stack([flow("gr1"), flow("up")], axis=0))
     input_grads = lax.dynamic_update_index_in_dim(first_half, flow("gr2"), 1, 0)[None]
     return (layer_outputs, input_grads)

time: 105 us -> 105 us (level)
  transfers between devices with their start and end apart: 32 -> 32, of which waited for: 15 -> 16; matrix products, arithmetic and copies ran while one was open for 12% -> 11% of each run, Pallas kernels for 0% -> 0%
where the time goes in v7:
time: 105 us
  starting transfers between devices  49.4 us (47%)
  waiting for transfers between devices  32.9 us (31%)
  matrix products  7.68 us (7%)
  blocking collectives  7.12 us (7%)
  other arithmetic  3.82 us (4%)
  local copies, waits for them, and re-layouts  2.36 us (2%)
  between operations  1.38 us (1%)
    ppermute x10, starting transfers between devices, across(): return lax.ppermute(value, ('row', 'col'), pairs)  22.5 us
    ppermute x4, waiting for transfers between devices, across(): return lax.ppermute(value, ('segment', 'row', 'col'), pairs)  13.5 us
    ppermute x12, waiting for transfers between devices, step_swap(): return lax.ppermute(value, ('row', 'col'), pairs)  11.5 us
    ppermute x12, starting transfers between devices, step_swap(): return lax.ppermute(value, ('row', 'col'), pairs)  11.4 us
    ppermute x4, starting transfers between devices, across(): return lax.ppermute(value, ('segment', 'row', 'col'), pairs)  9.02 us
    ppermute x3, starting transfers between devices, passed_along(): lax.ppermute(value, 'segment', [(source, source + steps) for source in ra...  5.8 us
    dot_general x4, matrix products, multiplied(): jnp.dot(full, flow('weight'), preferred_element_type=F32).astype(BF16)  5.11 us
    all_gather x2, blocking collectives, others(): halves = lax.all_gather(half, 'col', axis=0, tiled=False)  4.94 us
  transfers between devices with their start and end apart: 32, of which 16 were waited for; matrix products, arithmetic and copies ran while one was open for 11% of the time, Pallas kernels for 0%

profile of v7, /device:TPU:1, one launch (start us, length us, event | category | flops | bytes accessed | tf_op | source)
XLA Modules:
  0.0 104.8 jit_solution(10631279861435326842)
XLA Ops:
  0.6 1.1 %slice_bitcast_fusion = (bf16[64,2048]{1,0:T(8,128)(2,1)S(1)}, bf16[64,2048]{1,0:T(8,128)(2,1)S(1)}) fusion(bf16[1,2,64,2048]{3,2,1,0:T(8,128)(2,1)} %param.13), kind=kLoop, calls=%fused_computation.86 | loop fusion | bytes 1048576 | tf_op jit(solution)/shard_map/squeeze | solution.py:296
  1.7 4.5 %collective-permute-start.1 = (bf16[64,1024]{1,0:T(8,128)(2,1)S(1)}, bf16[64,1024]{1,0:T(8,128)(2,1)S(1)}, u32[]{:S(2)}, u32[]{:S(2)}) collective-permute-start(bf16[64,1024]{1,0:T(8,128)(2,1)S(1)} %get-tuple-element.156), channel_id=1, source_target_pairs={{0,0},{1,4},{2,2},{3,6},{5,5},{4,1},{7,7},{6,3},{8,8},{9,12},{10,1... | collective-permute-start | bytes 393224 | tf_op jit(solution)/shard_map/ppermute | solution.py:139
  6.3 1.0 collective-permute-start.2
  7.3 1.0 broadcast_select_fusion.34
  8.3 3.6 %collective-permute-start = (bf16[64,1024]{1,0:T(8,128)(2,1)S(1)}, bf16[64,1024]{1,0:T(8,128)(2,1)S(1)}, u32[]{:S(2)}, u32[]{:S(2)}) collective-permute-start(bf16[64,1024]{1,0:T(8,128)(2,1)S(1)} %get-tuple-element.157), channel_id=1, source_target_pairs={{0,0},{1,4},{2,2},{3,6},{5,5},{4,1},{7,7},{6,3},{8,8},{9,12},{10,1... | collective-permute-start | bytes 393224 | tf_op jit(solution)/shard_map/ppermute | solution.py:139
  12.5 2.3 %all-gather = bf16[256,1024]{1,0:T(8,128)(2,1)S(1)} all-gather(bf16[128,1024]{1,0:T(8,128)(2,1)S(1)} %pad_maximum_fusion.4), channel_id=2, replica_groups=mesh['segment'=4,'row'=4,'col'=2] {'col'}, dimensions={0}, use_global_device_ids=true | all-gather | bytes 786432 | tf_op jit(solution)/shard_map/all_gather | solution.py:207
  14.9 1.3 %convolution_convert_fusion.3 = bf16[256,2048]{1,0:T(8,128)(2,1)S(1)} fusion(bf16[64,1024]{1,0:T(8,128)(2,1)S(1)} %get-tuple-element.154, bf16[64,1024]{1,0:T(8,128)(2,1)S(1)} %get-tuple-element.120, bf16[64,1024]{1,0:T(8,128)(2,1)S(1)} %get-tuple-element.119, bf16[64,1024]{1,0:T(8,128)(2,1)S(1)} %get-tuple-element.153, bf16[1,1024,2048]{2,1,0:T(8,128)(2,1)S(1)} %copy-done.7), kind=kOutput, calls=%fused_computation.3 | convolution fusion | flops 1076363264 | bytes 5767168 | tf_op jit(solution)/shard_map/dot_general | solution.py:224
  16.3 0.8 collective-permute-start.6
  17.3 2.6 %all-gather.1 = bf16[256,1024]{1,0:T(8,128)(2,1)S(1)} all-gather(bf16[128,1024]{1,0:T(8,128)(2,1)S(1)} %pad_maximum_fusion.5), channel_id=3, replica_groups=mesh['segment'=4,'row'=4,'col'=2] {'col'}, dimensions={0}, use_global_device_ids=true | all-gather | bytes 786432 | tf_op jit(solution)/shard_map/all_gather | solution.py:207
  20.0 1.3 %convolution_convert_fusion.2 = bf16[256,2048]{1,0:T(8,128)(2,1)S(1)} fusion(bf16[64,1024]{1,0:T(8,128)(2,1)S(1)} %get-tuple-element.152, bf16[64,1024]{1,0:T(8,128)(2,1)S(1)} %get-tuple-element.116, bf16[64,1024]{1,0:T(8,128)(2,1)S(1)} %get-tuple-element.115, bf16[64,1024]{1,0:T(8,128)(2,1)S(1)} %get-tuple-element.151, bf16[1,1024,2048]{2,1,0:T(8,128)(2,1)S(1)} %copy-done.7), kind=kOutput, calls=%fused_computation.2 | convolution fusion | flops 1076363264 | bytes 5767168 | tf_op jit(solution)/shard_map/dot_general | solution.py:224
  21.4 0.9 collective-permute-start.4
  22.3 2.5 %collective-permute-start.14 = (bf16[64,1024]{1,0:T(8,128)(2,1)S(1)}, bf16[64,1024]{1,0:T(8,128)(2,1)S(1)}, u32[]{:S(2)}, u32[]{:S(2)}) collective-permute-start(bf16[64,1024]{1,0:T(8,128)(2,1)S(1)} %get-tuple-element.147), channel_id=1, source_target_pairs={{0,0},{1,4},{2,2},{3,6},{5,5},{4,1},{7,7},{6,3},{8,8},{9,12},{10,1... | collective-permute-start | bytes 393224 | tf_op jit(solution)/shard_map/ppermute | solution.py:139
  24.8 1.3 %collective-permute-start.15 = (bf16[64,1024]{1,0:T(8,128)(2,1)S(1)}, bf16[64,1024]{1,0:T(8,128)(2,1)S(1)}, u32[]{:S(2)}, u32[]{:S(2)}) collective-permute-start(bf16[64,1024]{1,0:T(8,128)(2,1)S(1)} %get-tuple-element.148), channel_id=1, source_target_pairs={{0,2},{1,6},{2,0},{3,4},{5,7},{4,3},{7,5},{6,1},{8,10},{9,14},{10,... | collective-permute-start | bytes 393224 | tf_op jit(solution)/shard_map/ppermute | solution.py:139
  26.3 5.9 %collective-permute-done.4 = bf16[128,2048]{1,0:T(8,128)(2,1)S(1)} collective-permute-done((bf16[128,2048]{1,0:T(8,128)(2,1)S(1)}, bf16[128,2048]{1,0:T(8,128)(2,1)S(1)}, u32[]{:S(2)}, u32[]{:S(2)}) %collective-permute-start.4) | collective-permute-done | bytes 524320 | tf_op jit(solution)/shard_map/ppermute | solution.py:129
  32.5 0.8 collective-permute-start.5
  33.9 1.3 %collective-permute-start.11 = (bf16[64,2048]{1,0:T(8,128)(2,1)S(1)}, bf16[64,2048]{1,0:T(8,128)(2,1)S(1)}, u32[]{:S(2)}, u32[]{:S(2)}) collective-permute-start(bf16[64,2048]{1,0:T(8,128)(2,1)S(1)} %bitcast.50), channel_id=1, source_target_pairs={{8,0},{16,8},{24,16},{9,1},{17,9},{25,17},{10,2},{18,10},{26,18},{... | collective-permute-start | bytes 786440 | tf_op jit(solution)/shard_map/ppermute | solution.py:56
  35.2 1.9 %collective-permute-done.7 = bf16[64,2048]{1,0:T(8,128)(2,1)S(1)} collective-permute-done((bf16[64,2048]{1,0:T(8,128)(2,1)S(1)}, bf16[64,2048]{1,0:T(8,128)(2,1)S(1)}, u32[]{:S(2)}, u32[]{:S(2)}) %collective-permute-start.7) | collective-permute-done | bytes 262176 | tf_op jit(solution)/shard_map/ppermute | solution.py:129
  37.3 2.1 %collective-permute-start.12 = (bf16[64,2048]{1,0:T(8,128)(2,1)S(1)}, bf16[64,2048]{1,0:T(8,128)(2,1)S(1)}, u32[]{:S(2)}, u32[]{:S(2)}) collective-permute-start(bf16[64,2048]{1,0:T(8,128)(2,1)S(1)} %fusion.7), channel_id=1, source_target_pairs={{0,2},{1,5},{2,0},{3,7},{4,6},{5,1},{6,4},{7,3},{8,10},{9,13},{10,... | collective-permute-start | bytes 786440 | tf_op jit(solution)/shard_map/ppermute | solution.py:129
  39.6 3.2 %collective-permute-start.8 = (bf16[64,2048]{1,0:T(8,128)(2,1)S(1)}, bf16[64,2048]{1,0:T(8,128)(2,1)S(1)}, u32[]{:S(2)}, u32[]{:S(2)}) collective-permute-start(bf16[64,2048]{1,0:T(8,128)(2,1)S(1)} %add_convert_fusion.3), channel_id=1, source_target_pairs={{0,8},{8,16},{16,24},{1,9},{9,17},{17,25},{2,10},{10,18},{18,26},{... | collective-permute-start | bytes 786440 | tf_op jit(solution)/shard_map/ppermute | solution.py:56
  43.0 0.5 collective-permute-done.12
  43.5 1.1 %collective-permute-start.13 = (bf16[128,2048]{1,0:T(8,128)(2,1)S(1)}, bf16[128,2048]{1,0:T(8,128)(2,1)S(1)}, u32[]{:S(2)}, u32[]{:S(2)}) collective-permute-start(bf16[128,2048]{1,0:T(8,128)(2,1)S(1)} %pad_maximum_fusion.1), channel_id=1, source_target_pairs={{0,4},{1,3},{2,6},{3,1},{4,0},{5,7},{6,2},{7,5},{8,12},{9,11},{10,... | collective-permute-start | bytes 1572872 | tf_op jit(solution)/shard_map/ppermute | solution.py:129
  44.6 3.6 %collective-permute-done.8 = bf16[64,2048]{1,0:T(8,128)(2,1)S(1)} collective-permute-done((bf16[64,2048]{1,0:T(8,128)(2,1)S(1)}, bf16[64,2048]{1,0:T(8,128)(2,1)S(1)}, u32[]{:S(2)}, u32[]{:S(2)}) %collective-permute-start.8) | collective-permute-done | bytes 262176 | tf_op jit(solution)/shard_map/ppermute | solution.py:56
  48.3 3.2 %collective-permute-start.9 = (bf16[64,1024]{1,0:T(8,128)(2,1)S(1)}, bf16[64,1024]{1,0:T(8,128)(2,1)S(1)}, u32[]{:S(2)}, u32[]{:S(2)}) collective-permute-start(bf16[64,1024]{1,0:T(8,128)(2,1)S(1)} %get-tuple-element.150), channel_id=1, source_target_pairs={{0,0},{1,4},{2,2},{3,6},{5,5},{4,1},{7,7},{6,3},{8,8},{9,12},{10,1... | collective-permute-start | bytes 393224 | tf_op jit(solution)/shard_map/ppermute | solution.py:139
  51.6 1.3 %convolution_convert_fusion.1 = bf16[256,2048]{1,0:T(8,128)(2,1)S(1)} fusion(bf16[64,1024]{1,0:T(8,128)(2,1)S(1)} %get-tuple-element.69, bf16[64,1024]{1,0:T(8,128)(2,1)S(1)} %get-tuple-element.142, bf16[64,1024]{1,0:T(8,128)(2,1)S(1)} %get-tuple-element.141, bf16[64,1024]{1,0:T(8,128)(2,1)S(1)} %get-tuple-element.66, bf16[1,1024,2048]{2,1,0:T(8,128)(2,1)S(1)} %copy-done.7), kind=kOutput, calls=%fused_computation.1 | convolution fusion | flops 1076363264 | bytes 5767168 | tf_op jit(solution)/shard_map/dot_general | solution.py:224
  53.0 1.8 %collective-permute-start.10 = (bf16[64,1024]{1,0:T(8,128)(2,1)S(1)}, bf16[64,1024]{1,0:T(8,128)(2,1)S(1)}, u32[]{:S(2)}, u32[]{:S(2)}) collective-permute-start(bf16[64,1024]{1,0:T(8,128)(2,1)S(1)} %get-tuple-element.149), channel_id=1, source_target_pairs={{0,2},{1,6},{2,0},{3,4},{5,7},{4,3},{7,5},{6,1},{8,10},{9,14},{10,... | collective-permute-start | bytes 393224 | tf_op jit(solution)/shard_map/ppermute | solution.py:139
  54.9 1.3 %convolution_convert_fusion.5 = bf16[256,1024]{1,0:T(8,128)(2,1)S(1)} fusion(bf16[128,2048]{1,0:T(8,128)(2,1)S(1)} %collective-permute-done.13, bf16[128,2048]{1,0:T(8,128)(2,1)S(1)} %pad_maximum_fusion.1, bf16[1,1024,2048]{2,1,0:T(8,128)(2,1)S(1)} %copy-done.7), kind=kOutput, calls=%fused_computation.5 | convolution fusion | flops 1076101120 | bytes 5767168 | tf_op jit(solution)/shard_map/dot_general | solution.py:252
  56.4 2.2 %all-gather.2 = bf16[256,1024]{1,0:T(8,128)(2,1)S(1)} all-gather(bf16[128,1024]{1,0:T(8,128)(2,1)S(1)} %get-tuple-element.74), channel_id=4, replica_groups=mesh['segment'=4,'row'=4,'col'=2] {'col'}, dimensions={0}, use_global_device_ids=true | all-gather | bytes 786432 | tf_op jit(solution)/shard_map/all_gather | solution.py:262
  58.7 1.3 %collective-permute-start.18 = (bf16[64,1024]{1,0:T(8,128)(2,1)S(1)}, bf16[64,1024]{1,0:T(8,128)(2,1)S(1)}, u32[]{:S(2)}, u32[]{:S(2)}) collective-permute-start(bf16[64,1024]{1,0:T(8,128)(2,1)S(1)} %get-tuple-element.140), channel_id=1, source_target_pairs={{8,0},{9,4},{10,2},{11,6},{13,5},{12,1},{15,7},{14,3},{16,8},{17,1... | collective-permute-start | bytes 393224 | tf_op jit(solution)/shard_map/ppermute | solution.py:147
  60.0 1.3 %collective-permute-start.17 = (bf16[64,1024]{1,0:T(8,128)(2,1)S(1)}, bf16[64,1024]{1,0:T(8,128)(2,1)S(1)}, u32[]{:S(2)}, u32[]{:S(2)}) collective-permute-start(bf16[64,1024]{1,0:T(8,128)(2,1)S(1)} %get-tuple-element.139), channel_id=1, source_target_pairs={{8,2},{9,6},{10,0},{11,4},{13,7},{12,3},{15,5},{14,1},{16,10},{17,... | collective-permute-start | bytes 393224 | tf_op jit(solution)/shard_map/ppermute | solution.py:147
  61.5 1.4 %collective-permute-start.20 = (bf16[64,2048]{1,0:T(8,128)(2,1)S(1)}, bf16[64,2048]{1,0:T(8,128)(2,1)S(1)}, u32[]{:S(2)}, u32[]{:S(2)}) collective-permute-start(bf16[64,2048]{1,0:T(8,128)(2,1)S(1)} %split.333), channel_id=1, source_target_pairs={{0,4},{1,3},{2,6},{3,1},{4,0},{5,7},{6,2},{7,5},{8,12},{9,11},{10,... | collective-permute-start | bytes 786440 | tf_op jit(solution)/shard_map/ppermute | solution.py:129
  62.9 4.6 %collective-permute-done.18 = bf16[64,1024]{1,0:T(8,128)(2,1)S(1)} collective-permute-done((bf16[64,1024]{1,0:T(8,128)(2,1)S(1)}, bf16[64,1024]{1,0:T(8,128)(2,1)S(1)}, u32[]{:S(2)}, u32[]{:S(2)}) %collective-permute-start.18) | collective-permute-done | bytes 131104 | tf_op jit(solution)/shard_map/ppermute | solution.py:147
  67.6 3.3 %collective-permute-done.17 = bf16[64,1024]{1,0:T(8,128)(2,1)S(1)} collective-permute-done((bf16[64,1024]{1,0:T(8,128)(2,1)S(1)}, bf16[64,1024]{1,0:T(8,128)(2,1)S(1)}, u32[]{:S(2)}, u32[]{:S(2)}) %collective-permute-start.17) | collective-permute-done | bytes 131104 | tf_op jit(solution)/shard_map/ppermute | solution.py:147
  71.6 1.5 %collective-permute-start.23 = (bf16[64,2048]{1,0:T(8,128)(2,1)S(1)}, bf16[64,2048]{1,0:T(8,128)(2,1)S(1)}, u32[]{:S(2)}, u32[]{:S(2)}) collective-permute-start(bf16[64,2048]{1,0:T(8,128)(2,1)S(1)} %get-tuple-element.94), channel_id=1, source_target_pairs={{0,4},{1,3},{2,6},{3,1},{4,0},{5,7},{6,2},{7,5},{8,12},{9,11},{10,... | collective-permute-start | bytes 786440 | tf_op jit(solution)/shard_map/ppermute | solution.py:129
  73.3 1.3 %convolution_convert_fusion = bf16[256,2048]{1,0:T(8,128)(2,1)S(1)} fusion(bf16[64,1024]{1,0:T(8,128)(2,1)S(1)} %get-tuple-element.82, bf16[64,1024]{1,0:T(8,128)(2,1)S(1)} %get-tuple-element.132, bf16[64,1024]{1,0:T(8,128)(2,1)S(1)} %get-tuple-element.131, bf16[64,1024]{1,0:T(8,128)(2,1)S(1)} %get-tuple-element.79, bf16[1,1024,2048]{2,1,0:T(8,128)(2,1)S(1)} %copy-done.7), kind=kOutput, calls=%fused_computation | convolution fusion | flops 1076363264 | bytes 5767168 | tf_op jit(solution)/shard_map/dot_general | solution.py:224
  74.6 0.9 collective-permute-start.22
  75.6 3.4 %collective-permute-start.28 = (bf16[64,1024]{1,0:T(8,128)(2,1)S(1)}, bf16[64,1024]{1,0:T(8,128)(2,1)S(1)}, u32[]{:S(2)}, u32[]{:S(2)}) collective-permute-start(bf16[64,1024]{1,0:T(8,128)(2,1)S(1)} %get-tuple-element.139), channel_id=1, source_target_pairs={{0,2},{1,6},{2,0},{3,4},{5,7},{4,3},{7,5},{6,1}} | collective-permute-start | bytes 393224 | tf_op jit(solution)/shard_map/ppermute | solution.py:147
  79.1 3.0 %collective-permute-start.29 = (bf16[64,1024]{1,0:T(8,128)(2,1)S(1)}, bf16[64,1024]{1,0:T(8,128)(2,1)S(1)}, u32[]{:S(2)}, u32[]{:S(2)}) collective-permute-start(bf16[64,1024]{1,0:T(8,128)(2,1)S(1)} %get-tuple-element.140), channel_id=1, source_target_pairs={{0,0},{1,4},{2,2},{3,6},{5,5},{4,1},{7,7},{6,3}} | collective-permute-start | bytes 393224 | tf_op jit(solution)/shard_map/ppermute | solution.py:147
  82.2 4.7 %collective-permute-done.28 = bf16[64,1024]{1,0:T(8,128)(2,1)S(1)} collective-permute-done((bf16[64,1024]{1,0:T(8,128)(2,1)S(1)}, bf16[64,1024]{1,0:T(8,128)(2,1)S(1)}, u32[]{:S(2)}, u32[]{:S(2)}) %collective-permute-start.28) | collective-permute-done | bytes 131104 | tf_op jit(solution)/shard_map/ppermute | solution.py:147
  86.9 1.0 collective-permute-done.29
  88.1 1.3 %collective-permute-start.27 = (bf16[64,2048]{1,0:T(8,128)(2,1)S(1)}, bf16[64,2048]{1,0:T(8,128)(2,1)S(1)}, u32[]{:S(2)}, u32[]{:S(2)}) collective-permute-start(bf16[64,2048]{1,0:T(8,128)(2,1)S(1)} %get-tuple-element.90), channel_id=1, source_target_pairs={{0,8},{8,16},{16,24},{1,9},{9,17},{17,25},{2,10},{10,18},{18,26},{... | collective-permute-start | bytes 786440 | tf_op jit(solution)/shard_map/ppermute | solution.py:56
  89.4 3.0 %collective-permute-done.25 = bf16[128,2048]{1,0:T(8,128)(2,1)S(1)} collective-permute-done((bf16[128,2048]{1,0:T(8,128)(2,1)S(1)}, bf16[128,2048]{1,0:T(8,128)(2,1)S(1)}, u32[]{:S(2)}, u32[]{:S(2)}) %collective-permute-start.25) | collective-permute-done | bytes 524320 | tf_op jit(solution)/shard_map/ppermute | solution.py:129
  92.4 1.3 %convolution_convert_fusion.4 = bf16[256,1024]{1,0:T(8,128)(2,1)S(1)} fusion(bf16[128,2048]{1,0:T(8,128)(2,1)S(1)} %collective-permute-done.25, bf16[128,2048]{1,0:T(8,128)(2,1)S(1)} %pad_maximum_fusion.2, bf16[1,1024,2048]{2,1,0:T(8,128)(2,1)S(1)} %copy-done.7), kind=kOutput, calls=%fused_computation.4 | convolution fusion | flops 1076101120 | bytes 5767168 | tf_op jit(solution)/shard_map/dot_general | solution.py:252
  94.0 1.5 %collective-permute-start.24 = (bf16[64,2048]{1,0:T(8,128)(2,1)S(1)}, bf16[64,2048]{1,0:T(8,128)(2,1)S(1)}, u32[]{:S(2)}, u32[]{:S(2)}) collective-permute-start(bf16[64,2048]{1,0:T(8,128)(2,1)S(1)} %split.332), channel_id=1, source_target_pairs={{0,4},{1,3},{2,6},{3,1},{4,0},{5,7},{6,2},{7,5},{8,12},{9,11},{10,... | collective-permute-start | bytes 786440 | tf_op jit(solution)/shard_map/ppermute | solution.py:129
  95.6 2.0 %collective-permute-start.30 = (bf16[64,1024]{1,0:T(8,128)(2,1)S(1)}, bf16[64,1024]{1,0:T(8,128)(2,1)S(1)}, u32[]{:S(2)}, u32[]{:S(2)}) collective-permute-start(bf16[64,1024]{1,0:T(8,128)(2,1)S(1)} %get-tuple-element.127), channel_id=1, source_target_pairs={{0,2},{1,6},{2,0},{3,4},{5,7},{4,3},{7,5},{6,1},{8,10},{9,14},{10,... | collective-permute-start | bytes 393224 | tf_op jit(solution)/shard_map/ppermute | solution.py:139
  97.6 2.5 %collective-permute-start.31 = (bf16[64,1024]{1,0:T(8,128)(2,1)S(1)}, bf16[64,1024]{1,0:T(8,128)(2,1)S(1)}, u32[]{:S(2)}, u32[]{:S(2)}) collective-permute-start(bf16[64,1024]{1,0:T(8,128)(2,1)S(1)} %get-tuple-element.128), channel_id=1, source_target_pairs={{0,0},{1,4},{2,2},{3,6},{5,5},{4,1},{7,7},{6,3},{8,8},{9,12},{10,1... | collective-permute-start | bytes 393224 | tf_op jit(solution)/shard_map/ppermute | solution.py:139
  100.5 1.9 %collective-permute-done.30 = bf16[64,1024]{1,0:T(8,128)(2,1)S(1)} collective-permute-done((bf16[64,1024]{1,0:T(8,128)(2,1)S(1)}, bf16[64,1024]{1,0:T(8,128)(2,1)S(1)}, u32[]{:S(2)}, u32[]{:S(2)}) %collective-permute-start.30) | collective-permute-done | bytes 131104 | tf_op jit(solution)/shard_map/ppermute | solution.py:139
  102.4 1.4 %collective-permute-done.31 = bf16[64,1024]{1,0:T(8,128)(2,1)S(1)} collective-permute-done((bf16[64,1024]{1,0:T(8,128)(2,1)S(1)}, bf16[64,1024]{1,0:T(8,128)(2,1)S(1)}, u32[]{:S(2)}, u32[]{:S(2)}) %collective-permute-start.31) | collective-permute-done | bytes 131104 | tf_op jit(solution)/shard_map/ppermute | solution.py:139
  104.0 0.8 copy-done.3
  (99 shorter events, 5.5 us)
Async XLA Ops:
  1.7 10.3 %collective-permute-start.1 = (bf16[64,1024]{1,0:T(8,128)(2,1)S(1)}, bf16[64,1024]{1,0:T(8,128)(2,1)S(1)}, u32[]{:S(2)}, u32[]{:S(2)}) collective-permute-start(bf16[64,1024]{1,0:T(8,128)(2,1)S(1)} %get-tuple-element.156), channel_id=1, source_target_pairs={{0,0},{1,4},{2,2},{3,6},{5,5},{4,1},{7,7},{6,3},{8,8},{9,12},{10,1... | collective-permute-start | bytes 393224 | tf_op jit(solution)/shard_map/ppermute | solution.py:139
  6.3 6.1 %collective-permute-start.2 = (bf16[64,1024]{1,0:T(8,128)(2,1)S(1)}, bf16[64,1024]{1,0:T(8,128)(2,1)S(1)}, u32[]{:S(2)}, u32[]{:S(2)}) collective-permute-start(bf16[64,1024]{1,0:T(8,128)(2,1)S(1)} %get-tuple-element.155), channel_id=1, source_target_pairs={{0,2},{1,6},{2,0},{3,4},{5,7},{4,3},{7,5},{6,1},{8,10},{9,14},{10,... | collective-permute-start | bytes 393224 | tf_op jit(solution)/shard_map/ppermute | solution.py:139
  8.3 8.0 %collective-permute-start = (bf16[64,1024]{1,0:T(8,128)(2,1)S(1)}, bf16[64,1024]{1,0:T(8,128)(2,1)S(1)}, u32[]{:S(2)}, u32[]{:S(2)}) collective-permute-start(bf16[64,1024]{1,0:T(8,128)(2,1)S(1)} %get-tuple-element.157), channel_id=1, source_target_pairs={{0,0},{1,4},{2,2},{3,6},{5,5},{4,1},{7,7},{6,3},{8,8},{9,12},{10,1... | collective-permute-start | bytes 393224 | tf_op jit(solution)/shard_map/ppermute | solution.py:139
  11.9 5.4 %collective-permute-start.3 = (bf16[64,1024]{1,0:T(8,128)(2,1)S(1)}, bf16[64,1024]{1,0:T(8,128)(2,1)S(1)}, u32[]{:S(2)}, u32[]{:S(2)}) collective-permute-start(bf16[64,1024]{1,0:T(8,128)(2,1)S(1)} %get-tuple-element.158), channel_id=1, source_target_pairs={{0,2},{1,6},{2,0},{3,4},{5,7},{4,3},{7,5},{6,1},{8,10},{9,14},{10,... | collective-permute-start | bytes 393224 | tf_op jit(solution)/shard_map/ppermute | solution.py:139
  12.1 2.9 %copy-start.7 = (bf16[1,1024,2048]{2,1,0:T(8,128)(2,1)S(1)}, bf16[1,1024,2048]{2,1,0:T(8,128)(2,1)}, u32[]{:S(2)}) copy-start(bf16[1,1024,2048]{2,1,0:T(8,128)(2,1)} %param.7) | copy-start | bytes 12582916
  16.3 9.8 %collective-permute-start.6 = (bf16[128,2048]{1,0:T(8,128)(2,1)S(1)}, bf16[128,2048]{1,0:T(8,128)(2,1)S(1)}, u32[]{:S(2)}, u32[]{:S(2)}) collective-permute-start(bf16[128,2048]{1,0:T(8,128)(2,1)S(1)} %split.238), channel_id=1, source_target_pairs={{0,4},{1,3},{2,6},{3,1},{4,0},{5,7},{6,2},{7,5},{8,12},{9,11},{10,... | collective-permute-start | bytes 1572872 | tf_op jit(solution)/shard_map/ppermute | solution.py:129
  21.3 12.6 %copy-start = (bf16[1,64,2048]{2,1,0:T(8,128)(2,1)S(1)}, bf16[1,64,2048]{2,1,0:T(8,128)(2,1)}, u32[]{:S(2)}) copy-start(bf16[1,64,2048]{2,1,0:T(8,128)(2,1)} %param.11) | copy-start | bytes 786436
  21.3 15.8 %copy-start.6 = (f32[1,2048]{1,0:T(1,128)S(1)}, f32[1,2048]{1,0:T(1,128)}, u32[]{:S(2)}) copy-start(f32[1,2048]{1,0:T(1,128)} %param.8) | copy-start | bytes 24580
  21.3 18.1 %copy-start.1 = (bf16[1,64,2048]{2,1,0:T(8,128)(2,1)S(1)}, bf16[1,64,2048]{2,1,0:T(8,128)(2,1)}, u32[]{:S(2)}) copy-start(bf16[1,64,2048]{2,1,0:T(8,128)(2,1)} %param.9) | copy-start | bytes 786436
  21.4 10.9 %collective-permute-start.4 = (bf16[128,2048]{1,0:T(8,128)(2,1)S(1)}, bf16[128,2048]{1,0:T(8,128)(2,1)S(1)}, u32[]{:S(2)}, u32[]{:S(2)}) collective-permute-start(bf16[128,2048]{1,0:T(8,128)(2,1)S(1)} %split.244), channel_id=1, source_target_pairs={{0,2},{1,5},{2,0},{3,7},{4,6},{5,1},{6,4},{7,3},{8,10},{9,13},{10,... | collective-permute-start | bytes 1572872 | tf_op jit(solution)/shard_map/ppermute | solution.py:129
  22.3 11.0 %collective-permute-start.14 = (bf16[64,1024]{1,0:T(8,128)(2,1)S(1)}, bf16[64,1024]{1,0:T(8,128)(2,1)S(1)}, u32[]{:S(2)}, u32[]{:S(2)}) collective-permute-start(bf16[64,1024]{1,0:T(8,128)(2,1)S(1)} %get-tuple-element.147), channel_id=1, source_target_pairs={{0,0},{1,4},{2,2},{3,6},{5,5},{4,1},{7,7},{6,3},{8,8},{9,12},{10,1... | collective-permute-start | bytes 393224 | tf_op jit(solution)/shard_map/ppermute | solution.py:139
  24.8 8.8 %collective-permute-start.15 = (bf16[64,1024]{1,0:T(8,128)(2,1)S(1)}, bf16[64,1024]{1,0:T(8,128)(2,1)S(1)}, u32[]{:S(2)}, u32[]{:S(2)}) collective-permute-start(bf16[64,1024]{1,0:T(8,128)(2,1)S(1)} %get-tuple-element.148), channel_id=1, source_target_pairs={{0,2},{1,6},{2,0},{3,4},{5,7},{4,3},{7,5},{6,1},{8,10},{9,14},{10,... | collective-permute-start | bytes 393224 | tf_op jit(solution)/shard_map/ppermute | solution.py:139
  26.3 10.8 %collective-permute-start.7 = (bf16[64,2048]{1,0:T(8,128)(2,1)S(1)}, bf16[64,2048]{1,0:T(8,128)(2,1)S(1)}, u32[]{:S(2)}, u32[]{:S(2)}) collective-permute-start(bf16[64,2048]{1,0:T(8,128)(2,1)S(1)} %split.334), channel_id=1, source_target_pairs={{0,2},{1,5},{2,0},{3,7},{4,6},{5,1},{6,4},{7,3},{8,10},{9,13},{10,... | collective-permute-start | bytes 786440 | tf_op jit(solution)/shard_map/ppermute | solution.py:129
  32.4 15.8 %copy-start.4 = (bf16[64,2048]{1,0:T(8,128)(2,1)S(1)}, bf16[64,2048]{1,0:T(8,128)(2,1)}, u32[]{:S(2)}) copy-start(bf16[64,2048]{1,0:T(8,128)(2,1)} %param.10) | copy-start | bytes 786436
  32.5 7.0 %collective-permute-start.5 = (bf16[64,2048]{1,0:T(8,128)(2,1)S(1)}, bf16[64,2048]{1,0:T(8,128)(2,1)S(1)}, u32[]{:S(2)}, u32[]{:S(2)}) collective-permute-start(bf16[64,2048]{1,0:T(8,128)(2,1)S(1)} %split.335), channel_id=1, source_target_pairs={{0,4},{1,3},{2,6},{3,1},{4,0},{5,7},{6,2},{7,5},{8,12},{9,11},{10,... | collective-permute-start | bytes 786440 | tf_op jit(solution)/shard_map/ppermute | solution.py:129
  33.7 5.9 %collective-permute-start.16 = (bf16[128,1024]{1,0:T(8,128)(2,1)S(1)}, bf16[128,1024]{1,0:T(8,128)(2,1)S(1)}, u32[]{:S(2)}, u32[]{:S(2)}) collective-permute-start(bf16[128,1024]{1,0:T(8,128)(2,1)S(1)} %pad_maximum_fusion.6), channel_id=1, source_target_pairs={{0,1},{1,0},{2,3},{3,2},{4,5},{5,4},{6,7},{7,6},{8,9},{9,8},{10,11... | collective-permute-start | bytes 786440 | tf_op jit(solution)/shard_map/ppermute | solution.py:81
  33.9 19.1 %collective-permute-start.11 = (bf16[64,2048]{1,0:T(8,128)(2,1)S(1)}, bf16[64,2048]{1,0:T(8,128)(2,1)S(1)}, u32[]{:S(2)}, u32[]{:S(2)}) collective-permute-start(bf16[64,2048]{1,0:T(8,128)(2,1)S(1)} %bitcast.50), channel_id=1, source_target_pairs={{8,0},{16,8},{24,16},{9,1},{17,9},{25,17},{10,2},{18,10},{26,18},{... | collective-permute-start | bytes 786440 | tf_op jit(solution)/shard_map/ppermute | solution.py:56
  37.3 6.1 %collective-permute-start.12 = (bf16[64,2048]{1,0:T(8,128)(2,1)S(1)}, bf16[64,2048]{1,0:T(8,128)(2,1)S(1)}, u32[]{:S(2)}, u32[]{:S(2)}) collective-permute-start(bf16[64,2048]{1,0:T(8,128)(2,1)S(1)} %fusion.7), channel_id=1, source_target_pairs={{0,2},{1,5},{2,0},{3,7},{4,6},{5,1},{6,4},{7,3},{8,10},{9,13},{10,... | collective-permute-start | bytes 786440 | tf_op jit(solution)/shard_map/ppermute | solution.py:129
  39.6 8.6 %collective-permute-start.8 = (bf16[64,2048]{1,0:T(8,128)(2,1)S(1)}, bf16[64,2048]{1,0:T(8,128)(2,1)S(1)}, u32[]{:S(2)}, u32[]{:S(2)}) collective-permute-start(bf16[64,2048]{1,0:T(8,128)(2,1)S(1)} %add_convert_fusion.3), channel_id=1, source_target_pairs={{0,8},{8,16},{16,24},{1,9},{9,17},{17,25},{2,10},{10,18},{18,26},{... | collective-permute-start | bytes 786440 | tf_op jit(solution)/shard_map/ppermute | solution.py:56
  43.5 11.4 %collective-permute-start.13 = (bf16[128,2048]{1,0:T(8,128)(2,1)S(1)}, bf16[128,2048]{1,0:T(8,128)(2,1)S(1)}, u32[]{:S(2)}, u32[]{:S(2)}) collective-permute-start(bf16[128,2048]{1,0:T(8,128)(2,1)S(1)} %pad_maximum_fusion.1), channel_id=1, source_target_pairs={{0,4},{1,3},{2,6},{3,1},{4,0},{5,7},{6,2},{7,5},{8,12},{9,11},{10,... | collective-permute-start | bytes 1572872 | tf_op jit(solution)/shard_map/ppermute | solution.py:129
  48.3 6.6 %collective-permute-start.9 = (bf16[64,1024]{1,0:T(8,128)(2,1)S(1)}, bf16[64,1024]{1,0:T(8,128)(2,1)S(1)}, u32[]{:S(2)}, u32[]{:S(2)}) collective-permute-start(bf16[64,1024]{1,0:T(8,128)(2,1)S(1)} %get-tuple-element.150), channel_id=1, source_target_pairs={{0,0},{1,4},{2,2},{3,6},{5,5},{4,1},{7,7},{6,3},{8,8},{9,12},{10,1... | collective-permute-start | bytes 393224 | tf_op jit(solution)/shard_map/ppermute | solution.py:139
  52.9 8.4 %collective-permute-start.19 = (bf16[128,2048]{1,0:T(8,128)(2,1)S(1)}, bf16[128,2048]{1,0:T(8,128)(2,1)S(1)}, u32[]{:S(2)}, u32[]{:S(2)}) collective-permute-start(bf16[128,2048]{1,0:T(8,128)(2,1)S(1)} %split.261), channel_id=1, source_target_pairs={{0,2},{1,5},{2,0},{3,7},{4,6},{5,1},{6,4},{7,3},{8,10},{9,13},{10,... | collective-permute-start | bytes 1572872 | tf_op jit(solution)/shard_map/ppermute | solution.py:129
  53.0 18.2 %collective-permute-start.10 = (bf16[64,1024]{1,0:T(8,128)(2,1)S(1)}, bf16[64,1024]{1,0:T(8,128)(2,1)S(1)}, u32[]{:S(2)}, u32[]{:S(2)}) collective-permute-start(bf16[64,1024]{1,0:T(8,128)(2,1)S(1)} %get-tuple-element.149), channel_id=1, source_target_pairs={{0,2},{1,6},{2,0},{3,4},{5,7},{4,3},{7,5},{6,1},{8,10},{9,14},{10,... | collective-permute-start | bytes 393224 | tf_op jit(solution)/shard_map/ppermute | solution.py:139
  56.2 14.7 %copy-start.5 = (bf16[64,2048]{1,0:T(8,128)(2,1)S(1)}, bf16[64,2048]{1,0:T(8,128)(2,1)}, u32[]{:S(2)}) copy-start(bf16[64,2048]{1,0:T(8,128)(2,1)} %param.12) | copy-start | bytes 786436
  58.7 8.8 %collective-permute-start.18 = (bf16[64,1024]{1,0:T(8,128)(2,1)S(1)}, bf16[64,1024]{1,0:T(8,128)(2,1)S(1)}, u32[]{:S(2)}, u32[]{:S(2)}) collective-permute-start(bf16[64,1024]{1,0:T(8,128)(2,1)S(1)} %get-tuple-element.140), channel_id=1, source_target_pairs={{8,0},{9,4},{10,2},{11,6},{13,5},{12,1},{15,7},{14,3},{16,8},{17,1... | collective-permute-start | bytes 393224 | tf_op jit(solution)/shard_map/ppermute | solution.py:147
  60.0 10.8 %collective-permute-start.17 = (bf16[64,1024]{1,0:T(8,128)(2,1)S(1)}, bf16[64,1024]{1,0:T(8,128)(2,1)S(1)}, u32[]{:S(2)}, u32[]{:S(2)}) collective-permute-start(bf16[64,1024]{1,0:T(8,128)(2,1)S(1)} %get-tuple-element.139), channel_id=1, source_target_pairs={{8,2},{9,6},{10,0},{11,4},{13,7},{12,3},{15,5},{14,1},{16,10},{17,... | collective-permute-start | bytes 393224 | tf_op jit(solution)/shard_map/ppermute | solution.py:147
  61.5 9.3 %collective-permute-start.20 = (bf16[64,2048]{1,0:T(8,128)(2,1)S(1)}, bf16[64,2048]{1,0:T(8,128)(2,1)S(1)}, u32[]{:S(2)}, u32[]{:S(2)}) collective-permute-start(bf16[64,2048]{1,0:T(8,128)(2,1)S(1)} %split.333), channel_id=1, source_target_pairs={{0,4},{1,3},{2,6},{3,1},{4,0},{5,7},{6,2},{7,5},{8,12},{9,11},{10,... | collective-permute-start | bytes 786440 | tf_op jit(solution)/shard_map/ppermute | solution.py:129
  71.2 1.9 %collective-permute-start.21 = (bf16[128,1024]{1,0:T(8,128)(2,1)S(1)}, bf16[128,1024]{1,0:T(8,128)(2,1)S(1)}, u32[]{:S(2)}, u32[]{:S(2)}) collective-permute-start(bf16[128,1024]{1,0:T(8,128)(2,1)S(1)} %constant_dynamic-update-slice_fusion), channel_id=1, source_target_pairs={{0,1},{1,0},{2,3},{3,2},{4,5},{5,4},{6,7},{7,6},{8,9},{9,8},{10,11... | collective-permute-start | bytes 786440 | tf_op jit(solution)/shard_map/ppermute | solution.py:81
  71.6 10.4 %collective-permute-start.23 = (bf16[64,2048]{1,0:T(8,128)(2,1)S(1)}, bf16[64,2048]{1,0:T(8,128)(2,1)S(1)}, u32[]{:S(2)}, u32[]{:S(2)}) collective-permute-start(bf16[64,2048]{1,0:T(8,128)(2,1)S(1)} %get-tuple-element.94), channel_id=1, source_target_pairs={{0,4},{1,3},{2,6},{3,1},{4,0},{5,7},{6,2},{7,5},{8,12},{9,11},{10,... | collective-permute-start | bytes 786440 | tf_op jit(solution)/shard_map/ppermute | solution.py:129
  74.6 13.3 %collective-permute-start.22 = (bf16[128,2048]{1,0:T(8,128)(2,1)S(1)}, bf16[128,2048]{1,0:T(8,128)(2,1)S(1)}, u32[]{:S(2)}, u32[]{:S(2)}) collective-permute-start(bf16[128,2048]{1,0:T(8,128)(2,1)S(1)} %split.269), channel_id=1, source_target_pairs={{0,2},{1,5},{2,0},{3,7},{4,6},{5,1},{6,4},{7,3},{8,10},{9,13},{10,... | collective-permute-start | bytes 1572872 | tf_op jit(solution)/shard_map/ppermute | solution.py:129
  75.6 11.3 %collective-permute-start.28 = (bf16[64,1024]{1,0:T(8,128)(2,1)S(1)}, bf16[64,1024]{1,0:T(8,128)(2,1)S(1)}, u32[]{:S(2)}, u32[]{:S(2)}) collective-permute-start(bf16[64,1024]{1,0:T(8,128)(2,1)S(1)} %get-tuple-element.139), channel_id=1, source_target_pairs={{0,2},{1,6},{2,0},{3,4},{5,7},{4,3},{7,5},{6,1}} | collective-permute-start | bytes 393224 | tf_op jit(solution)/shard_map/ppermute | solution.py:147
  79.1 8.8 %collective-permute-start.29 = (bf16[64,1024]{1,0:T(8,128)(2,1)S(1)}, bf16[64,1024]{1,0:T(8,128)(2,1)S(1)}, u32[]{:S(2)}, u32[]{:S(2)}) collective-permute-start(bf16[64,1024]{1,0:T(8,128)(2,1)S(1)} %get-tuple-element.140), channel_id=1, source_target_pairs={{0,0},{1,4},{2,2},{3,6},{5,5},{4,1},{7,7},{6,3}} | collective-permute-start | bytes 393224 | tf_op jit(solution)/shard_map/ppermute | solution.py:147
  82.1 10.2 %collective-permute-start.25 = (bf16[128,2048]{1,0:T(8,128)(2,1)S(1)}, bf16[128,2048]{1,0:T(8,128)(2,1)S(1)}, u32[]{:S(2)}, u32[]{:S(2)}) collective-permute-start(bf16[128,2048]{1,0:T(8,128)(2,1)S(1)} %pad_maximum_fusion.2), channel_id=1, source_target_pairs={{0,2},{1,5},{2,0},{3,7},{4,6},{5,1},{6,4},{7,3},{8,10},{9,13},{10,... | collective-permute-start | bytes 1572872 | tf_op jit(solution)/shard_map/ppermute | solution.py:129
  88.1 7.4 %collective-permute-start.27 = (bf16[64,2048]{1,0:T(8,128)(2,1)S(1)}, bf16[64,2048]{1,0:T(8,128)(2,1)S(1)}, u32[]{:S(2)}, u32[]{:S(2)}) collective-permute-start(bf16[64,2048]{1,0:T(8,128)(2,1)S(1)} %get-tuple-element.90), channel_id=1, source_target_pairs={{0,8},{8,16},{16,24},{1,9},{9,17},{17,25},{2,10},{10,18},{18,26},{... | collective-permute-start | bytes 786440 | tf_op jit(solution)/shard_map/ppermute | solution.py:56
  93.8 1.6 %collective-permute-start.26 = (bf16[128,1024]{1,0:T(8,128)(2,1)S(1)}, bf16[128,1024]{1,0:T(8,128)(2,1)S(1)}, u32[]{:S(2)}, u32[]{:S(2)}) collective-permute-start(bf16[128,1024]{1,0:T(8,128)(2,1)S(1)} %get-tuple-element.89), channel_id=1, source_target_pairs={{0,1},{1,0},{2,3},{3,2},{4,5},{5,4},{6,7},{7,6},{8,9},{9,8},{10,11... | collective-permute-start | bytes 786440 | tf_op jit(solution)/shard_map/ppermute | solution.py:81
  94.0 6.2 %collective-permute-start.24 = (bf16[64,2048]{1,0:T(8,128)(2,1)S(1)}, bf16[64,2048]{1,0:T(8,128)(2,1)S(1)}, u32[]{:S(2)}, u32[]{:S(2)}) collective-permute-start(bf16[64,2048]{1,0:T(8,128)(2,1)S(1)} %split.332), channel_id=1, source_target_pairs={{0,4},{1,3},{2,6},{3,1},{4,0},{5,7},{6,2},{7,5},{8,12},{9,11},{10,... | collective-permute-start | bytes 786440 | tf_op jit(solution)/shard_map/ppermute | solution.py:129
  95.6 6.8 %collective-permute-start.30 = (bf16[64,1024]{1,0:T(8,128)(2,1)S(1)}, bf16[64,1024]{1,0:T(8,128)(2,1)S(1)}, u32[]{:S(2)}, u32[]{:S(2)}) collective-permute-start(bf16[64,1024]{1,0:T(8,128)(2,1)S(1)} %get-tuple-element.127), channel_id=1, source_target_pairs={{0,2},{1,6},{2,0},{3,4},{5,7},{4,3},{7,5},{6,1},{8,10},{9,14},{10,... | collective-permute-start | bytes 393224 | tf_op jit(solution)/shard_map/ppermute | solution.py:139
  97.6 6.3 %collective-permute-start.31 = (bf16[64,1024]{1,0:T(8,128)(2,1)S(1)}, bf16[64,1024]{1,0:T(8,128)(2,1)S(1)}, u32[]{:S(2)}, u32[]{:S(2)}) collective-permute-start(bf16[64,1024]{1,0:T(8,128)(2,1)S(1)} %get-tuple-element.128), channel_id=1, source_target_pairs={{0,0},{1,4},{2,2},{3,6},{5,5},{4,1},{7,7},{6,3},{8,8},{9,12},{10,1... | collective-permute-start | bytes 393224 | tf_op jit(solution)/shard_map/ppermute | solution.py:139
  100.4 3.6 %copy-start.2 = (bf16[1,2,64,2048]{3,2,1,0:T(8,128)(2,1)}, bf16[1,2,64,2048]{3,2,1,0:T(8,128)(2,1)S(1)}, u32[]{:S(2)}) copy-start(bf16[1,2,64,2048]{3,2,1,0:T(8,128)(2,1)S(1)} %bitcast_dynamic-update-slice_fusion) | copy-start | bytes 1572868
  104.0 0.8 copy-start.3
